TPU v7x, 32 devices: a whole 2x2x4 slice. The times are simulated.
32 devices in a mesh: dp: 16 (over z, y, core), seq: 2 (over x).
Axes of the slice: x: 2, y: 2, z: 4, core: 2. Of those that a mesh axis runs over, the one named last changes fastest.
Arguments:
- images: bfloat16 [32, 256, 2048], P('dp', 'seq'), may hold values from -6 to 6
- captions: bfloat16 [32, 128, 4096], P('dp', 'seq'), may hold values from -6 to 6
- cap_lengths: int32 [32], P('dp'), may hold values from 5 to 128, as said below
- norm1_gain: bfloat16 [2048], P('dp'), may hold values from 0.25 to 1.75
- w_query: bfloat16 [2048, 2048], P('dp'), may hold values from -0.125 to 0.125
- w_key: bfloat16 [2048, 2048], P('dp'), may hold values from -0.125 to 0.125
- w_value: bfloat16 [2048, 2048], P('dp'), may hold values from -0.125 to 0.125
- w_out: bfloat16 [2048, 2048], P('dp'), may hold values from -0.5 to 0.5
- norm2_gain: bfloat16 [2048], P('dp'), may hold values from 0.25 to 1.75
- w_text: bfloat16 [4096, 2048], P('dp'), may hold values from -0.09375 to 0.09375
- w_cross_query: bfloat16 [2048, 2048], P('dp'), may hold values from -0.125 to 0.125
- w_cross_key: bfloat16 [2048, 2048], P('dp'), may hold values from -0.125 to 0.125
- w_cross_value: bfloat16 [2048, 2048], P('dp'), may hold values from -0.125 to 0.125
- w_cross_out: bfloat16 [2048, 2048], P('dp'), may hold values from -0.5 to 0.5
- norm3_gain: bfloat16 [2048], P('dp'), may hold values from 0.25 to 1.75
- w_up: bfloat16 [2048, 8192], P('dp'), may hold values from -0.125 to 0.125
- w_down: bfloat16 [8192, 2048], P('dp'), may hold values from -0.0625 to 0.0625
- out_grad: bfloat16 [32, 256, 2048], P('dp', 'seq'), may hold values from -6 to 6
Outputs:
- layer_out: bfloat16 [32, 256, 2048], P('dp', 'seq')
- image_grad: float32 [32, 256, 2048], P('dp', 'seq')
- caption_grad: float32 [32, 128, 4096], P('dp', 'seq')
- grad_norm1: float32 [2048], P('dp')
- grad_query: float32 [2048, 2048], P('dp')
- grad_key: float32 [2048, 2048], P('dp')
- grad_value: float32 [2048, 2048], P('dp')
- grad_out: float32 [2048, 2048], P('dp')
- grad_norm2: float32 [2048], P('dp')
- grad_text: float32 [4096, 2048], P('dp')
- grad_cross_query: float32 [2048, 2048], P('dp')
- grad_cross_key: float32 [2048, 2048], P('dp')
- grad_cross_value: float32 [2048, 2048], P('dp')
- grad_cross_out: float32 [2048, 2048], P('dp')
- grad_norm3: float32 [2048], P('dp')
- grad_up: float32 [2048, 8192], P('dp')
- grad_down: float32 [8192, 2048], P('dp')
Inputs may be any that keep to these rules, and one draw needn't show every extreme that they name: `cap_lengths`: caption slots at and after a caption's length are padding. Of the 2 images of each index of dp, at least one has all 128 slots real.
All inputs are finite; a program needn't handle non-finite values.
Results may differ from a plain program's by a relative error of at most 0.024.
Values may be sent and summed in bfloat16 or wider, within the bound.
A program may use at most 640 MiB of HBM per device.

v0:
```python
import jax
import jax.numpy as jnp
from jax import lax
from jax.sharding import PartitionSpec as P

HEADS = 16
HEAD_DIM = 128
CAPTION = 128


EPSILON = 1e-05


def rounded(values):
    return values.astype(jnp.bfloat16)


def matmul(left, right):
    return jnp.einsum("brk,kn->brn", left, right, preferred_element_type=jnp.float32)


def matmul_t(left, right):
    return jnp.einsum("brn,kn->brk", left, right, preferred_element_type=jnp.float32)


def outer_sum(left, right):
    return jnp.einsum("brk,brn->kn", left, right, preferred_element_type=jnp.float32)


def layer_norm(values, norm_gain):
    centred = values - jnp.mean(values, axis=-1, keepdims=True)
    spread = jnp.mean(centred * centred, axis=-1, keepdims=True)
    return centred * lax.rsqrt(spread + EPSILON) * norm_gain


def norm_back(values, norm_gain, grad_normed):
    result, pullback = jax.vjp(layer_norm, values, norm_gain)
    return pullback(grad_normed)


def exact_gelu(values):
    return jax.nn.gelu(values, approximate=False)


def split_heads(values):
    return values.reshape(values.shape[0], values.shape[1], HEADS, HEAD_DIM)


def attend(queries, key_rows, value_rows, usable):
    score_scale = HEAD_DIM ** (-0.5)
    raw_scores = jnp.einsum(
        "bqhd,bkhd->bhqk",
        split_heads(queries),
        split_heads(key_rows),
        preferred_element_type=jnp.float32,
    )
    scores = raw_scores * score_scale
    if usable is not None:
        scores = jnp.where(usable[:, None, None, :], scores, -1e30)
    attn_prob = jax.nn.softmax(scores, axis=-1)
    blended = jnp.einsum(
        "bhqk,bkhd->bqhd",
        rounded(attn_prob),
        split_heads(value_rows),
        preferred_element_type=jnp.float32,
    )
    return (attn_prob, rounded(blended.reshape(queries.shape)))


def attend_back(queries, key_rows, value_rows, attn_prob, grad_blended):
    score_scale = HEAD_DIM ** (-0.5)
    grad_heads = split_heads(grad_blended)
    grad_prob = jnp.einsum(
        "bqhd,bkhd->bhqk", grad_heads, split_heads(value_rows), preferred_element_type=jnp.float32
    )
    grad_values = jnp.einsum(
        "bhqk,bqhd->bkhd", rounded(attn_prob), grad_heads, preferred_element_type=jnp.float32
    )
    grad_scores = attn_prob * (grad_prob - jnp.sum(attn_prob * grad_prob, axis=-1, keepdims=True))
    grad_raw = rounded(grad_scores * score_scale)
    grad_queries = jnp.einsum(
        "bhqk,bkhd->bqhd", grad_raw, split_heads(key_rows), preferred_element_type=jnp.float32
    )
    grad_keys = jnp.einsum(
        "bhqk,bqhd->bkhd", grad_raw, split_heads(queries), preferred_element_type=jnp.float32
    )
    return (
        grad_queries.reshape(queries.shape),
        grad_keys.reshape(key_rows.shape),
        grad_values.reshape(value_rows.shape),
    )


def self_forward(stream, weights):
    norm_gain, query_full, key_full, value_full, out_full = weights
    normed = rounded(layer_norm(stream, norm_gain.astype(jnp.float32)))
    queries = rounded(matmul(normed, query_full))
    key_rows = rounded(matmul(normed, key_full))
    value_rows = rounded(matmul(normed, value_full))
    all_keys, all_values = (
        lax.all_gather(key_rows, "seq", axis=1, tiled=True),
        lax.all_gather(value_rows, "seq", axis=1, tiled=True),
    )
    attn_prob, blended = attend(queries, all_keys, all_values, None)
    return (
        stream + matmul(blended, out_full),
        (normed, queries, all_keys, all_values, attn_prob, blended),
    )


def cross_forward(stream, captions, usable, weights):
    norm_gain, text_full, cquery_full, ckey_full, cvalue_full, cout_full = weights
    normed = rounded(layer_norm(stream, norm_gain.astype(jnp.float32)))
    caption_feat = rounded(matmul(captions, text_full))
    key_rows = rounded(matmul(caption_feat, ckey_full))
    value_rows = rounded(matmul(caption_feat, cvalue_full))
    all_keys, all_values = (
        lax.all_gather(key_rows, "seq", axis=1, tiled=True),
        lax.all_gather(value_rows, "seq", axis=1, tiled=True),
    )
    queries = rounded(matmul(normed, cquery_full))
    attn_prob, blended = attend(queries, all_keys, all_values, usable)
    return (
        stream + matmul(blended, cout_full),
        (normed, caption_feat, queries, all_keys, all_values, attn_prob, blended),
    )


def mlp_forward(stream, weights):
    norm_gain, up_full, down_full = weights
    normed = rounded(layer_norm(stream, norm_gain.astype(jnp.float32)))
    hidden = matmul(normed, up_full)
    active = rounded(exact_gelu(hidden))
    return (stream + matmul(active, down_full), (normed, hidden, active))


def on_device(
    images,
    captions,
    cap_lengths,
    norm1_gain,
    w_query,
    w_key,
    w_value,
    w_out,
    norm2_gain,
    w_text,
    w_cross_query,
    w_cross_key,
    w_cross_value,
    w_cross_out,
    norm3_gain,
    w_up,
    w_down,
    out_grad,
):

    def fetch_self():
        return (
            lax.all_gather(norm1_gain, "dp", axis=0, tiled=True),
            lax.all_gather(w_query, "dp", axis=0, tiled=True),
            lax.all_gather(w_key, "dp", axis=0, tiled=True),
            lax.all_gather(w_value, "dp", axis=0, tiled=True),
            lax.all_gather(w_out, "dp", axis=0, tiled=True),
        )

    def fetch_cross():
        return (
            lax.all_gather(norm2_gain, "dp", axis=0, tiled=True),
            lax.all_gather(w_text, "dp", axis=0, tiled=True),
            lax.all_gather(w_cross_query, "dp", axis=0, tiled=True),
            lax.all_gather(w_cross_key, "dp", axis=0, tiled=True),
            lax.all_gather(w_cross_value, "dp", axis=0, tiled=True),
            lax.all_gather(w_cross_out, "dp", axis=0, tiled=True),
        )

    def fetch_mlp():
        return (
            lax.all_gather(norm3_gain, "dp", axis=0, tiled=True),
            lax.all_gather(w_up, "dp", axis=0, tiled=True),
            lax.all_gather(w_down, "dp", axis=0, tiled=True),
        )

    stream = images.astype(jnp.float32)
    usable = jnp.arange(CAPTION)[None, :] < cap_lengths[:, None]
    self_full = fetch_self()
    after_self, self_kept = self_forward(stream, self_full)
    cross_full = fetch_cross()
    after_cross, cross_kept = cross_forward(after_self, captions, usable, cross_full)
    mlp_full = fetch_mlp()
    layer_sum, mlp_kept = mlp_forward(after_cross, mlp_full)
    layer_out = rounded(layer_sum)
    mlp_full = fetch_mlp()
    norm3_full, up_full, down_full = mlp_full
    normed3, hidden, active = mlp_kept
    grad_top = out_grad.astype(jnp.float32)
    grad_branch = rounded(grad_top)
    grad_down_part = outer_sum(active, grad_branch)
    grad_active = rounded(matmul_t(grad_branch, down_full))
    gelu_value, gelu_pull = jax.vjp(exact_gelu, hidden)
    grad_hidden = rounded(gelu_pull(grad_active.astype(jnp.float32))[0])
    grad_up_part = outer_sum(normed3, grad_hidden)
    grad_normed = matmul_t(grad_hidden, up_full)
    grad_stream_mlp, grad_norm3_part = norm_back(
        after_cross, norm3_full.astype(jnp.float32), grad_normed
    )
    grad_after_cross = grad_top + grad_stream_mlp
    mlp_parts = (
        lax.psum_scatter(grad_norm3_part, "dp", scatter_dimension=0, tiled=True),
        lax.psum_scatter(grad_up_part, "dp", scatter_dimension=0, tiled=True),
        lax.psum_scatter(grad_down_part, "dp", scatter_dimension=0, tiled=True),
    )
    cross_full = fetch_cross()
    norm2_full, text_full, cquery_full, ckey_full, cvalue_full, cout_full = cross_full
    normed2, caption_feat, cross_queries, cross_keys, cross_values, cross_prob, cross_mix = (
        cross_kept
    )
    grad_branch = rounded(grad_after_cross)
    grad_cout_part = outer_sum(cross_mix, grad_branch)
    grad_mix = rounded(matmul_t(grad_branch, cout_full))
    grad_cquery_rows, grad_ckey_rows, grad_cvalue_rows = attend_back(
        cross_queries, cross_keys, cross_values, cross_prob, grad_mix
    )
    own_keys, own_values = (
        lax.psum_scatter(
            grad_ckey_rows.astype(jnp.bfloat16), "seq", scatter_dimension=1, tiled=True
        ).astype(jnp.float32),
        lax.psum_scatter(
            grad_cvalue_rows.astype(jnp.bfloat16), "seq", scatter_dimension=1, tiled=True
        ).astype(jnp.float32),
    )
    own_keys = rounded(own_keys)
    own_values = rounded(own_values)
    grad_cquery_rows = rounded(grad_cquery_rows)
    grad_cquery_part = outer_sum(normed2, grad_cquery_rows)
    grad_ckey_part = outer_sum(caption_feat, own_keys)
    grad_cvalue_part = outer_sum(caption_feat, own_values)
    grad_feat = rounded(matmul_t(own_keys, ckey_full) + matmul_t(own_values, cvalue_full))
    grad_text_part = outer_sum(captions, grad_feat)
    caption_grad = matmul_t(grad_feat, text_full)
    grad_normed = matmul_t(grad_cquery_rows, cquery_full)
    grad_stream_cross, grad_norm2_part = norm_back(
        after_self, norm2_full.astype(jnp.float32), grad_normed
    )
    grad_after_self = grad_after_cross + grad_stream_cross
    cross_parts = (
        lax.psum_scatter(grad_norm2_part, "dp", scatter_dimension=0, tiled=True),
        lax.psum_scatter(grad_text_part, "dp", scatter_dimension=0, tiled=True),
        lax.psum_scatter(grad_cquery_part, "dp", scatter_dimension=0, tiled=True),
        lax.psum_scatter(grad_ckey_part, "dp", scatter_dimension=0, tiled=True),
        lax.psum_scatter(grad_cvalue_part, "dp", scatter_dimension=0, tiled=True),
        lax.psum_scatter(grad_cout_part, "dp", scatter_dimension=0, tiled=True),
    )
    self_full = fetch_self()
    norm1_full, query_full, key_full, value_full, out_full = self_full
    normed1, queries, all_keys, all_values, self_prob, self_mix = self_kept
    grad_branch = rounded(grad_after_self)
    grad_out_part = outer_sum(self_mix, grad_branch)
    grad_mix = rounded(matmul_t(grad_branch, out_full))
    grad_query_rows, grad_key_rows, grad_value_rows = attend_back(
        queries, all_keys, all_values, self_prob, grad_mix
    )
    own_keys, own_values = (
        lax.psum_scatter(
            grad_key_rows.astype(jnp.bfloat16), "seq", scatter_dimension=1, tiled=True
        ).astype(jnp.float32),
        lax.psum_scatter(
            grad_value_rows.astype(jnp.bfloat16), "seq", scatter_dimension=1, tiled=True
        ).astype(jnp.float32),
    )
    own_keys = rounded(own_keys)
    own_values = rounded(own_values)
    grad_query_rows = rounded(grad_query_rows)
    grad_query_part = outer_sum(normed1, grad_query_rows)
    grad_key_part = outer_sum(normed1, own_keys)
    grad_value_part = outer_sum(normed1, own_values)
    grad_normed = (
        matmul_t(grad_query_rows, query_full)
        + matmul_t(own_keys, key_full)
        + matmul_t(own_values, value_full)
    )
    grad_stream_self, grad_norm1_part = norm_back(
        stream, norm1_full.astype(jnp.float32), grad_normed
    )
    image_grad = grad_after_self + grad_stream_self
    self_parts = (
        lax.psum_scatter(grad_norm1_part, "dp", scatter_dimension=0, tiled=True),
        lax.psum_scatter(grad_query_part, "dp", scatter_dimension=0, tiled=True),
        lax.psum_scatter(grad_key_part, "dp", scatter_dimension=0, tiled=True),
        lax.psum_scatter(grad_value_part, "dp", scatter_dimension=0, tiled=True),
        lax.psum_scatter(grad_out_part, "dp", scatter_dimension=0, tiled=True),
    )
    summed = (
        lax.psum(self_parts[0].astype(jnp.bfloat16), "seq").astype(jnp.float32),
        lax.psum(self_parts[1].astype(jnp.bfloat16), "seq").astype(jnp.float32),
        lax.psum(self_parts[2].astype(jnp.bfloat16), "seq").astype(jnp.float32),
        lax.psum(self_parts[3].astype(jnp.bfloat16), "seq").astype(jnp.float32),
        lax.psum(self_parts[4].astype(jnp.bfloat16), "seq").astype(jnp.float32),
        lax.psum(cross_parts[0].astype(jnp.bfloat16), "seq").astype(jnp.float32),
        lax.psum(cross_parts[1].astype(jnp.bfloat16), "seq").astype(jnp.float32),
        lax.psum(cross_parts[2].astype(jnp.bfloat16), "seq").astype(jnp.float32),
        lax.psum(cross_parts[3].astype(jnp.bfloat16), "seq").astype(jnp.float32),
        lax.psum(cross_parts[4].astype(jnp.bfloat16), "seq").astype(jnp.float32),
        lax.psum(cross_parts[5].astype(jnp.bfloat16), "seq").astype(jnp.float32),
        lax.psum(mlp_parts[0].astype(jnp.bfloat16), "seq").astype(jnp.float32),
        lax.psum(mlp_parts[1].astype(jnp.bfloat16), "seq").astype(jnp.float32),
        lax.psum(mlp_parts[2].astype(jnp.bfloat16), "seq").astype(jnp.float32),
    )
    return (
        layer_out,
        image_grad,
        caption_grad,
        summed[0],
        summed[1],
        summed[2],
        summed[3],
        summed[4],
        summed[5],
        summed[6],
        summed[7],
        summed[8],
        summed[9],
        summed[10],
        summed[11],
        summed[12],
        summed[13],
    )


def solution(mesh):
    in_specs = (
        P("dp", "seq", None),
        P("dp", "seq", None),
        P("dp"),
        P("dp"),
        P("dp", None),
        P("dp", None),
        P("dp", None),
        P("dp", None),
        P("dp"),
        P("dp", None),
        P("dp", None),
        P("dp", None),
        P("dp", None),
        P("dp", None),
        P("dp"),
        P("dp", None),
        P("dp", None),
        P("dp", "seq", None),
    )
    out_specs = (
        P("dp", "seq", None),
        P("dp", "seq", None),
        P("dp", "seq", None),
        P("dp"),
        P("dp", None),
        P("dp", None),
        P("dp", None),
        P("dp", None),
        P("dp"),
        P("dp", None),
        P("dp", None),
        P("dp", None),
        P("dp", None),
        P("dp", None),
        P("dp"),
        P("dp", None),
        P("dp", None),
    )
    return jax.shard_map(
        on_device, mesh=mesh, in_specs=in_specs, out_specs=out_specs, check_vma=False
    )
```

profile of v0, /device:TPU:0, one launch (start us, length us, event | category | flops | bytes accessed | tf_op | source)
XLA Modules:
  0.0 4746.2 jit_solution(8715010487798121352)
XLA Ops:
  11.2 23.3 all-gather
  35.2 52.6 %all-gather.25.cloned.1.call-done = bf16[2048,2048]{1,0:T(8,128)(2,1)} async-done(((bf16[128,2048]{1,0:T(8,128)(2,1)}), bf16[2048,2048]{1,0:T(8,128)(2,1)}) %all-gather.25.cloned.1.call-update) | async-done | bytes 8388624 | tf_op jit(solution)/shard_map/all_gather | solution.py:162
  87.9 6.7 fusion.99
  94.7 68.5 %all-gather.19.cloned.1.call-done = bf16[2048,2048]{1,0:T(8,128)(2,1)} async-done(((bf16[128,2048]{1,0:T(8,128)(2,1)}), bf16[2048,2048]{1,0:T(8,128)(2,1)}) %all-gather.19.cloned.1.call-update) | async-done | bytes 8388624 | tf_op jit(solution)/shard_map/all_gather | solution.py:163
  163.2 6.7 fusion.93
  171.3 119.2 %all-gather.31.cloned.1.call-done = bf16[4096,2048]{1,0:T(8,128)(2,1)} async-done(((bf16[256,2048]{1,0:T(8,128)(2,1)}), bf16[4096,2048]{1,0:T(8,128)(2,1)}) %all-gather.31.cloned.1.call-update) | async-done | bytes 16777232 | tf_op jit(solution)/shard_map/all_gather | solution.py:170
  290.5 8.1 fusion.129
  298.7 67.0 %all-gather.39.cloned.1.call-done = bf16[2048,2048]{1,0:T(8,128)(2,1)} async-done(((bf16[128,2048]{1,0:T(8,128)(2,1)}), bf16[2048,2048]{1,0:T(8,128)(2,1)}) %all-gather.39.cloned.1.call-update) | async-done | bytes 8388624 | tf_op jit(solution)/shard_map/all_gather | solution.py:172
  371.2 69.7 %all-gather.33.cloned.1.call-done = bf16[2048,2048]{1,0:T(8,128)(2,1)} async-done(((bf16[128,2048]{1,0:T(8,128)(2,1)}), bf16[2048,2048]{1,0:T(8,128)(2,1)}) %all-gather.33.cloned.1.call-update) | async-done | bytes 8388624 | tf_op jit(solution)/shard_map/all_gather | solution.py:173
  448.3 18.7 all-gather.1
  467.1 17.9 all-gather.2
  485.0 31.1 all-gather.23.cloned.1.call-done
  516.1 5.8 fusion.96
  523.2 26.4 all-gather.27.cloned.1.call-done
  557.9 27.0 all-gather.21.cloned.1.call-done
  590.0 72.0 %all-gather.29.cloned.1.call-done = bf16[2048,2048]{1,0:T(8,128)(2,1)} async-done(((bf16[128,2048]{1,0:T(8,128)(2,1)}), bf16[2048,2048]{1,0:T(8,128)(2,1)}) %all-gather.29.cloned.1.call-update) | async-done | bytes 8388624 | tf_op jit(solution)/shard_map/all_gather | solution.py:164
  662.0 6.3 fusion.219
  668.7 68.5 %all-gather.37.cloned.1.call-done = bf16[2048,2048]{1,0:T(8,128)(2,1)} async-done(((bf16[128,2048]{1,0:T(8,128)(2,1)}), bf16[2048,2048]{1,0:T(8,128)(2,1)}) %all-gather.37.cloned.1.call-update) | async-done | bytes 8388624 | tf_op jit(solution)/shard_map/all_gather | solution.py:171
  737.2 6.7 fusion.105
  746.2 12.7 all-gather.41.cloned.1.call-done
  765.4 16.8 all-gather.35.cloned.1.call-done
  785.6 73.7 %all-gather.43.cloned.1.call-done = bf16[2048,2048]{1,0:T(8,128)(2,1)} async-done(((bf16[128,2048]{1,0:T(8,128)(2,1)}), bf16[2048,2048]{1,0:T(8,128)(2,1)}) %all-gather.43.cloned.1.call-update) | async-done | bytes 8388624 | tf_op jit(solution)/shard_map/all_gather | solution.py:174
  859.3 6.1 fusion.221
  867.2 159.9 %all-gather.45.cloned.1.call-done = bf16[2048,8192]{1,0:T(8,128)(2,1)} async-done(((bf16[128,8192]{1,0:T(8,128)(2,1)}), bf16[2048,8192]{1,0:T(8,128)(2,1)}) %all-gather.45.cloned.1.call-update) | async-done | bytes 33554448 | tf_op jit(solution)/shard_map/all_gather | solution.py:180
  1027.1 22.2 fusion.147
  1049.3 147.3 %all-gather.47.cloned.1.call-done = bf16[8192,2048]{1,0:T(8,128)(2,1)} async-done(((bf16[512,2048]{1,0:T(8,128)(2,1)}), bf16[8192,2048]{1,0:T(8,128)(2,1)}) %all-gather.47.cloned.1.call-update) | async-done | bytes 33554448 | tf_op jit(solution)/shard_map/all_gather | solution.py:181
  1196.7 35.0 fusion.24
  1231.7 18.5 multiply_reduce_fusion.2
  1255.8 6.7 fusion.108
  1287.7 6.4 multiply_reduce_fusion.4
  1302.1 6.8 fusion.102
  1315.9 30.3 fusion.150
  1359.3 30.2 fusion.162
  1389.5 10.1 convolution_bitcast_fusion.10
  1399.6 10.1 convolution_bitcast_fusion.7
  1409.8 9.5 convolution_bitcast_fusion.6
  1420.8 7.6 convolution_bitcast_fusion.3
  1429.5 12.5 convolution_bitcast_fusion.5
  1442.1 9.8 convolution_bitcast_fusion.4
  1453.1 9.8 convolution_bitcast_fusion.9
  1463.0 9.5 convolution_bitcast_fusion.8
  1473.6 6.3 fusion.31
  1480.0 6.4 fusion.126
  1487.2 13.7 convolution_bitcast_fusion.2
  1502.5 26.2 convolution_bitcast_fusion.1
  1529.9 35.5 convolution_bitcast_fusion
  1567.3 32.1 reduce-scatter.24.cloned.1.call-done
  1601.5 179.7 %reduce-scatter.30.cloned.1.call-done = f32[128,2048]{1,0:T(8,128)} async-done(((f32[2048,2048]{1,0:T(8,128)}), f32[128,2048]{1,0:T(8,128)}) %reduce-scatter.30.cloned.1.call-update) | async-done | bytes 1048592 | tf_op jit(solution)/shard_map/reduce_scatter | solution.py:291
  1783.2 179.6 %reduce-scatter.34.cloned.1.call-done = f32[128,2048]{1,0:T(8,128)} async-done(((f32[2048,2048]{1,0:T(8,128)}), f32[128,2048]{1,0:T(8,128)}) %reduce-scatter.34.cloned.1.call-update) | async-done | bytes 1048592 | tf_op jit(solution)/shard_map/reduce_scatter | solution.py:249
  1964.9 179.6 %reduce-scatter.40.cloned.1.call-done = f32[128,2048]{1,0:T(8,128)} async-done(((f32[2048,2048]{1,0:T(8,128)}), f32[128,2048]{1,0:T(8,128)}) %reduce-scatter.40.cloned.1.call-update) | async-done | bytes 1048592 | tf_op jit(solution)/shard_map/reduce_scatter | solution.py:252
  2146.6 179.4 %reduce-scatter.36.cloned.1.call-done = f32[128,2048]{1,0:T(8,128)} async-done(((f32[2048,2048]{1,0:T(8,128)}), f32[128,2048]{1,0:T(8,128)}) %reduce-scatter.36.cloned.1.call-update) | async-done | bytes 1048592 | tf_op jit(solution)/shard_map/reduce_scatter | solution.py:250
  2328.2 179.6 %reduce-scatter.38.cloned.1.call-done = f32[128,2048]{1,0:T(8,128)} async-done(((f32[2048,2048]{1,0:T(8,128)}), f32[128,2048]{1,0:T(8,128)}) %reduce-scatter.38.cloned.1.call-update) | async-done | bytes 1048592 | tf_op jit(solution)/shard_map/reduce_scatter | solution.py:251
  2509.9 179.4 %reduce-scatter.26.cloned.1.call-done = f32[128,2048]{1,0:T(8,128)} async-done(((f32[2048,2048]{1,0:T(8,128)}), f32[128,2048]{1,0:T(8,128)}) %reduce-scatter.26.cloned.1.call-update) | async-done | bytes 1048592 | tf_op jit(solution)/shard_map/reduce_scatter | solution.py:289
  2691.4 179.5 %reduce-scatter.28.cloned.1.call-done = f32[128,2048]{1,0:T(8,128)} async-done(((f32[2048,2048]{1,0:T(8,128)}), f32[128,2048]{1,0:T(8,128)}) %reduce-scatter.28.cloned.1.call-update) | async-done | bytes 1048592 | tf_op jit(solution)/shard_map/reduce_scatter | solution.py:290
  2872.9 334.1 %reduce-scatter.32.cloned.1.call-done = f32[256,2048]{0,1:T(8,128)} async-done(((f32[4096,2048]{0,1:T(8,128)}), f32[256,2048]{0,1:T(8,128)}) %reduce-scatter.32.cloned.1.call-update) | async-done | bytes 2097168 | tf_op jit(solution)/shard_map/reduce_scatter | solution.py:248
  3209.7 637.4 %reduce-scatter.42.cloned.1.call-done = f32[128,8192]{1,0:T(8,128)} async-done(((f32[2048,8192]{1,0:T(8,128)}), f32[128,8192]{1,0:T(8,128)}) %reduce-scatter.42.cloned.1.call-update) | async-done | bytes 4194320 | tf_op jit(solution)/shard_map/reduce_scatter | solution.py:210
  3850.8 636.1 %reduce-scatter.44.cloned.1.call-done = f32[512,2048]{1,0:T(8,128)} async-done(((f32[8192,2048]{1,0:T(8,128)}), f32[512,2048]{1,0:T(8,128)}) %reduce-scatter.44.cloned.1.call-update) | async-done | bytes 4194320 | tf_op jit(solution)/shard_map/reduce_scatter | solution.py:211
  4490.7 31.8 fusion.90
  4522.6 13.2 fusion.12
  4535.8 5.9 fusion.47
  4541.7 6.3 fusion.79
  4548.1 6.0 fusion.137
  4556.3 59.8 %all-reduce.3 = (bf16[2048]{0:T(1024)(128)(2,1)S(1)}, bf16[2048]{0:T(1024)(128)(2,1)S(1)}, bf16[2048]{0:T(1024)(128)(2,1)S(1)}) all-reduce(f32[2048]{0:T(1024)S(1)} %get-tuple-element.57, f32[2048]{0:T(1024)S(1)} %copy-done.47, f32[2048]{0:T(1024)S(1)} %copy-done.56), channel_id=6, replica_groups=mesh['dp'=16,'seq'=2] {'dp'}, use_global_device_ids=true, to_apply=%region_23.24.clone | all-reduce | flops 6144 | bytes 36864
  4626.7 90.4 %all-reduce.8.cloned.1.call-done = (bf16[256,2048]{0,1:T(8,128)(2,1)}, bf16[128,2048]{1,0:T(8,128)(2,1)}, bf16[128,2048]{1,0:T(8,128)(2,1)}, bf16[128,2048]{1,0:...) async-done(((bf16[256,2048]{0,1:T(8,128)(2,1)}, ...) | async-done | bytes 9437200 | tf_op jit(solution)/shard_map/psum | solution.py:300
  (266 shorter events, 178.0 us)
Async XLA Ops:
  7.2 283.4 %copy-start = (bf16[2,64,4096]{2,1,0:T(8,128)(2,1)S(1)}, bf16[2,64,4096]{2,1,0:T(8,128)(2,1)}, u32[]{:S(2)}) copy-start(bf16[2,64,4096]{2,1,0:T(8,128)(2,1)} %param.19) | copy-start | bytes 3145732
  7.2 27.3 copy-start.2
  7.2 80.6 %all-gather.25.cloned.1.call-start = ((), (), s32[]{:S(2)}) async-start(), calls=%async_computation.18 | async-start | bytes 8912896 | tf_op jit(solution)/shard_map/all_gather | solution.py:162
  8.0 155.3 %all-gather.19.cloned.1.call-start = ((), (), s32[]{:S(2)}) async-start(), calls=%async_computation.15 | async-start | bytes 8912896 | tf_op jit(solution)/shard_map/all_gather | solution.py:163
  8.7 281.8 %all-gather.31.cloned.1.call-start = ((), (), s32[]{:S(2)}) async-start(), calls=%async_computation.21 | async-start | bytes 17825792 | tf_op jit(solution)/shard_map/all_gather | solution.py:170
  9.4 356.2 %all-gather.39.cloned.1.call-start = ((), (), s32[]{:S(2)}) async-start(), calls=%async_computation.25 | async-start | bytes 8912896 | tf_op jit(solution)/shard_map/all_gather | solution.py:172
  10.0 430.8 %all-gather.33.cloned.1.call-start = ((), (), s32[]{:S(2)}) async-start(), calls=%async_computation.22 | async-start | bytes 8912896 | tf_op jit(solution)/shard_map/all_gather | solution.py:173
  10.6 505.5 %all-gather.23.cloned.1.call-start = ((), (), s32[]{:S(2)}) async-start(), calls=%async_computation.17 | async-start | bytes 8912896 | tf_op jit(solution)/shard_map/all_gather | solution.py:161
  11.2 538.5 %all-gather.27.cloned.1.call-start = ((), (), s32[]{:S(2)}) async-start(), calls=%async_computation.19 | async-start | bytes 3145728 | tf_op jit(solution)/shard_map/all_gather | solution.py:101
  34.5 481.6 %copy-start.34 = (f32[16,1,128]{2,1,0:T(1,128)}, f32[16,1,128]{2,1,0:T(1,128)S(1)}, u32[]{:S(2)}) copy-start(f32[16,1,128]{2,1,0:T(1,128)S(1)} %convert_element_type.338) | copy-start | bytes 24580
  34.8 481.3 %copy-start.37 = (f32[2,128]{1,0:T(2,128)}, f32[2,128]{1,0:T(2,128)S(1)}, u32[]{:S(2)}) copy-start(f32[2,128]{1,0:T(2,128)S(1)} %broadcast_multiply_fusion.2) | copy-start | bytes 3076
  35.2 59.4 %copy-start.54 = (f32[2,128]{1,0:T(2,128)}, f32[2,128]{1,0:T(2,128)S(1)}, u32[]{:S(2)}) copy-start(f32[2,128]{1,0:T(2,128)S(1)} %fusion.136) | copy-start | bytes 3076
  35.2 480.9 %copy-start.42 = (f32[2,128]{1,0:T(2,128)}, f32[2,128]{1,0:T(2,128)S(1)}, u32[]{:S(2)}) copy-start(f32[2,128]{1,0:T(2,128)S(1)} %fusion.195) | copy-start | bytes 3076
  94.6 490.3 %all-gather.21.cloned.1.call-start = ((), (), s32[]{:S(2)}) async-start(), calls=%async_computation.16 | async-start | bytes 3145728 | tf_op jit(solution)/shard_map/all_gather | solution.py:102
  170.0 492.0 %all-gather.29.cloned.1.call-start = ((), (), s32[]{:S(2)}) async-start(), calls=%async_computation.20 | async-start | bytes 8912896 | tf_op jit(solution)/shard_map/all_gather | solution.py:164
  170.7 566.5 %all-gather.37.cloned.1.call-start = ((), (), s32[]{:S(2)}) async-start(), calls=%async_computation.24 | async-start | bytes 8912896 | tf_op jit(solution)/shard_map/all_gather | solution.py:171
  171.3 587.6 %all-gather.41.cloned.1.call-start = ((), (), s32[]{:S(2)}) async-start(), calls=%async_computation.26 | async-start | bytes 1572864 | tf_op jit(solution)/shard_map/all_gather | solution.py:118
  298.7 142.2 %copy-start.10 = (bf16[2,64,2048]{2,1,0:T(8,128)(2,1)}, bf16[2,64,2048]{2,1,0:T(8,128)(2,1)S(1)}, u32[]{:S(2)}) copy-start(bf16[2,64,2048]{2,1,0:T(8,128)(2,1)S(1)} %fusion.129) | copy-start | bytes 1572868
  371.1 411.1 %all-gather.35.cloned.1.call-start = ((), (), s32[]{:S(2)}) async-start(), calls=%async_computation.23 | async-start | bytes 1572864 | tf_op jit(solution)/shard_map/all_gather | solution.py:119
  446.3 20.8 copy-start.58
  446.3 38.7 copy-start.59
  446.3 413.0 %all-gather.43.cloned.1.call-start = ((), (), s32[]{:S(2)}) async-start(), calls=%async_computation.27 | async-start | bytes 8912896 | tf_op jit(solution)/shard_map/all_gather | solution.py:174
  447.1 580.0 %all-gather.45.cloned.1.call-start = ((), (), s32[]{:S(2)}) async-start(), calls=%async_computation.28 | async-start | bytes 35651584 | tf_op jit(solution)/shard_map/all_gather | solution.py:180
  447.7 749.0 %all-gather.47.cloned.1.call-start = ((), (), s32[]{:S(2)}) async-start(), calls=%async_computation.29 | async-start | bytes 35651584 | tf_op jit(solution)/shard_map/all_gather | solution.py:181
  448.2 980.2 %reduce-scatter.20.cloned.1.call-start = ((), (), s32[]{:S(2)}) async-start(), calls=%async_computation.32 | async-start | bytes 1572864 | tf_op jit(solution)/shard_map/reduce_scatter | solution.py:225
  485.0 765.3 %copy-start.30 = (f32[16,1,128]{2,1,0:T(1,128)}, f32[16,1,128]{2,1,0:T(1,128)S(1)}, u32[]{:S(2)}) copy-start(f32[16,1,128]{2,1,0:T(1,128)S(1)} %convert_element_type.340) | copy-start | bytes 24580
  552.5 37.5 copy-start.12
  557.9 32.1 copy-start.50
  668.7 75.2 %copy-start.52 = (f32[2,128]{1,0:T(2,128)}, f32[2,128]{1,0:T(2,128)S(1)}, u32[]{:S(2)}) copy-start(f32[2,128]{1,0:T(2,128)S(1)} %multiply_reduce_fusion.8) | copy-start | bytes 3076
  668.7 75.2 %copy-start.48 = (f32[2,128]{1,0:T(2,128)}, f32[2,128]{1,0:T(2,128)S(1)}, u32[]{:S(2)}) copy-start(f32[2,128]{1,0:T(2,128)S(1)} %fusion.196) | copy-start | bytes 3076
  865.5 384.8 %copy-start.40 = (f32[2,128]{1,0:T(2,128)}, f32[2,128]{1,0:T(2,128)S(1)}, u32[]{:S(2)}) copy-start(f32[2,128]{1,0:T(2,128)S(1)} %broadcast_multiply_fusion) | copy-start | bytes 3076
  867.2 383.1 %copy-start.45 = (f32[2,128]{1,0:T(2,128)}, f32[2,128]{1,0:T(2,128)S(1)}, u32[]{:S(2)}) copy-start(f32[2,128]{1,0:T(2,128)S(1)} %fusion.197) | copy-start | bytes 3076
  1276.0 166.0 %reduce-scatter.22.cloned.1.call-start = ((), (), s32[]{:S(2)}) async-start(), calls=%async_computation.33 | async-start | bytes 1572864 | tf_op jit(solution)/shard_map/reduce_scatter | solution.py:228
  1287.7 6.4 copy-start.53
  1287.7 7.7 copy-start.49
  1296.8 155.1 %reduce-scatter.16.cloned.1.call-start = ((), (), s32[]{:S(2)}) async-start(), calls=%async_computation.30 | async-start | bytes 3145728 | tf_op jit(solution)/shard_map/reduce_scatter | solution.py:264
  1350.3 112.7 %reduce-scatter.18.cloned.1.call-start = ((), (), s32[]{:S(2)}) async-start(), calls=%async_computation.31 | async-start | bytes 3145728 | tf_op jit(solution)/shard_map/reduce_scatter | solution.py:267
  1359.0 30.5 copy-start.35
  1359.0 30.5 copy-start.38
  1359.1 30.5 copy-start.43
  1359.1 240.3 %reduce-scatter.24.cloned.1.call-start = ((), (), s32[]{:S(2)}) async-start(), calls=%async_computation.34 | async-start | bytes 17825792 | tf_op jit(solution)/shard_map/reduce_scatter | solution.py:288
  1399.6 381.5 %reduce-scatter.30.cloned.1.call-start = ((), (), s32[]{:S(2)}) async-start(), calls=%async_computation.37 | async-start | bytes 17825792 | tf_op jit(solution)/shard_map/reduce_scatter | solution.py:291
  1409.7 553.1 %reduce-scatter.34.cloned.1.call-start = ((), (), s32[]{:S(2)}) async-start(), calls=%async_computation.39 | async-start | bytes 17825792 | tf_op jit(solution)/shard_map/reduce_scatter | solution.py:249
  1419.3 725.2 %reduce-scatter.40.cloned.1.call-start = ((), (), s32[]{:S(2)}) async-start(), calls=%async_computation.42 | async-start | bytes 17825792 | tf_op jit(solution)/shard_map/reduce_scatter | solution.py:252
  1428.4 897.6 %reduce-scatter.36.cloned.1.call-start = ((), (), s32[]{:S(2)}) async-start(), calls=%async_computation.40 | async-start | bytes 17825792 | tf_op jit(solution)/shard_map/reduce_scatter | solution.py:250
  1442.0 1065.8 %reduce-scatter.38.cloned.1.call-start = ((), (), s32[]{:S(2)}) async-start(), calls=%async_computation.41 | async-start | bytes 17825792 | tf_op jit(solution)/shard_map/reduce_scatter | solution.py:251
  1451.9 1237.4 %reduce-scatter.26.cloned.1.call-start = ((), (), s32[]{:S(2)}) async-start(), calls=%async_computation.35 | async-start | bytes 17825792 | tf_op jit(solution)/shard_map/reduce_scatter | solution.py:289
  1463.0 1407.9 %reduce-scatter.28.cloned.1.call-start = ((), (), s32[]{:S(2)}) async-start(), calls=%async_computation.36 | async-start | bytes 17825792 | tf_op jit(solution)/shard_map/reduce_scatter | solution.py:290
  1472.6 7.4 copy-start.23
  1472.6 1734.4 %reduce-scatter.32.cloned.1.call-start = ((), (), s32[]{:S(2)}) async-start(), calls=%async_computation.38 | async-start | bytes 35651584 | tf_op jit(solution)/shard_map/reduce_scatter | solution.py:248
  1500.9 2346.1 %reduce-scatter.42.cloned.1.call-start = ((), (), s32[]{:S(2)}) async-start(), calls=%async_computation.43 | async-start | bytes 71303168 | tf_op jit(solution)/shard_map/reduce_scatter | solution.py:210
  1528.7 2958.1 %reduce-scatter.44.cloned.1.call-start = ((), (), s32[]{:S(2)}) async-start(), calls=%async_computation.44 | async-start | bytes 71303168 | tf_op jit(solution)/shard_map/reduce_scatter | solution.py:211
  1565.4 3151.7 %all-reduce.8.cloned.1.call-start = ((), (), s32[]{:S(2)}) async-start(), calls=%async_computation.45 | async-start | bytes 18874368 | tf_op jit(solution)/shard_map/psum | solution.py:300
  4490.7 31.8 copy-start.16
  4522.6 13.2 copy-start.26
  4541.6 6.3 copy-start.4
  4548.0 7.4 copy-start.44
  4548.0 8.3 copy-start.47
  4548.1 8.3 copy-start.56
  4554.1 68.8 %copy-start.8 = (f32[2,128,2048]{2,1,0:T(8,128)S(1)}, f32[2,128,2048]{2,1,0:T(8,128)}, u32[]{:S(2)}) copy-start(f32[2,128,2048]{2,1,0:T(8,128)} %copy-done.7) | copy-start | bytes 6291460
  4717.1 6.5 copy-start.33
  4717.1 7.5 copy-start.29
  4724.7 9.2 copy-start.25
  4726.4 6.4 copy-start.32
  (28 other events, 73.4 us)
Sparse Core Ops, SparseCore 0:
  10.2 77.6 all-gather.24
  90.0 73.1 all-gather.18
  165.4 125.1 all-gather.30
  292.6 73.0 all-gather.38
  367.7 73.1 all-gather.32
  442.9 73.1 all-gather.22
  518.2 31.3 all-gather.26
  551.7 33.1 all-gather.20
  587.1 74.8 all-gather.28
  664.0 73.1 all-gather.36
  739.3 19.5 all-gather.40
  760.9 21.2 all-gather.34
  784.4 74.8 all-gather.42
  860.8 166.2 all-gather.44
  1028.6 168.0 all-gather.46
  1276.2 20.3 reduce-scatter.19
  1299.3 20.3 reduce-scatter.21
  1350.4 32.0 reduce-scatter.15
  1384.8 31.9 reduce-scatter.17
  1420.7 178.5 reduce-scatter.23
  1603.5 177.5 reduce-scatter.29
  1785.2 177.5 reduce-scatter.33
  1966.9 177.5 reduce-scatter.39
  2148.5 177.5 reduce-scatter.35
  2330.2 177.5 reduce-scatter.37
  2511.8 177.4 reduce-scatter.25
  2693.2 177.5 reduce-scatter.27
  2875.1 331.8 reduce-scatter.31
  3211.3 635.7 reduce-scatter.41
  3851.1 635.6 reduce-scatter.43
  4492.1 224.9 all-reduce.7
where the time goes:
time: 4760 us; the launch traced here: 4750 us
  waiting for transfers between devices  4010 us (84%)
  matrix products  489 us (10%)
  blocking collectives  125 us (3%)
  other arithmetic  62.8 us (1%)
    reduce_scatter x1, waiting for transfers between devices, on_device(): lax.psum_scatter(grad_up_part, 'dp', scatter_dimension=0, tiled=True)  637 us
    reduce_scatter x1, waiting for transfers between devices, on_device(): lax.psum_scatter(grad_down_part, 'dp', scatter_dimension=0, tiled=True)  636 us
    reduce_scatter x1, waiting for transfers between devices, on_device(): lax.psum_scatter(grad_text_part, 'dp', scatter_dimension=0, tiled=True)  334 us
    reduce_scatter x1, waiting for transfers between devices, on_device(): lax.psum_scatter(grad_out_part, 'dp', scatter_dimension=0, tiled=True)  180 us
    reduce_scatter x1, waiting for transfers between devices, on_device(): lax.psum_scatter(grad_cvalue_part, 'dp', scatter_dimension=0, tiled=True)  180 us
    reduce_scatter x1, waiting for transfers between devices, on_device(): lax.psum_scatter(grad_cquery_part, 'dp', scatter_dimension=0, tiled=True)  180 us
    reduce_scatter x1, waiting for transfers between devices, on_device(): lax.psum_scatter(grad_cout_part, 'dp', scatter_dimension=0, tiled=True)  180 us
    reduce_scatter x1, waiting for transfers between devices, on_device(): lax.psum_scatter(grad_value_part, 'dp', scatter_dimension=0, tiled=True)  179 us
  transfers between devices with their start and end apart: 31, of which 27 were waited for; matrix products, arithmetic and copies ran while one was open for 10% of the time, Pallas kernels for 0%

commit v1 on v0

v1 whole, which is shorter than its diff:
```python
import functools

import jax
import jax.numpy as jnp
from jax import lax
from jax.experimental import pallas as pl
from jax.experimental.pallas import tpu as pltpu
from jax.sharding import PartitionSpec as P

HEADS = 16
HEAD_DIM = 128
EPSILON = 1e-05
SCALE = HEAD_DIM ** (-0.5)
BF16 = jnp.bfloat16
F32 = jnp.float32
TP_HEADS = HEADS // 4
TP_WIDTH = TP_HEADS * HEAD_DIM


def rounded(values):
    return values.astype(BF16)


def mm(left, right):
    return lax.dot_general(left, right, (((1,), (0,)), ((), ())), preferred_element_type=F32)


def mm_t(left, right):
    return lax.dot_general(left, right, (((1,), (1,)), ((), ())), preferred_element_type=F32)


def outer(left, right):
    return lax.dot_general(left, right, (((0,), (0,)), ((), ())), preferred_element_type=F32)


def layer_norm(values, norm_gain):
    centred = values - jnp.mean(values, axis=-1, keepdims=True)
    spread = jnp.mean(centred * centred, axis=-1, keepdims=True)
    return centred * lax.rsqrt(spread + EPSILON) * norm_gain


def norm_back(values, norm_gain, grad_normed):
    centred = values - jnp.mean(values, axis=-1, keepdims=True)
    inverse = lax.rsqrt(jnp.mean(centred * centred, axis=-1, keepdims=True) + EPSILON)
    unit = centred * inverse
    scaled = grad_normed * norm_gain
    result = inverse * (
        scaled
        - jnp.mean(scaled, axis=-1, keepdims=True)
        - unit * jnp.mean(scaled * unit, axis=-1, keepdims=True)
    )
    return result, jnp.sum(grad_normed * unit, axis=tuple(range(values.ndim - 1)))


def exact_gelu(values):
    return jax.nn.gelu(values, approximate=False)


def dot_nt(left, right):
    return lax.dot_general(left, right, (((1,), (1,)), ((), ())), preferred_element_type=F32)


def dot_nn(left, right):
    return lax.dot_general(left, right, (((1,), (0,)), ((), ())), preferred_element_type=F32)


def dot_tn(left, right):
    return lax.dot_general(left, right, (((0,), (0,)), ((), ())), preferred_element_type=F32)


def soft(queries, keys, usable):
    scores = dot_nt(queries, keys) * SCALE
    if usable is not None:
        scores = jnp.where(usable, scores, -1e30)
    grown = jnp.exp(scores - jnp.max(scores, axis=-1, keepdims=True))
    return grown / jnp.sum(grown, axis=-1, keepdims=True)


def cut(ref, index):
    return ref[0, :, index * HEAD_DIM : (index + 1) * HEAD_DIM]


def put(ref, index, values):
    ref[0, :, index * HEAD_DIM : (index + 1) * HEAD_DIM] = values.astype(ref.dtype)


def attend_body(query_ref, query_at, pair_ref, key_at, value_at, usable, mix_ref):
    for head in range(TP_HEADS):
        prob = soft(cut(query_ref, query_at + head), cut(pair_ref, key_at + head), usable)
        put(mix_ref, head, dot_nn(rounded(prob), cut(pair_ref, value_at + head)))


def attend_back_body(
    query_ref, query_at, pair_ref, key_at, value_at, usable, grad_ref, gquery_ref, gpair_ref
):
    for head in range(TP_HEADS):
        queries = cut(query_ref, query_at + head)
        keys = cut(pair_ref, key_at + head)
        values = cut(pair_ref, value_at + head)
        grad_mix = cut(grad_ref, head)
        prob = soft(queries, keys, usable)
        grad_prob = dot_nt(grad_mix, values)
        put(gpair_ref, value_at + head, dot_tn(rounded(prob), grad_mix))
        grad_scores = prob * (grad_prob - jnp.sum(prob * grad_prob, axis=-1, keepdims=True))
        grad_raw = rounded(grad_scores * SCALE)
        put(gquery_ref, query_at + head, dot_nn(grad_raw, keys))
        put(gpair_ref, key_at + head, dot_tn(grad_raw, queries))


def self_kernel(qkv_ref, mix_ref):
    attend_body(qkv_ref, 0, qkv_ref, TP_HEADS, 2 * TP_HEADS, None, mix_ref)


def self_back_kernel(qkv_ref, grad_ref, gqkv_ref):
    attend_back_body(
        qkv_ref, 0, qkv_ref, TP_HEADS, 2 * TP_HEADS, None, grad_ref, gqkv_ref, gqkv_ref
    )


def cross_kernel(query_ref, pair_ref, usable_ref, mix_ref):
    attend_body(query_ref, 0, pair_ref, 0, TP_HEADS, usable_ref[0] > 0, mix_ref)


def cross_back_kernel(query_ref, pair_ref, usable_ref, grad_ref, gquery_ref, gpair_ref):
    attend_back_body(
        query_ref, 0, pair_ref, 0, TP_HEADS, usable_ref[0] > 0, grad_ref, gquery_ref, gpair_ref
    )


def per_image(kernel, outs, *args):
    images = args[0].shape[0]

    def block(shape):
        return pl.BlockSpec((1,) + tuple(shape[1:]), lambda i: (i, 0, 0))

    many = [jax.ShapeDtypeStruct(shape, BF16) for shape in outs]
    return pl.pallas_call(
        kernel,
        grid=(images,),
        in_specs=[block(arg.shape) for arg in args],
        out_specs=[block(shape) for shape in outs],
        out_shape=many,
        compiler_params=pltpu.CompilerParams(vmem_limit_bytes=32 * 1024 * 1024),
    )(*args)


def make(devices):
    planes = 4
    spread = devices // (2 * planes)
    half_spread = spread // 2
    groups = [
        [(a * 2 + y) * spread + b for a in range(planes) for b in range(spread)] for y in range(2)
    ]

    def swap(values, over_y, over_x):
        if not over_y:
            return lax.ppermute(values, "seq", [(0, 1), (1, 0)])
        if not over_x:
            return lax.ppermute(values, "dp", [(d, d ^ spread) for d in range(devices)])
        pairs = [(2 * d + x, 2 * (d ^ spread) + 1 - x) for d in range(devices) for x in range(2)]
        return lax.ppermute(values, ("dp", "seq"), pairs)

    def shuffle(values):
        lead = values.shape[:-1]
        blocks = values.reshape(lead + (planes, 2, spread, -1))
        return jnp.swapaxes(blocks, -3, -2).reshape(values.shape)

    def unshuffle(values):
        lead = values.shape[:-1]
        blocks = values.reshape(lead + (planes, spread, 2, -1))
        return jnp.swapaxes(blocks, -3, -2).reshape(values.shape)

    def gather_tokens(own):
        over_x, over_y, over_both = swap(own, 0, 1), swap(own, 1, 0), swap(own, 1, 1)
        near = jnp.stack([own, over_x], axis=1)
        far = jnp.stack([over_y, over_both], axis=1)
        images, tokens, features = own.shape
        return jnp.stack([near, far]).reshape(2 * images, 2 * tokens, features)

    def scatter_tokens(parts):
        images, tokens, features = parts.shape
        parts = parts.reshape(2, images // 2, 2, tokens // 2, features)
        total = parts[0, :, 0].astype(F32) + swap(parts[0, :, 1], 0, 1).astype(F32)
        total = total + swap(parts[1, :, 0], 1, 0).astype(F32)
        return total + swap(parts[1, :, 1], 1, 1).astype(F32)

    def gather_weight(payload):
        return lax.all_gather(payload, "dp", axis=0, tiled=True, axis_index_groups=groups)

    def reduce_weight(parts):
        return lax.psum_scatter(
            parts, "dp", scatter_dimension=0, tiled=True, axis_index_groups=groups
        )

    def on_device(
        images,
        captions,
        cap_lengths,
        norm1_gain,
        w_query,
        w_key,
        w_value,
        w_out,
        norm2_gain,
        w_text,
        w_cross_query,
        w_cross_key,
        w_cross_value,
        w_cross_out,
        norm3_gain,
        w_up,
        w_down,
        out_grad,
    ):
        d = lax.axis_index("dp")
        x = lax.axis_index("seq")
        y = (d // spread) % 2
        top = (d % spread) // half_spread
        d_model = images.shape[-1]
        ff_rows = w_down.shape[0]
        ff = ff_rows * devices
        group_images, group_tokens = 2 * images.shape[0], 2 * images.shape[1]
        slots = 2 * captions.shape[1]


        def head_columns(weight, yy):
            first = (2 * yy + x) * HEAD_DIM
            return [
                lax.dynamic_slice_in_dim(weight, 4 * HEAD_DIM * a + first, HEAD_DIM, 1)
                for a in range(planes)
            ]

        def heads_of(weights, yy):
            return jnp.concatenate([c for w in weights for c in head_columns(w, yy)], axis=1)

        def up_columns(yy):
            return jnp.concatenate(
                [
                    lax.dynamic_slice_in_dim(
                        w_up,
                        ((a * 2 + yy) * spread + b) * ff_rows + x * (ff_rows // 2),
                        ff_rows // 2,
                        1,
                    )
                    for a in range(planes)
                    for b in range(spread)
                ],
                axis=1,
            )

        def text_columns(yy):
            return lax.dynamic_slice_in_dim(w_text, (2 * yy + x) * TP_WIDTH, TP_WIDTH, 1)

        def both_rows(columns):
            own, other = columns(y), swap(columns(1 - y), 1, 0)
            first = jnp.where(y == 0, own, other)
            second = jnp.where(y == 0, other, own)
            return jnp.concatenate([first, second], axis=0)

        def pass_top(values):
            return lax.ppermute(values, "dp", [(i, i ^ half_spread) for i in range(devices)])

        def head_rows(weight):
            half = weight.shape[0] // 2
            kept = lax.dynamic_slice_in_dim(weight, top * half, half, 0)
            passed = lax.dynamic_slice_in_dim(weight, (1 - top) * half, half, 0)
            payload = jnp.where(top == x, kept, pass_top(passed))
            full = gather_weight(payload).reshape(planes, 2, half_spread, half, -1)
            return jnp.swapaxes(full, 1, 2).reshape(TP_WIDTH, -1)

        image_all = gather_tokens(shuffle(images))
        qkv_full = gather_weight(
            both_rows(lambda yy: heads_of((w_query, w_key, w_value), yy))
        )
        gains = lax.all_gather(
            jnp.stack([norm1_gain, norm2_gain, norm3_gain]), "dp", axis=1, tiled=True
        ).astype(F32)
        out_full = head_rows(w_out)
        caption_all = gather_tokens(shuffle(captions)).reshape(group_images * slots, -1)
        text_full = gather_weight(both_rows(text_columns))
        cross_full = gather_weight(
            both_rows(lambda yy: heads_of((w_cross_query, w_cross_key, w_cross_value), yy))
        )
        cquery_full, cpair_full = cross_full[:, :TP_WIDTH], cross_full[:, TP_WIDTH:]
        cout_full = head_rows(w_cross_out)
        up_full = gather_weight(both_rows(up_columns))
        down_full = gather_weight(
            lax.dynamic_slice_in_dim(w_down, x * (ff_rows // 2), ff_rows // 2, 0)
        )
        out_grad_all = gather_tokens(out_grad).reshape(-1, d_model)

        all_lengths = jnp.concatenate([cap_lengths, swap(cap_lengths, 1, 0)])
        position = jnp.arange(slots // 2)
        place = jnp.concatenate([x * (slots // 2) + position, (1 - x) * (slots // 2) + position])
        usable = (place[None, :] < all_lengths[:, None]).astype(F32)[:, None, :]

        stream = images.astype(F32)
        normed1 = rounded(layer_norm(image_all.astype(F32), shuffle(gains[0])))
        normed1 = normed1.reshape(-1, d_model)
        qkv = rounded(mm(normed1, qkv_full)).reshape(group_images, group_tokens, -1)
        (self_mix,) = per_image(
            self_kernel, [(group_images, group_tokens, TP_WIDTH)], qkv
        )
        self_mix = self_mix.reshape(-1, TP_WIDTH)
        self_part = rounded(mm(self_mix, out_full)).reshape(group_images, group_tokens, d_model)
        after_self = stream + scatter_tokens(self_part)

        quarter = 2 * y + x
        part_feat = rounded(mm(caption_all, text_full))

        def inner_shuffle(values, back):
            outer_dim, inner_dim = (spread, 2) if back else (2, spread)
            blocks = values.reshape(values.shape[0], outer_dim, inner_dim, -1)
            return jnp.swapaxes(blocks, 1, 2).reshape(values.shape)

        def swap_slots(values, ky, kx):
            rows = swap(values, ky, kx).reshape(2, group_images // 2, 2, slots // 2, -1)
            rows = rows[::-1] if ky else rows
            rows = rows[:, :, ::-1] if kx else rows
            return rows.reshape(values.shape)

        part_feat = inner_shuffle(part_feat, False)
        caption_feat = jnp.zeros((group_images * slots, d_model), BF16)
        for ky in range(2):
            for kx in range(2):
                piece = swap_slots(part_feat, ky, kx) if ky or kx else part_feat
                caption_feat = lax.dynamic_update_slice(
                    caption_feat, piece, (0, (quarter ^ (2 * ky + kx)) * TP_WIDTH)
                )
        cpair = rounded(mm(caption_feat, cpair_full)).reshape(group_images, slots, -1)

        normed2 = rounded(layer_norm(after_self, gains[1]))
        normed2 = gather_tokens(shuffle(normed2)).reshape(-1, d_model)
        cquery = rounded(mm(normed2, cquery_full)).reshape(group_images, group_tokens, -1)
        (cross_mix,) = per_image(
            cross_kernel, [(group_images, group_tokens, TP_WIDTH)], cquery, cpair, usable
        )
        cross_mix = cross_mix.reshape(-1, TP_WIDTH)
        cross_part = rounded(mm(cross_mix, cout_full)).reshape(group_images, group_tokens, d_model)
        after_cross = after_self + scatter_tokens(cross_part)

        normed3 = rounded(layer_norm(after_cross, gains[2]))
        normed3 = gather_tokens(shuffle(normed3)).reshape(-1, d_model)
        hidden = mm(normed3, up_full)
        active = rounded(exact_gelu(hidden))
        grad_down_part = rounded(outer(active, out_grad_all))
        layer_part = rounded(mm(active, down_full)).reshape(group_images, group_tokens, d_model)
        layer_out = rounded(after_cross + scatter_tokens(layer_part))

        grad_active = rounded(mm_t(out_grad_all, down_full))
        gelu_value, gelu_pull = jax.vjp(exact_gelu, hidden)
        grad_hidden = rounded(gelu_pull(grad_active.astype(F32))[0])
        grad_normed3 = rounded(mm_t(grad_hidden, up_full))
        grad_up_part = rounded(outer(normed3, grad_hidden))
        grad_normed3 = unshuffle(
            scatter_tokens(grad_normed3.reshape(group_images, group_tokens, d_model))
        )
        grad_stream, grad_norm3 = norm_back(after_cross, gains[2], grad_normed3)
        grad_after_cross = out_grad.astype(F32) + grad_stream

        branch2 = gather_tokens(rounded(grad_after_cross)).reshape(-1, d_model)
        grad_cross_mix = rounded(mm_t(branch2, cout_full))
        grad_cout_part = rounded(outer(cross_mix, branch2))
        gcquery, gcpair = per_image(
            cross_back_kernel,
            [cquery.shape, cpair.shape],
            cquery,
            cpair,
            usable,
            grad_cross_mix.reshape(group_images, group_tokens, TP_WIDTH),
        )
        gcquery = gcquery.reshape(-1, TP_WIDTH)
        gcpair = gcpair.reshape(-1, 2 * TP_WIDTH)
        grad_normed2 = rounded(mm_t(gcquery, cquery_full))
        grad_normed2 = unshuffle(
            scatter_tokens(grad_normed2.reshape(group_images, group_tokens, d_model))
        )
        grad_cross_part = rounded(
            jnp.concatenate([outer(normed2, gcquery), outer(caption_feat, gcpair)], axis=1)
        )
        grad_stream, grad_norm2 = norm_back(after_self, gains[1], grad_normed2)
        grad_after_self = grad_after_cross + grad_stream

        grad_feat_part = rounded(mm_t(gcpair, cpair_full))
        grad_feat = None
        for ky in range(2):
            for kx in range(2):
                piece = lax.dynamic_slice_in_dim(
                    grad_feat_part, (quarter ^ (2 * ky + kx)) * TP_WIDTH, TP_WIDTH, 1
                )
                if ky or kx:
                    grad_feat = grad_feat + swap_slots(piece, ky, kx).astype(F32)
                else:
                    grad_feat = piece.astype(F32)
        grad_feat = inner_shuffle(rounded(grad_feat), True)
        grad_text_part = rounded(outer(caption_all, grad_feat))
        caption_part = rounded(mm_t(grad_feat, text_full)).reshape(group_images, slots, -1)
        caption_grad = unshuffle(scatter_tokens(caption_part))

        branch1 = gather_tokens(rounded(grad_after_self)).reshape(-1, d_model)
        grad_self_mix = rounded(mm_t(branch1, out_full))
        (gqkv,) = per_image(
            self_back_kernel,
            [qkv.shape],
            qkv,
            grad_self_mix.reshape(group_images, group_tokens, TP_WIDTH),
        )
        gqkv = gqkv.reshape(-1, 3 * TP_WIDTH)
        grad_qkv_part = rounded(outer(normed1, gqkv))
        grad_out_part = rounded(outer(self_mix, branch1))
        grad_normed1 = rounded(mm_t(gqkv, qkv_full))
        grad_normed1 = unshuffle(
            scatter_tokens(grad_normed1.reshape(group_images, group_tokens, d_model))
        )
        grad_stream, grad_norm1 = norm_back(stream, gains[0], grad_normed1)
        image_grad = grad_after_self + grad_stream


        def rows_back(parts):
            summed = reduce_weight(parts)
            rows = summed.shape[0] // 2
            own = jnp.where(y == 0, summed[:rows], summed[rows:])
            other = jnp.where(y == 0, summed[rows:], summed[:rows])
            near = [own, swap(own, 0, 1)]
            far = [swap(other, 1, 0), swap(other, 1, 1)]
            near = [jnp.where(x == 0, near[0], near[1]), jnp.where(x == 0, near[1], near[0])]
            far = [jnp.where(x == 0, far[0], far[1]), jnp.where(x == 0, far[1], far[0])]
            return [
                [jnp.where(y == 0, near[i], far[i]) for i in range(2)],
                [jnp.where(y == 0, far[i], near[i]) for i in range(2)],
            ]

        def heads_back(pieces, at):
            return jnp.concatenate(
                [
                    pieces[yy][xx][:, at + a * HEAD_DIM : at + (a + 1) * HEAD_DIM]
                    for a in range(planes)
                    for yy in range(2)
                    for xx in range(2)
                ],
                axis=1,
            ).astype(F32)

        def head_rows_back(parts):
            columns = parts.shape[1]
            rows = TP_WIDTH // (planes * spread)
            parts = parts.reshape(planes, half_spread, 2, rows, columns)
            own = reduce_weight(jnp.swapaxes(parts, 1, 2).reshape(TP_WIDTH, columns))
            other = pass_top(own)
            whole = jnp.concatenate(
                [jnp.where(top == 0, own, other), jnp.where(top == 0, other, own)], axis=0
            )
            return jnp.where(top == x, whole, swap(whole, 0, 1)).astype(F32)

        half_down = reduce_weight(grad_down_part)
        other_down = swap(half_down, 0, 1)
        grad_down = jnp.concatenate(
            [
                jnp.where(x == 0, half_down, other_down),
                jnp.where(x == 0, other_down, half_down),
            ],
            axis=0,
        ).astype(F32)

        up_pieces = rows_back(grad_up_part)
        step = ff_rows // 2
        grad_up = jnp.concatenate(
            [
                up_pieces[yy][xx][:, (a * spread + b) * step : (a * spread + b + 1) * step]
                for a in range(planes)
                for yy in range(2)
                for b in range(spread)
                for xx in range(2)
            ],
            axis=1,
        ).astype(F32)
        grad_cross_out = head_rows_back(grad_cout_part)
        cross_pieces = rows_back(grad_cross_part)
        text_pieces = rows_back(grad_text_part)
        grad_text = jnp.concatenate(
            [text_pieces[yy][xx] for yy in range(2) for xx in range(2)], axis=1
        ).astype(F32)
        grad_out = head_rows_back(grad_out_part)
        qkv_pieces = rows_back(grad_qkv_part)

        norm_sums = lax.psum(
            jnp.stack([grad_norm1, grad_norm2, grad_norm3]), ("dp", "seq")
        )
        norm_rows = norm1_gain.shape[0]
        norm_sums = lax.dynamic_slice_in_dim(norm_sums, d * norm_rows, norm_rows, 1)
        return (
            layer_out,
            image_grad,
            caption_grad,
            norm_sums[0],
            heads_back(qkv_pieces, 0),
            heads_back(qkv_pieces, TP_WIDTH),
            heads_back(qkv_pieces, 2 * TP_WIDTH),
            grad_out,
            norm_sums[1],
            grad_text,
            heads_back(cross_pieces, 0),
            heads_back(cross_pieces, TP_WIDTH),
            heads_back(cross_pieces, 2 * TP_WIDTH),
            grad_cross_out,
            norm_sums[2],
            grad_up,
            grad_down,
        )

    return on_device


def solution(mesh):
    tokens = P("dp", "seq", None)
    rows = P("dp", None)
    vector = P("dp")
    in_specs = (
        (tokens, tokens, vector)
        + (vector, rows, rows, rows, rows)
        + (vector, rows, rows, rows, rows, rows)
        + (vector, rows, rows)
        + (tokens,)
    )
    out_specs = (
        (tokens, tokens, tokens)
        + (vector, rows, rows, rows, rows)
        + (vector, rows, rows, rows, rows, rows)
        + (vector, rows, rows)
    )
    return jax.shard_map(
        make(mesh.shape["dp"]), mesh=mesh, in_specs=in_specs, out_specs=out_specs, check_vma=False
    )
```

time: 4760 us -> 1380 us (0.29)
  waiting for transfers between devices: 4010 us -> 614 us
  matrix products: 489 us -> 210 us
  local copies, waits for them, and re-layouts: 44.2 us -> 207 us
  starting transfers between devices: 2.62 us -> 78.5 us
  other arithmetic: 62.8 us -> 120 us
    reduce_scatter x15 -> x7, waiting for transfers between devices: 2900 us -> 58.6 us  [reduce_weight(): lax.psum_scatter(parts, 'dp', scatter_dimension=0, tiled=True, axis_index...]
    all_gather x15 -> x7, waiting for transfers between devices: 1010 us -> 0.01 us  [gather_weight(): lax.all_gather(payload, 'dp', axis=0, tiled=True, axis_index_groups=groups)]
    ppermute x0 -> x72, waiting for transfers between devices: none -> 555 us  [the longest x25 307 us: swap(): return lax.ppermute(values, 'dp', [(d, d ^ spread) for d in range(devices)])]
    dot_general x43 -> x24, matrix products: 480 us -> 210 us  [the longest x8 79.3 us: mm(): lax.dot_general(left, right, (((1,), (0,)), ((), ())), preferred_element_...]
    psum x1 -> x0, waiting for transfers between devices: 90.4 us -> none  [on_device(): lax.psum(cross_parts[1].astype(jnp.bfloat16), 'seq').astype(jnp.float32)]
    ppermute x0 -> x72, starting transfers between devices: none -> 77.9 us  [the longest x25 31.1 us: swap(): return lax.ppermute(values, 'dp', [(d, d ^ spread) for d in range(devices)])]
    unnamed x127 -> x254, local copies, waits for them, and re-layouts: 18 us -> 87 us
    unnamed x1 -> x0, blocking collectives: 59.8 us -> none
  transfers between devices with their start and end apart: 31 -> 86, of which waited for: 27 -> 46; matrix products, arithmetic and copies ran while one was open for 10% -> 30% of each run, Pallas kernels for 0% -> 1%
where the time goes in v1:
time: 1380 us; the launch traced here: 1370 us
  waiting for transfers between devices  614 us (44%)
  matrix products  210 us (15%)
  local copies, waits for them, and re-layouts  207 us (15%)
  other arithmetic  120 us (9%)
  blocking collectives  96.2 us (7%)
  starting transfers between devices  78.5 us (6%)
  Pallas kernels  24.7 us (2%)
  between operations  16.6 us (1%)
    ppermute x25, waiting for transfers between devices, swap(): return lax.ppermute(values, 'dp', [(d, d ^ spread) for d in range(devices)])  307 us
    ppermute x20, waiting for transfers between devices, swap(): return lax.ppermute(values, ('dp', 'seq'), pairs)  174 us
    unnamed x254, local copies, waits for them, and re-layouts  87 us
    dot_general x8, matrix products, mm(): lax.dot_general(left, right, (((1,), (0,)), ((), ())), preferred_element_...  79.3 us
    ppermute x23, waiting for transfers between devices, swap(): return lax.ppermute(values, 'seq', [(0, 1), (1, 0)])  70.9 us
    dot_general x8, matrix products, outer(): lax.dot_general(left, right, (((0,), (0,)), ((), ())), preferred_element_...  67 us
    dot_general x8, matrix products, mm_t(): lax.dot_general(left, right, (((1,), (1,)), ((), ())), preferred_element_...  63.2 us
    reduce_scatter x7, waiting for transfers between devices, reduce_weight(): lax.psum_scatter(parts, 'dp', scatter_dimension=0, tiled=True, axis_index...  58.6 us
  transfers between devices with their start and end apart: 86, of which 46 were waited for; matrix products, arithmetic and copies ran while one was open for 30% of the time, Pallas kernels for 1%

profile of v1, /device:TPU:0, one launch (start us, length us, event | category | flops | bytes accessed | tf_op | source)
XLA Modules:
  0.0 1366.2 jit_solution(7701487912079226757)
XLA Ops:
  38.5 9.4 collective-permute-done.3
  55.4 7.3 collective-permute-done.15
  75.6 9.8 collective-permute-done.11
  99.5 12.2 collective-permute-done.27
  130.8 48.3 %all_gather.24 = bf16[3,2048]{1,0:T(4,128)(2,1)S(1)} all-gather(bf16[3,128]{1,0:T(4,128)(2,1)S(1)} %pad_maximum_fusion.14), channel_id=1, replica_groups=mesh['dp'=16,'seq'=2] {'dp'}, dimensions={1}, use_global_device_ids=true | all-gather | bytes 13056 | tf_op jit(solution)/shard_map/all_gather | solution.py:275
  192.0 8.7 copy.181
  218.3 10.1 convolution_convert_fusion.5
  254.9 6.0 convolution_convert_fusion.17
  264.1 5.2 collective-permute-done.7
  269.6 21.3 %collective-permute-done.6 = bf16[2,128,2048]{1,2,0:T(8,128)(2,1)} collective-permute-done((bf16[2,128,2048]{1,2,0:T(8,128)(2,1)}, bf16[2,128,2048]{1,2,0:T(8,128)(2,1)}, u32[]{:S(2)}, u32[]{:S(2)}) %collective-permute-start.6) | collective-permute-done | bytes 1048608 | tf_op jit(solution)/shard_map/ppermute | solution.py:159
  306.3 8.0 collective-permute-done.18
  319.0 5.2 fusion.65
  324.1 12.6 collective-permute-done.10
  336.8 21.4 %collective-permute-done.9 = bf16[2,128,2048]{1,2,0:T(8,128)(2,1)} collective-permute-done((bf16[2,128,2048]{1,2,0:T(8,128)(2,1)S(1)}, bf16[2,128,2048]{1,2,0:T(8,128)(2,1)}, u32[]{:S(2)}, u32[]{:S(2)}) %collective-permute-start.9) | collective-permute-done | bytes 1048608 | tf_op jit(solution)/shard_map/ppermute | solution.py:159
  363.8 6.2 copy.191
  369.9 5.2 fusion.62
  398.1 16.6 %collective-permute-done.23 = bf16[2,128,2048]{1,2,0:T(8,128)(2,1)} collective-permute-done((bf16[2,128,2048]{1,2,0:T(8,128)(2,1)}, bf16[2,128,2048]{1,2,0:T(8,128)(2,1)}, u32[]{:S(2)}, u32[]{:S(2)}) %collective-permute-start.23) | collective-permute-done | bytes 1048608 | tf_op jit(solution)/shard_map/ppermute | solution.py:161
  415.1 22.1 %collective-permute-done.22 = bf16[2,128,2048]{1,2,0:T(8,128)(2,1)} collective-permute-done((bf16[2,128,2048]{1,2,0:T(8,128)(2,1)}, bf16[2,128,2048]{1,2,0:T(8,128)(2,1)}, u32[]{:S(2)}, u32[]{:S(2)}) %collective-permute-start.22) | collective-permute-done | bytes 1048608 | tf_op jit(solution)/shard_map/ppermute | solution.py:159
  444.1 15.5 %collective-permute-done.33 = bf16[2,128,2048]{2,1,0:T(8,128)(2,1)} collective-permute-done((bf16[2,128,2048]{2,1,0:T(8,128)(2,1)S(1)}, bf16[2,128,2048]{2,1,0:T(8,128)(2,1)}, u32[]{:S(2)}, u32[]{:S(2)}) %collective-permute-start.33) | collective-permute-done | bytes 1048608 | tf_op jit(solution)/shard_map/ppermute | solution.py:161
  460.1 22.1 %collective-permute-done.32 = bf16[2,128,2048]{2,1,0:T(8,128)(2,1)} collective-permute-done((bf16[2,128,2048]{2,1,0:T(8,128)(2,1)S(1)}, bf16[2,128,2048]{2,1,0:T(8,128)(2,1)}, u32[]{:S(2)}, u32[]{:S(2)}) %collective-permute-start.32) | collective-permute-done | bytes 1048608 | tf_op jit(solution)/shard_map/ppermute | solution.py:159
  486.5 18.1 %collective-permute-done.26 = bf16[2,128,2048]{1,2,0:T(8,128)(2,1)S(1)} collective-permute-done((bf16[2,128,2048]{1,2,0:T(8,128)(2,1)S(1)}, bf16[2,128,2048]{1,2,0:T(8,128)(2,1)S(1)}, u32[]{:S(2)}, u32[]{:S(2)}) %collective-permute-start.26) | collective-permute-done | bytes 1048608 | tf_op jit(solution)/shard_map/ppermute | solution.py:161
  504.5 21.4 %collective-permute-done.25 = bf16[2,128,2048]{1,2,0:T(8,128)(2,1)S(1)} collective-permute-done((bf16[2,128,2048]{1,2,0:T(8,128)(2,1)S(1)}, bf16[2,128,2048]{1,2,0:T(8,128)(2,1)S(1)}, u32[]{:S(2)}, u32[]{:S(2)}) %collective-permute-start.25) | collective-permute-done | bytes 1048608 | tf_op jit(solution)/shard_map/ppermute | solution.py:159
  529.0 6.3 copy.207
  535.3 31.3 %multiply_convert_fusion.1 = (bf16[1024,2048]{1,0:T(8,128)(2,1)}, f32[1024,2048]{1,0:T(8,128)}, f32[1024,2048]{1,0:T(8,128)}) fusion(bf16[1024,2048]{1,0:T(8,128)(2,1)} %bitcast.370, bf16[2048,2048]{1,0:T(8,128)(2,1)} %all-gather.18.cloned.1.call-done), kind=kOutput, calls=%fused_computation.17 | convolution fusion | flops 8726249472 | bytes 33554432 | tf_op jit(solution)/shard_map/dot_general | solution.py:25
  566.7 18.2 %fusion.5 = bf16[1024,2048]{1,0:T(8,128)(2,1)S(1)} fusion(f32[1024,2048]{1,0:T(8,128)} %get-tuple-element.64, f32[1024,2048]{1,0:T(8,128)} %get-tuple-element.274, bf16[1024,2048]{1,0:T(8,128)(2,1)} %bitcast.368, bf16[2048,2048]{1,0:T(8,128)(2,1)} %all-gather.20.cloned.1.call-done), kind=kOutput, calls=%fused_computation.9 | convolution fusion | flops 8623489024 | bytes 33554432 | tf_op jit(solution)/shard_map/dot_general | solution.py:29
  584.9 12.8 convolution_convert_fusion.8
  604.8 23.1 %collective-permute-done.36 = bf16[2,128,2048]{2,1,0:T(8,128)(2,1)} collective-permute-done((bf16[2,128,2048]{2,1,0:T(8,128)(2,1)}, bf16[2,128,2048]{2,1,0:T(8,128)(2,1)}, u32[]{:S(2)}, u32[]{:S(2)}) %collective-permute-start.36) | collective-permute-done | bytes 1048608 | tf_op jit(solution)/shard_map/ppermute | solution.py:161
  627.9 20.4 %collective-permute-done.35 = bf16[2,128,2048]{2,1,0:T(8,128)(2,1)} collective-permute-done((bf16[2,128,2048]{2,1,0:T(8,128)(2,1)}, bf16[2,128,2048]{2,1,0:T(8,128)(2,1)}, u32[]{:S(2)}, u32[]{:S(2)}) %collective-permute-start.35) | collective-permute-done | bytes 1048608 | tf_op jit(solution)/shard_map/ppermute | solution.py:159
  671.5 12.8 convolution_convert_fusion.9
  684.3 10.7 collective-permute-done.39
  695.0 20.2 %collective-permute-done.38 = bf16[2,128,2048]{1,2,0:T(8,128)(2,1)S(1)} collective-permute-done((bf16[2,128,2048]{1,2,0:T(8,128)(2,1)S(1)}, bf16[2,128,2048]{1,2,0:T(8,128)(2,1)S(1)}, u32[]{:S(2)}, u32[]{:S(2)}) %collective-permute-start.38) | collective-permute-done | bytes 1048608 | tf_op jit(solution)/shard_map/ppermute | solution.py:159
  718.0 6.3 copy.217
  724.3 5.3 convolution_convert_fusion.16
  729.6 7.5 shard_map.307
  760.6 5.9 convolution_convert_fusion.12
  766.6 5.4 collective-permute-done.42
  773.1 21.4 %collective-permute-done.41 = bf16[2,128,2048]{2,1,0:T(8,128)(2,1)} collective-permute-done((bf16[2,128,2048]{2,1,0:T(8,128)(2,1)}, bf16[2,128,2048]{2,1,0:T(8,128)(2,1)}, u32[]{:S(2)}, u32[]{:S(2)}) %collective-permute-start.41) | collective-permute-done | bytes 1048608 | tf_op jit(solution)/shard_map/ppermute | solution.py:159
  812.1 4.9 collective-permute-done.30
  817.0 21.0 %collective-permute-done.29 = bf16[2,128,2048]{1,2,0:T(8,128)(2,1)} collective-permute-done((bf16[2,128,2048]{1,2,0:T(8,128)(2,1)}, bf16[2,128,2048]{1,2,0:T(8,128)(2,1)}, u32[]{:S(2)}, u32[]{:S(2)}) %collective-permute-start.29) | collective-permute-done | bytes 1048608 | tf_op jit(solution)/shard_map/ppermute | solution.py:159
  838.0 4.9 fusion.71
  846.4 23.5 %collective-permute-done.45 = bf16[2,128,2048]{1,2,0:T(8,128)(2,1)S(1)} collective-permute-done((bf16[2,128,2048]{1,2,0:T(8,128)(2,1)S(1)}, bf16[2,128,2048]{1,2,0:T(8,128)(2,1)S(1)}, u32[]{:S(2)}, u32[]{:S(2)}) %collective-permute-start.45) | collective-permute-done | bytes 1048608 | tf_op jit(solution)/shard_map/ppermute | solution.py:161
  869.9 21.5 %collective-permute-done.44 = bf16[2,128,2048]{1,2,0:T(8,128)(2,1)S(1)} collective-permute-done((bf16[2,128,2048]{1,2,0:T(8,128)(2,1)S(1)}, bf16[2,128,2048]{1,2,0:T(8,128)(2,1)S(1)}, u32[]{:S(2)}, u32[]{:S(2)}) %collective-permute-start.44) | collective-permute-done | bytes 1048608 | tf_op jit(solution)/shard_map/ppermute | solution.py:159
  894.1 6.3 copy.222
  900.5 5.9 convolution_convert_fusion.14
  916.8 12.2 collective-permute-done.51
  931.0 8.5 collective-permute-done.50
  947.1 6.9 convolution_convert_fusion.2
  970.2 9.0 shard_map.308
  979.3 13.4 bitcast_convert_fusion
  992.7 14.1 %convolution_convert_fusion.1 = bf16[2048,2048]{1,0:T(8,128)(2,1)} fusion(bf16[1024,2048]{1,0:T(8,128)(2,1)} %bitcast.371, bf16[1024,2048]{1,0:T(8,128)(2,1)} %copy-done.65), kind=kOutput, calls=%fused_computation.33 | convolution fusion | flops 8594128896 | bytes 16777216 | tf_op jit(solution)/shard_map/dot_general | solution.py:33
  1007.0 14.3 %convolution_convert_fusion = bf16[2048,2048]{1,0:T(8,128)(2,1)} fusion(bf16[1024,2048]{1,0:T(8,128)(2,1)} %get-tuple-element.63, bf16[1024,2048]{1,0:T(8,128)(2,1)} %bitcast.369), kind=kOutput, calls=%fused_computation.32 | convolution fusion | flops 8594128896 | bytes 16777216 | tf_op jit(solution)/shard_map/dot_general | solution.py:33
  1035.4 8.8 convolution_convert_fusion.4
  1049.7 7.2 collective-permute-done.54
  1058.0 21.5 %collective-permute-done.53 = bf16[2,64,4096]{2,1,0:T(8,128)(2,1)} collective-permute-done((bf16[2,64,4096]{2,1,0:T(8,128)(2,1)}, bf16[2,64,4096]{2,1,0:T(8,128)(2,1)}, u32[]{:S(2)}, u32[]{:S(2)}) %collective-permute-start.53) | collective-permute-done | bytes 1048608 | tf_op jit(solution)/shard_map/ppermute | solution.py:159
  1090.7 11.1 collective-permute-done.48
  1101.8 21.5 %collective-permute-done.47 = bf16[2,128,2048]{2,1,0:T(8,128)(2,1)} collective-permute-done((bf16[2,128,2048]{2,1,0:T(8,128)(2,1)}, bf16[2,128,2048]{2,1,0:T(8,128)(2,1)}, u32[]{:S(2)}, u32[]{:S(2)}) %collective-permute-start.47) | collective-permute-done | bytes 1048608 | tf_op jit(solution)/shard_map/ppermute | solution.py:159
  1135.6 47.9 %psum.7 = f32[3,2048]{1,0:T(4,128)S(1)} all-reduce(f32[3,2048]{1,0:T(4,128)S(1)} %pad_maximum_fusion.13), channel_id=1, replica_groups=mesh['dp'=16,'seq'=2] {'dp','seq'}, use_global_device_ids=true, to_apply=%region_17.18 | all-reduce | flops 6144 | bytes 49152 | tf_op jit(solution)/shard_map/psum | solution.py:486
  1192.0 8.9 collective-permute-done.67
  1202.0 9.8 collective-permute-done.59
  1223.0 8.1 collective-permute-done.60
  1234.8 12.0 collective-permute-done.63
  1259.0 14.7 %collective-permute-done.55 = bf16[128,1536]{1,0:T(8,128)(2,1)S(1)} collective-permute-done((bf16[128,1536]{1,0:T(8,128)(2,1)S(1)}, bf16[128,1536]{1,0:T(8,128)(2,1)S(1)}, u32[]{:S(2)}, u32[]{:S(2)}) %collective-permute-start.55) | collective-permute-done | bytes 393248 | tf_op jit(solution)/shard_map/ppermute | solution.py:157
  1274.9 58.6 %reduce-scatter.20.cloned.1.call-done = bf16[256,2048]{1,0:T(8,128)(2,1)} async-done(((bf16[2048,2048]{1,0:T(8,128)(2,1)}), bf16[256,2048]{1,0:T(8,128)(2,1)}) %reduce-scatter.20.cloned.1.call-update) | async-done | bytes 1048592 | tf_op jit(solution)/shard_map/reduce_scatter | solution.py:191
  1343.5 12.9 collective-permute-done.71
  (578 shorter events, 419.6 us)
Async XLA Ops:
  7.2 211.1 %all-gather.8.cloned.1.call-start = ((), (), s32[]{:S(2)}) async-start(), calls=%async_computation.7 | async-start | bytes 7077888 | tf_op jit(solution)/shard_map/all_gather | solution.py:188
  49.9 184.6 %all-gather.10.cloned.1.call-start = ((), (), s32[]{:S(2)}) async-start(), calls=%async_computation.8 | async-start | bytes 2359296 | tf_op jit(solution)/shard_map/all_gather | solution.py:188
  52.6 202.3 %all-gather.14.cloned.1.call-start = ((), (), s32[]{:S(2)}) async-start(), calls=%async_computation.10 | async-start | bytes 4718592 | tf_op jit(solution)/shard_map/all_gather | solution.py:188
  64.6 254.3 %all-gather.12.cloned.1.call-start = ((), (), s32[]{:S(2)}) async-start(), calls=%async_computation.9 | async-start | bytes 7077888 | tf_op jit(solution)/shard_map/all_gather | solution.py:188
  86.4 293.4 %all-gather.16.cloned.1.call-start = ((), (), s32[]{:S(2)}) async-start(), calls=%async_computation.11 | async-start | bytes 2359296 | tf_op jit(solution)/shard_map/all_gather | solution.py:188
  88.9 446.4 %all-gather.18.cloned.1.call-start = ((), (), s32[]{:S(2)}) async-start(), calls=%async_computation.12 | async-start | bytes 9437184 | tf_op jit(solution)/shard_map/all_gather | solution.py:188
  113.0 453.7 %all-gather.20.cloned.1.call-start = ((), (), s32[]{:S(2)}) async-start(), calls=%async_computation.13 | async-start | bytes 9437184 | tf_op jit(solution)/shard_map/all_gather | solution.py:188
  115.8 66.7 %collective-permute-start.2 = (bf16[2,128,2048]{1,2,0:T(8,128)(2,1)}, bf16[2,128,2048]{1,2,0:T(8,128)(2,1)}, u32[]{:S(2)}, u32[]{:S(2)}) collective-permute-start(bf16[2,128,2048]{1,2,0:T(8,128)(2,1)} %bitcast.4), channel_id=1, source_target_pairs={{0,5},{1,4},{2,7},{3,6},{4,1},{5,0},{6,3},{7,2},{8,13},{9,12},{10,... | collective-permute-start | bytes 3145736 | tf_op jit(solution)/shard_map/ppermute | solution.py:161
  115.8 67.5 %collective-permute-start.1 = (bf16[2,128,2048]{1,2,0:T(8,128)(2,1)}, bf16[2,128,2048]{1,2,0:T(8,128)(2,1)}, u32[]{:S(2)}, u32[]{:S(2)}) collective-permute-start(bf16[2,128,2048]{1,2,0:T(8,128)(2,1)} %bitcast.4), channel_id=1, source_target_pairs={{0,4},{2,6},{4,0},{6,2},{8,12},{10,14},{12,8},{14,10},{16,20},{18,... | collective-permute-start | bytes 3145736 | tf_op jit(solution)/shard_map/ppermute | solution.py:159
  117.5 67.6 %collective-permute-start = (bf16[2,128,2048]{1,2,0:T(8,128)(2,1)}, bf16[2,128,2048]{1,2,0:T(8,128)(2,1)}, u32[]{:S(2)}, u32[]{:S(2)}) collective-permute-start(bf16[2,128,2048]{1,2,0:T(8,128)(2,1)} %bitcast.4), channel_id=1, source_target_pairs={{0,1},{1,0},{2,3},{3,2},{4,5},{5,4},{6,7},{7,6},{8,9},{9,8},{10,11... | collective-permute-start | bytes 3145736 | tf_op jit(solution)/shard_map/ppermute | solution.py:157
  127.8 77.9 %collective-permute-start.14 = (bf16[2,64,4096]{2,1,0:T(8,128)(2,1)}, bf16[2,64,4096]{2,1,0:T(8,128)(2,1)}, u32[]{:S(2)}, u32[]{:S(2)}) collective-permute-start(bf16[2,64,4096]{2,1,0:T(8,128)(2,1)} %reshape.343), channel_id=1, source_target_pairs={{0,5},{1,4},{2,7},{3,6},{4,1},{5,0},{6,3},{7,2},{8,13},{9,12},{10,... | collective-permute-start | bytes 3145736 | tf_op jit(solution)/shard_map/ppermute | solution.py:161
  129.1 53.2 %collective-permute-start.19 = (s32[2]{0:T(128)S(1)}, s32[2]{0:T(128)S(1)}, u32[]{:S(2)}, u32[]{:S(2)}) collective-permute-start(s32[2]{0:T(128)S(1)} %copy-done.64), channel_id=1, source_target_pairs={{0,4},{2,6},{4,0},{6,2},{8,12},{10,14},{12,8},{14,10},{16,20},{18,... | collective-permute-start | bytes 32 | tf_op jit(solution)/shard_map/ppermute | solution.py:159
  130.8 1004.8 %reduce-scatter.16.cloned.1.call-start = ((), (), s32[]{:S(2)}) async-start(), calls=%async_computation.18 | async-start | bytes 2359296 | tf_op jit(solution)/shard_map/reduce_scatter | solution.py:191
  182.5 29.8 %collective-permute-start.12 = (bf16[2,64,4096]{2,1,0:T(8,128)(2,1)}, bf16[2,64,4096]{2,1,0:T(8,128)(2,1)}, u32[]{:S(2)}, u32[]{:S(2)}) collective-permute-start(bf16[2,64,4096]{2,1,0:T(8,128)(2,1)} %reshape.343), channel_id=1, source_target_pairs={{0,1},{1,0},{2,3},{3,2},{4,5},{5,4},{6,7},{7,6},{8,9},{9,8},{10,11... | collective-permute-start | bytes 3145736 | tf_op jit(solution)/shard_map/ppermute | solution.py:157
  242.0 27.3 %collective-permute-start.7 = (bf16[2,128,2048]{1,2,0:T(8,128)(2,1)}, bf16[2,128,2048]{1,2,0:T(8,128)(2,1)}, u32[]{:S(2)}, u32[]{:S(2)}) collective-permute-start(bf16[2,128,2048]{1,2,0:T(8,128)(2,1)} %bitcast.25), channel_id=1, source_target_pairs={{0,5},{1,4},{2,7},{3,6},{4,1},{5,0},{6,3},{7,2},{8,13},{9,12},{10,... | collective-permute-start | bytes 3145736 | tf_op jit(solution)/shard_map/ppermute | solution.py:161
  244.7 46.2 %collective-permute-start.6 = (bf16[2,128,2048]{1,2,0:T(8,128)(2,1)}, bf16[2,128,2048]{1,2,0:T(8,128)(2,1)}, u32[]{:S(2)}, u32[]{:S(2)}) collective-permute-start(bf16[2,128,2048]{1,2,0:T(8,128)(2,1)} %bitcast.408), channel_id=1, source_target_pairs={{0,4},{2,6},{4,0},{6,2},{8,12},{10,14},{12,8},{14,10},{16,20},{18,... | collective-permute-start | bytes 3145736 | tf_op jit(solution)/shard_map/ppermute | solution.py:159
  249.2 42.9 %collective-permute-start.5 = (bf16[2,128,2048]{1,2,0:T(8,128)(2,1)}, bf16[2,128,2048]{1,2,0:T(8,128)(2,1)}, u32[]{:S(2)}, u32[]{:S(2)}) collective-permute-start(bf16[2,128,2048]{1,2,0:T(8,128)(2,1)} %bitcast.409), channel_id=1, source_target_pairs={{0,1},{1,0},{2,3},{3,2},{4,5},{5,4},{6,7},{7,6},{8,9},{9,8},{10,11... | collective-permute-start | bytes 3145736 | tf_op jit(solution)/shard_map/ppermute | solution.py:157
  261.7 41.6 %collective-permute-start.16 = (bf16[512,512]{0,1:T(8,128)(2,1)}, bf16[512,512]{0,1:T(8,128)(2,1)}, u32[]{:S(2)}, u32[]{:S(2)}) collective-permute-start(bf16[512,512]{0,1:T(8,128)(2,1)} %bitcast.48), channel_id=1, source_target_pairs={{0,1},{1,0},{2,3},{3,2},{4,5},{5,4},{6,7},{7,6},{8,9},{9,8},{10,11... | collective-permute-start | bytes 1572872 | tf_op jit(solution)/shard_map/ppermute | solution.py:157
  262.3 42.5 %collective-permute-start.17 = (bf16[512,512]{0,1:T(8,128)(2,1)}, bf16[512,512]{0,1:T(8,128)(2,1)}, u32[]{:S(2)}, u32[]{:S(2)}) collective-permute-start(bf16[512,512]{0,1:T(8,128)(2,1)} %bitcast.48), channel_id=1, source_target_pairs={{0,4},{2,6},{4,0},{6,2},{8,12},{10,14},{12,8},{14,10},{16,20},{18,... | collective-permute-start | bytes 1572872 | tf_op jit(solution)/shard_map/ppermute | solution.py:159
  269.3 45.0 %collective-permute-start.18 = (bf16[512,512]{0,1:T(8,128)(2,1)}, bf16[512,512]{0,1:T(8,128)(2,1)}, u32[]{:S(2)}, u32[]{:S(2)}) collective-permute-start(bf16[512,512]{0,1:T(8,128)(2,1)} %bitcast.48), channel_id=1, source_target_pairs={{0,5},{1,4},{2,7},{3,6},{4,1},{5,0},{6,3},{7,2},{8,13},{9,12},{10,... | collective-permute-start | bytes 1572872 | tf_op jit(solution)/shard_map/ppermute | solution.py:161
  297.2 39.6 %collective-permute-start.10 = (bf16[2,128,2048]{1,2,0:T(8,128)(2,1)S(1)}, bf16[2,128,2048]{1,2,0:T(8,128)(2,1)}, u32[]{:S(2)}, u32[]{:S(2)}) collective-permute-start(bf16[2,128,2048]{1,2,0:T(8,128)(2,1)S(1)} %bitcast.389), channel_id=1, source_target_pairs={{0,5},{1,4},{2,7},{3,6},{4,1},{5,0},{6,3},{7,2},{8,13},{9,12},{10,... | collective-permute-start | bytes 3145736 | tf_op jit(solution)/shard_map/ppermute | solution.py:161
  297.6 60.6 %collective-permute-start.9 = (bf16[2,128,2048]{1,2,0:T(8,128)(2,1)S(1)}, bf16[2,128,2048]{1,2,0:T(8,128)(2,1)}, u32[]{:S(2)}, u32[]{:S(2)}) collective-permute-start(bf16[2,128,2048]{1,2,0:T(8,128)(2,1)S(1)} %bitcast.390), channel_id=1, source_target_pairs={{0,4},{2,6},{4,0},{6,2},{8,12},{10,14},{12,8},{14,10},{16,20},{18,... | collective-permute-start | bytes 3145736 | tf_op jit(solution)/shard_map/ppermute | solution.py:159
  317.5 42.4 %collective-permute-start.8 = (bf16[2,128,2048]{1,2,0:T(8,128)(2,1)S(1)}, bf16[2,128,2048]{1,2,0:T(8,128)(2,1)}, u32[]{:S(2)}, u32[]{:S(2)}) collective-permute-start(bf16[2,128,2048]{1,2,0:T(8,128)(2,1)S(1)} %bitcast.391), channel_id=1, source_target_pairs={{0,1},{1,0},{2,3},{3,2},{4,5},{5,4},{6,7},{7,6},{8,9},{9,8},{10,11... | collective-permute-start | bytes 3145736 | tf_op jit(solution)/shard_map/ppermute | solution.py:157
  387.4 27.3 %collective-permute-start.23 = (bf16[2,128,2048]{1,2,0:T(8,128)(2,1)}, bf16[2,128,2048]{1,2,0:T(8,128)(2,1)}, u32[]{:S(2)}, u32[]{:S(2)}) collective-permute-start(bf16[2,128,2048]{1,2,0:T(8,128)(2,1)} %bitcast.411), channel_id=1, source_target_pairs={{0,5},{1,4},{2,7},{3,6},{4,1},{5,0},{6,3},{7,2},{8,13},{9,12},{10,... | collective-permute-start | bytes 3145736 | tf_op jit(solution)/shard_map/ppermute | solution.py:161
  390.0 47.2 %collective-permute-start.22 = (bf16[2,128,2048]{1,2,0:T(8,128)(2,1)}, bf16[2,128,2048]{1,2,0:T(8,128)(2,1)}, u32[]{:S(2)}, u32[]{:S(2)}) collective-permute-start(bf16[2,128,2048]{1,2,0:T(8,128)(2,1)} %bitcast.410), channel_id=1, source_target_pairs={{0,4},{2,6},{4,0},{6,2},{8,12},{10,14},{12,8},{14,10},{16,20},{18,... | collective-permute-start | bytes 3145736 | tf_op jit(solution)/shard_map/ppermute | solution.py:159
  393.0 44.5 %collective-permute-start.21 = (bf16[2,128,2048]{1,2,0:T(8,128)(2,1)}, bf16[2,128,2048]{1,2,0:T(8,128)(2,1)}, u32[]{:S(2)}, u32[]{:S(2)}) collective-permute-start(bf16[2,128,2048]{1,2,0:T(8,128)(2,1)} %bitcast.412), channel_id=1, source_target_pairs={{0,1},{1,0},{2,3},{3,2},{4,5},{5,4},{6,7},{7,6},{8,9},{9,8},{10,11... | collective-permute-start | bytes 3145736 | tf_op jit(solution)/shard_map/ppermute | solution.py:157
  394.5 65.1 %collective-permute-start.33 = (bf16[2,128,2048]{2,1,0:T(8,128)(2,1)S(1)}, bf16[2,128,2048]{2,1,0:T(8,128)(2,1)}, u32[]{:S(2)}, u32[]{:S(2)}) collective-permute-start(bf16[2,128,2048]{2,1,0:T(8,128)(2,1)S(1)} %copy-done.31), channel_id=1, source_target_pairs={{0,5},{1,4},{2,7},{3,6},{4,1},{5,0},{6,3},{7,2},{8,13},{9,12},{10,... | collective-permute-start | bytes 3145736 | tf_op jit(solution)/shard_map/ppermute | solution.py:161
  395.8 86.3 %collective-permute-start.32 = (bf16[2,128,2048]{2,1,0:T(8,128)(2,1)S(1)}, bf16[2,128,2048]{2,1,0:T(8,128)(2,1)}, u32[]{:S(2)}, u32[]{:S(2)}) collective-permute-start(bf16[2,128,2048]{2,1,0:T(8,128)(2,1)S(1)} %copy-done.31), channel_id=1, source_target_pairs={{0,4},{2,6},{4,0},{6,2},{8,12},{10,14},{12,8},{14,10},{16,20},{18,... | collective-permute-start | bytes 3145736 | tf_op jit(solution)/shard_map/ppermute | solution.py:159
  414.7 69.2 %collective-permute-start.31 = (bf16[2,128,2048]{2,1,0:T(8,128)(2,1)S(1)}, bf16[2,128,2048]{2,1,0:T(8,128)(2,1)S(1)}, u32[]{:S(2)}, u32[]{:S(2)}) collective-permute-start(bf16[2,128,2048]{2,1,0:T(8,128)(2,1)S(1)} %copy-done.31), channel_id=1, source_target_pairs={{0,1},{1,0},{2,3},{3,2},{4,5},{5,4},{6,7},{7,6},{8,9},{9,8},{10,11... | collective-permute-start | bytes 3145736 | tf_op jit(solution)/shard_map/ppermute | solution.py:157
  442.4 62.1 %collective-permute-start.26 = (bf16[2,128,2048]{1,2,0:T(8,128)(2,1)S(1)}, bf16[2,128,2048]{1,2,0:T(8,128)(2,1)S(1)}, u32[]{:S(2)}, u32[]{:S(2)}) collective-permute-start(bf16[2,128,2048]{1,2,0:T(8,128)(2,1)S(1)} %bitcast.393), channel_id=1, source_target_pairs={{0,5},{1,4},{2,7},{3,6},{4,1},{5,0},{6,3},{7,2},{8,13},{9,12},{10,... | collective-permute-start | bytes 3145736 | tf_op jit(solution)/shard_map/ppermute | solution.py:161
  442.6 83.4 %collective-permute-start.25 = (bf16[2,128,2048]{1,2,0:T(8,128)(2,1)S(1)}, bf16[2,128,2048]{1,2,0:T(8,128)(2,1)S(1)}, u32[]{:S(2)}, u32[]{:S(2)}) collective-permute-start(bf16[2,128,2048]{1,2,0:T(8,128)(2,1)S(1)} %bitcast.394), channel_id=1, source_target_pairs={{0,4},{2,6},{4,0},{6,2},{8,12},{10,14},{12,8},{14,10},{16,20},{18,... | collective-permute-start | bytes 3145736 | tf_op jit(solution)/shard_map/ppermute | solution.py:159
  459.7 66.8 %collective-permute-start.24 = (bf16[2,128,2048]{1,2,0:T(8,128)(2,1)S(1)}, bf16[2,128,2048]{1,2,0:T(8,128)(2,1)S(1)}, u32[]{:S(2)}, u32[]{:S(2)}) collective-permute-start(bf16[2,128,2048]{1,2,0:T(8,128)(2,1)S(1)} %bitcast.395), channel_id=1, source_target_pairs={{0,1},{1,0},{2,3},{3,2},{4,5},{5,4},{6,7},{7,6},{8,9},{9,8},{10,11... | collective-permute-start | bytes 3145736 | tf_op jit(solution)/shard_map/ppermute | solution.py:157
  600.7 27.3 %collective-permute-start.36 = (bf16[2,128,2048]{2,1,0:T(8,128)(2,1)}, bf16[2,128,2048]{2,1,0:T(8,128)(2,1)}, u32[]{:S(2)}, u32[]{:S(2)}) collective-permute-start(bf16[2,128,2048]{2,1,0:T(8,128)(2,1)} %get-tuple-element.79), channel_id=1, source_target_pairs={{0,5},{1,4},{2,7},{3,6},{4,1},{5,0},{6,3},{7,2},{8,13},{9,12},{10,... | collective-permute-start | bytes 3145736 | tf_op jit(solution)/shard_map/ppermute | solution.py:161
  601.0 47.4 %collective-permute-start.35 = (bf16[2,128,2048]{2,1,0:T(8,128)(2,1)}, bf16[2,128,2048]{2,1,0:T(8,128)(2,1)}, u32[]{:S(2)}, u32[]{:S(2)}) collective-permute-start(bf16[2,128,2048]{2,1,0:T(8,128)(2,1)} %get-tuple-element.80), channel_id=1, source_target_pairs={{0,4},{2,6},{4,0},{6,2},{8,12},{10,14},{12,8},{14,10},{16,20},{18,... | collective-permute-start | bytes 3145736 | tf_op jit(solution)/shard_map/ppermute | solution.py:159
  602.5 47.1 %collective-permute-start.34 = (bf16[2,128,2048]{2,1,0:T(8,128)(2,1)}, bf16[2,128,2048]{2,1,0:T(8,128)(2,1)}, u32[]{:S(2)}, u32[]{:S(2)}) collective-permute-start(bf16[2,128,2048]{2,1,0:T(8,128)(2,1)} %get-tuple-element.78), channel_id=1, source_target_pairs={{0,1},{1,0},{2,3},{3,2},{4,5},{5,4},{6,7},{7,6},{8,9},{9,8},{10,11... | collective-permute-start | bytes 3145736 | tf_op jit(solution)/shard_map/ppermute | solution.py:157
  668.3 47.0 %collective-permute-start.38 = (bf16[2,128,2048]{1,2,0:T(8,128)(2,1)S(1)}, bf16[2,128,2048]{1,2,0:T(8,128)(2,1)S(1)}, u32[]{:S(2)}, u32[]{:S(2)}) collective-permute-start(bf16[2,128,2048]{1,2,0:T(8,128)(2,1)S(1)} %fusion.70), channel_id=1, source_target_pairs={{0,4},{2,6},{4,0},{6,2},{8,12},{10,14},{12,8},{14,10},{16,20},{18,... | collective-permute-start | bytes 3145736 | tf_op jit(solution)/shard_map/ppermute | solution.py:159
  669.7 45.7 %collective-permute-start.37 = (bf16[2,128,2048]{1,2,0:T(8,128)(2,1)S(1)}, bf16[2,128,2048]{1,2,0:T(8,128)(2,1)S(1)}, u32[]{:S(2)}, u32[]{:S(2)}) collective-permute-start(bf16[2,128,2048]{1,2,0:T(8,128)(2,1)S(1)} %fusion.70), channel_id=1, source_target_pairs={{0,1},{1,0},{2,3},{3,2},{4,5},{5,4},{6,7},{7,6},{8,9},{9,8},{10,11... | collective-permute-start | bytes 3145736 | tf_op jit(solution)/shard_map/ppermute | solution.py:157
  744.7 27.3 %collective-permute-start.42 = (bf16[2,128,2048]{2,1,0:T(8,128)(2,1)}, bf16[2,128,2048]{2,1,0:T(8,128)(2,1)}, u32[]{:S(2)}, u32[]{:S(2)}) collective-permute-start(bf16[2,128,2048]{2,1,0:T(8,128)(2,1)} %get-tuple-element.76), channel_id=1, source_target_pairs={{0,5},{1,4},{2,7},{3,6},{4,1},{5,0},{6,3},{7,2},{8,13},{9,12},{10,... | collective-permute-start | bytes 3145736 | tf_op jit(solution)/shard_map/ppermute | solution.py:161
  746.0 48.6 %collective-permute-start.41 = (bf16[2,128,2048]{2,1,0:T(8,128)(2,1)}, bf16[2,128,2048]{2,1,0:T(8,128)(2,1)}, u32[]{:S(2)}, u32[]{:S(2)}) collective-permute-start(bf16[2,128,2048]{2,1,0:T(8,128)(2,1)} %get-tuple-element.77), channel_id=1, source_target_pairs={{0,4},{2,6},{4,0},{6,2},{8,12},{10,14},{12,8},{14,10},{16,20},{18,... | collective-permute-start | bytes 3145736 | tf_op jit(solution)/shard_map/ppermute | solution.py:159
  747.2 47.3 %collective-permute-start.40 = (bf16[2,128,2048]{2,1,0:T(8,128)(2,1)}, bf16[2,128,2048]{2,1,0:T(8,128)(2,1)}, u32[]{:S(2)}, u32[]{:S(2)}) collective-permute-start(bf16[2,128,2048]{2,1,0:T(8,128)(2,1)} %get-tuple-element.75), channel_id=1, source_target_pairs={{0,1},{1,0},{2,3},{3,2},{4,5},{5,4},{6,7},{7,6},{8,9},{9,8},{10,11... | collective-permute-start | bytes 3145736 | tf_op jit(solution)/shard_map/ppermute | solution.py:157
  752.2 64.8 %collective-permute-start.30 = (bf16[2,128,2048]{1,2,0:T(8,128)(2,1)}, bf16[2,128,2048]{1,2,0:T(8,128)(2,1)}, u32[]{:S(2)}, u32[]{:S(2)}) collective-permute-start(bf16[2,128,2048]{1,2,0:T(8,128)(2,1)} %bitcast.406), channel_id=1, source_target_pairs={{0,5},{1,4},{2,7},{3,6},{4,1},{5,0},{6,3},{7,2},{8,13},{9,12},{10,... | collective-permute-start | bytes 3145736 | tf_op jit(solution)/shard_map/ppermute | solution.py:161
  754.8 83.2 %collective-permute-start.29 = (bf16[2,128,2048]{1,2,0:T(8,128)(2,1)}, bf16[2,128,2048]{1,2,0:T(8,128)(2,1)}, u32[]{:S(2)}, u32[]{:S(2)}) collective-permute-start(bf16[2,128,2048]{1,2,0:T(8,128)(2,1)} %bitcast.407), channel_id=1, source_target_pairs={{0,4},{2,6},{4,0},{6,2},{8,12},{10,14},{12,8},{14,10},{16,20},{18,... | collective-permute-start | bytes 3145736 | tf_op jit(solution)/shard_map/ppermute | solution.py:159
  766.6 417.0 %reduce-scatter.10.cloned.1.call-start = ((), (), s32[]{:S(2)}) async-start(), calls=%async_computation.15 | async-start | bytes 2359296 | tf_op jit(solution)/shard_map/reduce_scatter | solution.py:191
  772.0 65.9 %collective-permute-start.28 = (bf16[2,128,2048]{1,2,0:T(8,128)(2,1)}, bf16[2,128,2048]{1,2,0:T(8,128)(2,1)}, u32[]{:S(2)}, u32[]{:S(2)}) collective-permute-start(bf16[2,128,2048]{1,2,0:T(8,128)(2,1)} %bitcast.77), channel_id=1, source_target_pairs={{0,1},{1,0},{2,3},{3,2},{4,5},{5,4},{6,7},{7,6},{8,9},{9,8},{10,11... | collective-permute-start | bytes 3145736 | tf_op jit(solution)/shard_map/ppermute | solution.py:157
  844.5 46.9 %collective-permute-start.44 = (bf16[2,128,2048]{1,2,0:T(8,128)(2,1)S(1)}, bf16[2,128,2048]{1,2,0:T(8,128)(2,1)S(1)}, u32[]{:S(2)}, u32[]{:S(2)}) collective-permute-start(bf16[2,128,2048]{1,2,0:T(8,128)(2,1)S(1)} %get-tuple-element.61), channel_id=1, source_target_pairs={{0,4},{2,6},{4,0},{6,2},{8,12},{10,14},{12,8},{14,10},{16,20},{18,... | collective-permute-start | bytes 3145736 | tf_op jit(solution)/shard_map/ppermute | solution.py:159
  845.5 46.1 %collective-permute-start.43 = (bf16[2,128,2048]{1,2,0:T(8,128)(2,1)S(1)}, bf16[2,128,2048]{1,2,0:T(8,128)(2,1)S(1)}, u32[]{:S(2)}, u32[]{:S(2)}) collective-permute-start(bf16[2,128,2048]{1,2,0:T(8,128)(2,1)S(1)} %get-tuple-element.61), channel_id=1, source_target_pairs={{0,1},{1,0},{2,3},{3,2},{4,5},{5,4},{6,7},{7,6},{8,9},{9,8},{10,11... | collective-permute-start | bytes 3145736 | tf_op jit(solution)/shard_map/ppermute | solution.py:157
  906.4 306.5 %reduce-scatter.12.cloned.1.call-start = ((), (), s32[]{:S(2)}) async-start(), calls=%async_computation.16 | async-start | bytes 4718592 | tf_op jit(solution)/shard_map/reduce_scatter | solution.py:191
  954.0 264.3 %reduce-scatter.14.cloned.1.call-start = ((), (), s32[]{:S(2)}) async-start(), calls=%async_computation.17 | async-start | bytes 7077888 | tf_op jit(solution)/shard_map/reduce_scatter | solution.py:191
  963.9 287.1 %reduce-scatter.8.cloned.1.call-start = ((), (), s32[]{:S(2)}) async-start(), calls=%async_computation.14 | async-start | bytes 7077888 | tf_op jit(solution)/shard_map/reduce_scatter | solution.py:191
  992.7 263.0 %reduce-scatter.18.cloned.1.call-start = ((), (), s32[]{:S(2)}) async-start(), calls=%async_computation.19 | async-start | bytes 9437184 | tf_op jit(solution)/shard_map/reduce_scatter | solution.py:191
  1006.9 326.6 %reduce-scatter.20.cloned.1.call-start = ((), (), s32[]{:S(2)}) async-start(), calls=%async_computation.20 | async-start | bytes 9437184 | tf_op jit(solution)/shard_map/reduce_scatter | solution.py:191
  1029.6 27.3 %collective-permute-start.54 = (bf16[2,64,4096]{2,1,0:T(8,128)(2,1)}, bf16[2,64,4096]{2,1,0:T(8,128)(2,1)}, u32[]{:S(2)}, u32[]{:S(2)}) collective-permute-start(bf16[2,64,4096]{2,1,0:T(8,128)(2,1)} %get-tuple-element.70), channel_id=1, source_target_pairs={{0,5},{1,4},{2,7},{3,6},{4,1},{5,0},{6,3},{7,2},{8,13},{9,12},{10,... | collective-permute-start | bytes 3145736 | tf_op jit(solution)/shard_map/ppermute | solution.py:161
  1031.2 48.3 %collective-permute-start.53 = (bf16[2,64,4096]{2,1,0:T(8,128)(2,1)}, bf16[2,64,4096]{2,1,0:T(8,128)(2,1)}, u32[]{:S(2)}, u32[]{:S(2)}) collective-permute-start(bf16[2,64,4096]{2,1,0:T(8,128)(2,1)} %get-tuple-element.71), channel_id=1, source_target_pairs={{0,4},{2,6},{4,0},{6,2},{8,12},{10,14},{12,8},{14,10},{16,20},{18,... | collective-permute-start | bytes 3145736 | tf_op jit(solution)/shard_map/ppermute | solution.py:159
  1032.2 47.3 %collective-permute-start.52 = (bf16[2,64,4096]{2,1,0:T(8,128)(2,1)}, bf16[2,64,4096]{2,1,0:T(8,128)(2,1)}, u32[]{:S(2)}, u32[]{:S(2)}) collective-permute-start(bf16[2,64,4096]{2,1,0:T(8,128)(2,1)} %get-tuple-element.69), channel_id=1, source_target_pairs={{0,1},{1,0},{2,3},{3,2},{4,5},{5,4},{6,7},{7,6},{8,9},{9,8},{10,11... | collective-permute-start | bytes 3145736 | tf_op jit(solution)/shard_map/ppermute | solution.py:157
  1047.2 54.6 %collective-permute-start.48 = (bf16[2,128,2048]{2,1,0:T(8,128)(2,1)}, bf16[2,128,2048]{2,1,0:T(8,128)(2,1)S(1)}, u32[]{:S(2)}, u32[]{:S(2)}) collective-permute-start(bf16[2,128,2048]{2,1,0:T(8,128)(2,1)} %get-tuple-element.73), channel_id=1, source_target_pairs={{0,5},{1,4},{2,7},{3,6},{4,1},{5,0},{6,3},{7,2},{8,13},{9,12},{10,... | collective-permute-start | bytes 3145736 | tf_op jit(solution)/shard_map/ppermute | solution.py:161
  1048.7 74.6 %collective-permute-start.47 = (bf16[2,128,2048]{2,1,0:T(8,128)(2,1)}, bf16[2,128,2048]{2,1,0:T(8,128)(2,1)}, u32[]{:S(2)}, u32[]{:S(2)}) collective-permute-start(bf16[2,128,2048]{2,1,0:T(8,128)(2,1)} %get-tuple-element.74), channel_id=1, source_target_pairs={{0,4},{2,6},{4,0},{6,2},{8,12},{10,14},{12,8},{14,10},{16,20},{18,... | collective-permute-start | bytes 3145736 | tf_op jit(solution)/shard_map/ppermute | solution.py:159
  1056.9 66.4 %collective-permute-start.46 = (bf16[2,128,2048]{2,1,0:T(8,128)(2,1)}, bf16[2,128,2048]{2,1,0:T(8,128)(2,1)}, u32[]{:S(2)}, u32[]{:S(2)}) collective-permute-start(bf16[2,128,2048]{2,1,0:T(8,128)(2,1)} %get-tuple-element.72), channel_id=1, source_target_pairs={{0,1},{1,0},{2,3},{3,2},{4,5},{5,4},{6,7},{7,6},{8,9},{9,8},{10,11... | collective-permute-start | bytes 3145736 | tf_op jit(solution)/shard_map/ppermute | solution.py:157
  1135.6 48.1 %collective-permute-start.66 = (bf16[64,2048]{1,0:T(8,128)(2,1)}, bf16[64,2048]{1,0:T(8,128)(2,1)S(1)}, u32[]{:S(2)}, u32[]{:S(2)}) collective-permute-start(bf16[64,2048]{1,0:T(8,128)(2,1)} %reduce-scatter.16.cloned.1.call-done), channel_id=1, source_target_pairs={{0,2},{2,0},{4,6},{6,4},{8,10},{10,8},{12,14},{14,12},{16,18},{18,... | collective-permute-start | bytes 786440 | tf_op jit(solution)/shard_map/ppermute | solution.py:261
  1219.5 27.3 %collective-permute-start.65 = (bf16[128,1536]{1,0:T(8,128)(2,1)S(1)}, bf16[128,1536]{1,0:T(8,128)(2,1)S(1)}, u32[]{:S(2)}, u32[]{:S(2)}) collective-permute-start(bf16[128,1536]{1,0:T(8,128)(2,1)S(1)} %get-tuple-element.134), channel_id=1, source_target_pairs={{0,5},{1,4},{2,7},{3,6},{4,1},{5,0},{6,3},{7,2},{8,13},{9,12},{10,... | collective-permute-start | bytes 1179656 | tf_op jit(solution)/shard_map/ppermute | solution.py:161
  1252.1 81.4 %collective-permute-start.57 = (bf16[128,1536]{1,0:T(8,128)(2,1)S(1)}, bf16[128,1536]{1,0:T(8,128)(2,1)}, u32[]{:S(2)}, u32[]{:S(2)}) collective-permute-start(bf16[128,1536]{1,0:T(8,128)(2,1)S(1)} %get-tuple-element.136), channel_id=1, source_target_pairs={{0,5},{1,4},{2,7},{3,6},{4,1},{5,0},{6,3},{7,2},{8,13},{9,12},{10,... | collective-permute-start | bytes 1179656 | tf_op jit(solution)/shard_map/ppermute | solution.py:161
  1253.7 81.3 %collective-permute-start.56 = (bf16[128,1536]{1,0:T(8,128)(2,1)S(1)}, bf16[128,1536]{1,0:T(8,128)(2,1)}, u32[]{:S(2)}, u32[]{:S(2)}) collective-permute-start(bf16[128,1536]{1,0:T(8,128)(2,1)S(1)} %get-tuple-element.136), channel_id=1, source_target_pairs={{0,4},{2,6},{4,0},{6,2},{8,12},{10,14},{12,8},{14,10},{16,20},{18,... | collective-permute-start | bytes 1179656 | tf_op jit(solution)/shard_map/ppermute | solution.py:159
  1256.9 83.4 %collective-permute-start.70 = (bf16[128,2048]{1,0:T(8,128)(2,1)S(1)}, bf16[128,2048]{1,0:T(8,128)(2,1)S(1)}, u32[]{:S(2)}, u32[]{:S(2)}) collective-permute-start(bf16[128,2048]{1,0:T(8,128)(2,1)S(1)} %get-tuple-element.125), channel_id=1, source_target_pairs={{0,5},{1,4},{2,7},{3,6},{4,1},{5,0},{6,3},{7,2},{8,13},{9,12},{10,... | collective-permute-start | bytes 1572872 | tf_op jit(solution)/shard_map/ppermute | solution.py:161
  1258.5 81.8 %collective-permute-start.69 = (bf16[128,2048]{1,0:T(8,128)(2,1)S(1)}, bf16[128,2048]{1,0:T(8,128)(2,1)S(1)}, u32[]{:S(2)}, u32[]{:S(2)}) collective-permute-start(bf16[128,2048]{1,0:T(8,128)(2,1)S(1)} %get-tuple-element.125), channel_id=1, source_target_pairs={{0,4},{2,6},{4,0},{6,2},{8,12},{10,14},{12,8},{14,10},{16,20},{18,... | collective-permute-start | bytes 1572872 | tf_op jit(solution)/shard_map/ppermute | solution.py:159
  1274.4 65.9 %collective-permute-start.68 = (bf16[128,2048]{1,0:T(8,128)(2,1)S(1)}, bf16[128,2048]{1,0:T(8,128)(2,1)S(1)}, u32[]{:S(2)}, u32[]{:S(2)}) collective-permute-start(bf16[128,2048]{1,0:T(8,128)(2,1)S(1)} %get-tuple-element.126), channel_id=1, source_target_pairs={{0,1},{1,0},{2,3},{3,2},{4,5},{5,4},{6,7},{7,6},{8,9},{9,8},{10,11... | collective-permute-start | bytes 1572872 | tf_op jit(solution)/shard_map/ppermute | solution.py:157
  (91 other events, 1365.8 us)
Sparse Core Ops, SparseCore 0:
  50.1 66.2 all-gather.7
  118.5 27.7 all-gather.9
  148.5 46.6 all-gather.13
  197.2 63.5 all-gather.11
  262.2 27.7 all-gather.15
  292.0 81.5 all-gather.17
  375.8 80.6 all-gather.19
  766.7 43.2 reduce-scatter.15
  906.5 43.3 reduce-scatter.9
  954.1 57.6 reduce-scatter.11
  1014.1 67.9 reduce-scatter.13
  1084.3 68.1 reduce-scatter.7
  1154.8 88.7 reduce-scatter.17
  1245.7 87.7 reduce-scatter.19

commit v2 on v1

v2 whole, which is shorter than its diff:
```python
import functools

import jax
import jax.numpy as jnp
from jax import lax
from jax.experimental import pallas as pl
from jax.experimental.pallas import tpu as pltpu
from jax.sharding import PartitionSpec as P

HEADS = 16
HEAD_DIM = 128
EPSILON = 1e-05
SCALE = HEAD_DIM ** (-0.5)
BF16 = jnp.bfloat16
F32 = jnp.float32
TP_HEADS = HEADS // 4
TP_WIDTH = TP_HEADS * HEAD_DIM


def rounded(values):
    return values.astype(BF16)


def after(values, *earlier):
    return lax.optimization_barrier((values,) + earlier)[0]


def after_all(pieces, *earlier):
    return list(after(tuple(pieces), *earlier))


def mm(left, right):
    return lax.dot_general(left, right, (((1,), (0,)), ((), ())), preferred_element_type=F32)


def mm_t(left, right):
    return lax.dot_general(left, right, (((1,), (1,)), ((), ())), preferred_element_type=F32)


def outer(left, right):
    return lax.dot_general(left, right, (((0,), (0,)), ((), ())), preferred_element_type=F32)


def layer_norm(values, norm_gain):
    centred = values - jnp.mean(values, axis=-1, keepdims=True)
    spread = jnp.mean(centred * centred, axis=-1, keepdims=True)
    return centred * lax.rsqrt(spread + EPSILON) * norm_gain


def norm_back(values, norm_gain, grad_normed):
    centred = values - jnp.mean(values, axis=-1, keepdims=True)
    inverse = lax.rsqrt(jnp.mean(centred * centred, axis=-1, keepdims=True) + EPSILON)
    unit = centred * inverse
    scaled = grad_normed * norm_gain
    result = inverse * (
        scaled
        - jnp.mean(scaled, axis=-1, keepdims=True)
        - unit * jnp.mean(scaled * unit, axis=-1, keepdims=True)
    )
    return result, jnp.sum(grad_normed * unit, axis=tuple(range(values.ndim - 1)))


def feed_forward_kernel(*refs):
    normed_refs, grad_refs = refs[:4], refs[4:8]
    up, down, active_ref, grad_hidden_ref, normed, out_grad = refs[8:]
    rows = normed_refs[0].shape[0]

    @pl.when(pl.program_id(0) == 0)
    def _():
        for k in range(4):
            normed[k * rows : (k + 1) * rows, :] = normed_refs[k][...]
            out_grad[k * rows : (k + 1) * rows, :] = grad_refs[k][...]

    for part in range(2):
        here = slice(2 * part * rows, 2 * (part + 1) * rows)
        hidden = mm(normed[here, :], up[...])
        half = 0.5 * (1.0 + lax.erf(hidden * (0.5**0.5)))
        active_ref[here, :] = rounded(hidden * half)
        grad_active = rounded(mm_t(out_grad[here, :], down[...])).astype(F32)
        slope = half + hidden * (jnp.exp(-0.5 * hidden * hidden) * (0.5 / jnp.pi) ** 0.5)
        grad_hidden_ref[here, :] = rounded(slope * grad_active)


def feed_forward(normed, out_grad, up, down, block=256):
    rows, d_model = normed[0].shape
    hidden = up.shape[1]
    whole = pl.BlockSpec((rows, d_model), lambda i: (0, 0), pipeline_mode=pl.Buffered(1))
    result = jax.ShapeDtypeStruct((4 * rows, hidden), BF16)
    return pl.pallas_call(
        feed_forward_kernel,
        grid=(hidden // block,),
        in_specs=[whole] * 8
        + [
            pl.BlockSpec((d_model, block), lambda i: (0, i)),
            pl.BlockSpec((block, d_model), lambda i: (i, 0)),
        ],
        out_specs=[pl.BlockSpec((4 * rows, block), lambda i: (0, i))] * 2
        + [pl.BlockSpec((4 * rows, d_model), lambda i: (0, 0))] * 2,
        out_shape=[result, result] + [jax.ShapeDtypeStruct((4 * rows, d_model), BF16)] * 2,
        compiler_params=pltpu.CompilerParams(vmem_limit_bytes=56 * 1024 * 1024),
    )(*normed, *out_grad, up, down)


def soft(queries, keys, usable):
    scores = mm_t(queries, keys) * SCALE
    if usable is not None:
        scores = jnp.where(usable, scores, -1e30)
    grown = jnp.exp(scores - jnp.max(scores, axis=-1, keepdims=True))
    return grown / jnp.sum(grown, axis=-1, keepdims=True)


def columns_at(index):
    return slice(index * HEAD_DIM, (index + 1) * HEAD_DIM)


def cut(refs, ky, index):
    return jnp.concatenate([refs[2 * ky + kx][0, :, columns_at(index)] for kx in range(2)], axis=0)


def put(refs, ky, index, values):
    rows = values.shape[0] // 2
    for kx in range(2):
        part = values[kx * rows : (kx + 1) * rows]
        refs[2 * ky + kx][0, :, columns_at(index)] = part.astype(BF16)


def attend_body(queries, pairs, key_at, value_at, usable, mix):
    for ky in range(2):
        for head in range(TP_HEADS):
            mask = None if usable is None else usable[ky, 0] > 0
            prob = soft(cut(queries, ky, head), cut(pairs, ky, key_at + head), mask)
            put(mix, ky, head, mm(rounded(prob), cut(pairs, ky, value_at + head)))


def attend_back_body(queries, pairs, key_at, value_at, usable, grads, gqueries, gpairs):
    for ky in range(2):
        for head in range(TP_HEADS):
            mask = None if usable is None else usable[ky, 0] > 0
            query_rows = cut(queries, ky, head)
            key_rows = cut(pairs, ky, key_at + head)
            grad_mix = cut(grads, ky, head)
            prob = soft(query_rows, key_rows, mask)
            grad_prob = mm_t(grad_mix, cut(pairs, ky, value_at + head))
            put(gpairs, ky, value_at + head, outer(rounded(prob), grad_mix))
            grad_scores = prob * (grad_prob - jnp.sum(prob * grad_prob, axis=-1, keepdims=True))
            grad_raw = rounded(grad_scores * SCALE)
            put(gqueries, ky, head, mm(grad_raw, key_rows))
            put(gpairs, ky, key_at + head, outer(grad_raw, query_rows))


def self_kernel(*refs):
    attend_body(refs[:4], refs[:4], TP_HEADS, 2 * TP_HEADS, None, refs[4:])


def self_back_kernel(*refs):
    attend_back_body(
        refs[:4], refs[:4], TP_HEADS, 2 * TP_HEADS, None, refs[4:8], refs[8:], refs[8:]
    )


def cross_kernel(usable, *refs):
    attend_body(refs[:4], refs[4:8], 0, TP_HEADS, usable, refs[8:])


def cross_back_kernel(usable, *refs):
    attend_back_body(
        refs[:4], refs[4:8], 0, TP_HEADS, usable, refs[8:12], refs[12:16], refs[16:]
    )


def per_image(kernel, usable, pieces, widths):
    images = pieces[0].shape[0]

    def block(shape):
        return pl.BlockSpec((1,) + tuple(shape[1:]), lambda i: (i, 0, 0))

    shapes = [
        pieces[like].shape[:2] + (width,) for like, width in widths for _ in range(4)
    ]
    in_specs = [block(piece.shape) for piece in pieces]
    if usable is not None:
        slots = usable.shape[-1]
        in_specs = [pl.BlockSpec((2, 1, 1, slots), lambda i: (0, i, 0, 0))] + in_specs
        pieces = [usable] + list(pieces)
    return pl.pallas_call(
        kernel,
        grid=(images,),
        in_specs=in_specs,
        out_specs=[block(shape) for shape in shapes],
        out_shape=[jax.ShapeDtypeStruct(shape, BF16) for shape in shapes],
        compiler_params=pltpu.CompilerParams(vmem_limit_bytes=48 * 1024 * 1024),
    )(*pieces)


def whole_call(kernel, place, args, shapes, dtype=BF16):
    vmem = pl.BlockSpec(memory_space=pltpu.VMEM)
    return pl.pallas_call(
        kernel,
        in_specs=[pl.BlockSpec(memory_space=pltpu.SMEM)] + [vmem] * len(args),
        out_specs=[vmem] * len(shapes),
        out_shape=[jax.ShapeDtypeStruct(shape, dtype) for shape in shapes],
        compiler_params=pltpu.CompilerParams(vmem_limit_bytes=48 * 1024 * 1024),
    )(place, *args)


def joined(refs):
    return jnp.concatenate([ref[...] for ref in refs], axis=0)


def put_head_rows(target, column, mix, grads):
    full = outer(joined(mix), joined(grads))
    half = full.shape[0] // 2
    kept = jnp.where(pl.program_id(0) % 2 == 0, full[:half], full[half:]).astype(BF16)
    for j in range(4):
        target[j * half : (j + 1) * half, column:] = kept[:, j * TP_WIDTH : (j + 1) * TP_WIDTH]


def self_weights_kernel(*refs):
    normed, branch, gqkv, mix, target = refs[:4], refs[4:8], refs[8:12], refs[12:16], refs[16]
    wide = 3 * TP_WIDTH
    target[:, :wide] = outer(joined(normed), joined(gqkv)).astype(BF16)
    put_head_rows(target, wide, mix, branch)


def cross_weights_kernel(*refs):
    normed, branch, gquery, mix = refs[:4], refs[4:8], refs[8:12], refs[12:16]
    feat, gpair, target = refs[16:]
    wide = TP_WIDTH
    target[:, :wide] = outer(joined(normed), joined(gquery)).astype(BF16)
    target[:, wide : 3 * wide] = outer(feat[...], gpair[...]).astype(BF16)
    put_head_rows(target, 3 * wide, mix, branch)


def text_weights_kernel(*refs):
    low, high, gfeat, target = refs[:4], refs[4:8], refs[8], refs[9]
    target[:, :TP_WIDTH] = outer(joined(low), gfeat[...]).astype(BF16)
    target[:, TP_WIDTH:] = outer(joined(high), gfeat[...]).astype(BF16)


def weight_call(kernel, d_model, columns, args, specs, blocks):
    rows = d_model // blocks
    return pl.pallas_call(
        kernel,
        grid=(blocks,),
        in_specs=specs,
        out_specs=pl.BlockSpec((rows, columns), lambda i: (i, 0)),
        out_shape=jax.ShapeDtypeStruct((d_model, columns), BF16),
        compiler_params=pltpu.CompilerParams(vmem_limit_bytes=56 * 1024 * 1024),
    )(*args)


def column_block(rows, columns, index):
    return pl.BlockSpec((rows, columns), lambda i: (0, index(i)))


def whole_block(array):
    return pl.BlockSpec(array.shape, lambda i: (0, 0), pipeline_mode=pl.Buffered(1))


def self_weights(normed, branch, gqkv, mix, blocks=8):
    tokens, d_model = normed[0].shape
    rows = d_model // blocks
    specs = [column_block(tokens, rows, lambda i: i)] * 4
    specs += [whole_block(a) for a in branch + gqkv]
    specs += [column_block(tokens, HEAD_DIM, lambda i: i // 2)] * 4
    args = (*normed, *branch, *gqkv, *mix)
    return weight_call(self_weights_kernel, d_model, 4 * TP_WIDTH, args, specs, blocks)


def cross_weights(normed, branch, feat, gquery, gpair, mix, blocks=8):
    tokens, d_model = normed[0].shape
    rows = d_model // blocks
    specs = [column_block(tokens, rows, lambda i: i)] * 4
    specs += [whole_block(a) for a in branch + gquery]
    specs += [column_block(tokens, HEAD_DIM, lambda i: i // 2)] * 4
    specs += [column_block(feat.shape[0], rows, lambda i: i), whole_block(gpair)]
    args = (*normed, *branch, *gquery, *mix, feat, gpair)
    return weight_call(cross_weights_kernel, d_model, 4 * TP_WIDTH, args, specs, blocks)


def text_weights(captions, gfeat, blocks=8):
    slots, text_d = captions[0].shape
    rows = text_d // 2 // blocks
    specs = [column_block(slots, rows, lambda i: i)] * 4
    specs += [column_block(slots, rows, lambda i: i + blocks)] * 4 + [whole_block(gfeat)]
    args = (*captions, *captions, gfeat)
    return weight_call(text_weights_kernel, text_d // 2, 2 * TP_WIDTH, args, specs, blocks)


def make(devices, planes=4):
    spread = devices // (2 * planes)
    half_spread = spread // 2
    groups = [
        [(a * 2 + y) * spread + b for a in range(planes) for b in range(spread)] for y in range(2)
    ]

    def swap(values, over_y, over_x):
        if not over_y:
            return lax.ppermute(values, "seq", [(0, 1), (1, 0)])
        if not over_x:
            return lax.ppermute(values, "dp", [(d, d ^ spread) for d in range(devices)])
        pairs = [(2 * d + x, 2 * (d ^ spread) + 1 - x) for d in range(devices) for x in range(2)]
        return lax.ppermute(values, ("dp", "seq"), pairs)

    def flip(values, bit):
        return lax.ppermute(values, "dp", [(d, d ^ bit) for d in range(devices)])

    def shuffle(values):
        lead = values.shape[:-1]
        blocks = values.reshape(lead + (planes, 2, spread, -1))
        return jnp.swapaxes(blocks, -3, -2).reshape(values.shape)

    def unshuffle(values):
        lead = values.shape[:-1]
        blocks = values.reshape(lead + (planes, spread, 2, -1))
        return jnp.swapaxes(blocks, -3, -2).reshape(values.shape)

    def gather_tokens(own):
        half = own.shape[0] // 2
        over_x, over_y = swap(own, 0, 1), swap(own, 1, 0)
        far = jnp.concatenate([swap(over_y[:half], 0, 1), swap(over_x[half:], 1, 0)], axis=0)
        return [own, over_x, over_y, far]

    def gather_direct(own):
        return [own, swap(own, 0, 1), swap(own, 1, 0), swap(own, 1, 1)]

    def scatter_tokens(parts):
        here, to_x, to_y, far = lax.optimization_barrier(tuple(parts))
        half = here.shape[0] // 2
        by_x, by_y = swap(far[:half], 0, 1), swap(far[half:], 1, 0)
        to_y = jnp.concatenate([rounded(to_y[:half].astype(F32) + by_x), to_y[half:]], axis=0)
        to_x = jnp.concatenate([to_x[:half], rounded(to_x[half:].astype(F32) + by_y)], axis=0)
        total = here.astype(F32) + swap(to_x, 0, 1).astype(F32)
        return total + swap(to_y, 1, 0).astype(F32), (to_x, to_y)

    def gather_weight(payload):
        return lax.all_gather(payload, "dp", axis=0, tiled=True, axis_index_groups=groups)

    def reduce_weight(parts):
        return lax.psum_scatter(
            parts, "dp", scatter_dimension=0, tiled=True, axis_index_groups=groups
        )

    def gather_small(values, d):
        bit = 1
        while bit < devices:
            other = flip(values, bit)
            low = (d & bit) == 0
            values = jnp.concatenate(
                [jnp.where(low, values, other), jnp.where(low, other, values)], axis=1
            )
            bit *= 2
        return values

    def reduce_small(values, d):
        values = values + swap(values, 0, 1)
        bit = devices // 2
        while bit:
            half = values.shape[1] // 2
            low = (d & bit) == 0
            kept = jnp.where(low, values[:, :half], values[:, half:])
            values = kept + flip(jnp.where(low, values[:, half:], values[:, :half]), bit)
            bit //= 2
        return values


    def copy_heads(place, weights, own, other, at):
        y, x = place[0], place[1]
        for yy, target in ((y, own), (1 - y, other)):
            for index, weight in enumerate(weights):
                for a in range(planes):
                    start = pl.multiple_of((4 * a + 2 * yy + x) * HEAD_DIM, HEAD_DIM)
                    column = at + index * TP_WIDTH + a * HEAD_DIM
                    target[:, column : column + HEAD_DIM] = weight[:, pl.ds(start, HEAD_DIM)]

    def shuffled_blocks(columns):
        size = columns // devices
        for a in range(planes):
            for b in range(spread):
                for y in range(2):
                    yield (a * spread + b) * 2 + y, (a * 2 + y) * spread + b, size

    def copy_halves(place, weight, kept, passed):
        half = weight.shape[0] // 2
        top = place[2]
        for target, which in ((kept, top), (passed, 1 - top)):
            first = pl.multiple_of(which * half, half)
            for to, at, size in shuffled_blocks(weight.shape[1]):
                target[:, to * size : (to + 1) * size] = weight[
                    pl.ds(first, half), at * size : (at + 1) * size
                ]

    def prepare(place, images, out_grad, captions, down, *targets):
        pack_down(place, down, targets[3])
        for source, target in ((images, targets[0]), (out_grad, targets[1])):
            for to, at, size in shuffled_blocks(source.shape[1]):
                target[:, to * size : (to + 1) * size] = source[:, at * size : (at + 1) * size]
        half = captions.shape[1] // 2
        for to, at, size in shuffled_blocks(half):
            for h in range(2):
                first = 2 * at * size + h * size
                target = targets[2]
                target[:, h * half + to * size : h * half + (to + 1) * size] = captions[
                    :, first : first + size
                ]

    def natural(parts, place, source, target):
        del place
        width = source.shape[1] // parts
        for to, at, size in shuffled_blocks(width):
            for h in range(parts):
                first = parts * at * size + h * size
                target[:, first : first + size] = source[
                    :, h * width + to * size : h * width + (to + 1) * size
                ]

    def pack_self(place, query, key, value, out, own, other, kept, passed):
        copy_heads(place, (query, key, value), own, other, 0)
        copy_halves(place, out, kept, passed)

    def pack_cross(place, query, key, value, out, text, own, other, kept, passed):
        copy_heads(place, (query, key, value), own, other, 0)
        copy_halves(place, out, kept, passed)
        y, x = place[0], place[1]
        rows = query.shape[0]
        for yy, target in ((y, own), (1 - y, other)):
            start = pl.multiple_of((2 * yy + x) * TP_WIDTH, TP_WIDTH)
            size = TP_WIDTH // (2 * spread)
            for h in range(2):
                block = text[h * rows : (h + 1) * rows, pl.ds(start, TP_WIDTH)]
                for b in range(spread):
                    for yb in range(2):
                        at = (yb * spread + b) * size
                        column = (3 + h) * TP_WIDTH + (b * 2 + yb) * size
                        target[:, column : column + size] = block[:, at : at + size]

    def pack_down(place, down, payload):
        width = payload.shape[0]
        first = pl.multiple_of(place[1] * width, width)
        for to, at, size in shuffled_blocks(down.shape[1]):
            payload[:, to * size : (to + 1) * size] = down[
                pl.ds(first, width), at * size : (at + 1) * size
            ]

    def pack_up(place, up, own, other):
        y, x = place[0], place[1]
        ff_rows = up.shape[1] // devices
        width = ff_rows // 2
        for yy, target in ((y, own), (1 - y, other)):
            for a in range(planes):
                for b in range(spread):
                    start = ((a * 2 + yy) * spread + b) * ff_rows + x * width
                    column = (a * spread + b) * width
                    target[:, column : column + width] = up[
                        :, pl.ds(pl.multiple_of(start, width), width)
                    ]

    def join(place, own, other, *rest):
        payload = rest[-1]
        y = place[0]
        rows, columns = own.shape
        payload[pl.ds(pl.multiple_of(y * rows, rows), rows), :columns] = own[...]
        payload[pl.ds(pl.multiple_of((1 - y) * rows, rows), rows), :columns] = other[...]
        if len(rest) == 1:
            return
        kept, passed = rest[:2]
        half = kept.shape[0]

        def fill(source):
            for j in range(4):
                payload[j * half : (j + 1) * half, columns:] = source[
                    :, j * TP_WIDTH : (j + 1) * TP_WIDTH
                ]

        @pl.when(place[2] == place[1])
        def _():
            fill(kept)

        @pl.when(place[2] != place[1])
        def _():
            fill(passed)


    def at_place(place, write):
        for yy in range(2):
            for xx in range(2):
                pl.when((place[0] == yy) & (place[1] == xx))(lambda yy=yy, xx=xx: write(yy, xx))

    def unpack_down(place, own, other, target):
        width = own.shape[0]

        def write(y, x):
            for which, source in ((x, own), (1 - x, other)):
                for to, at, size in shuffled_blocks(own.shape[1]):
                    target[which * width : (which + 1) * width, at * size : (at + 1) * size] = (
                        source[:, to * size : (to + 1) * size].astype(F32)
                    )

        at_place(place, write)

    def unpack_up(place, *refs):
        pieces, target = refs[:4], refs[4]
        width = target.shape[1] // devices // 2

        def write(y, x):
            for k in range(4):
                yy, xx = y ^ (k // 2), x ^ (k % 2)
                for a in range(planes):
                    for b in range(spread):
                        to = ((a * 2 + yy) * spread + b) * 2 * width + xx * width
                        at = (a * spread + b) * width
                        target[:, to : to + width] = pieces[k][:, at : at + width].astype(F32)

        at_place(place, write)

    def unpack_text(place, *refs):
        pieces, target = refs[:4], refs[4]
        rows = pieces[0].shape[0]
        size = TP_WIDTH // (2 * spread)

        def write(y, x):
            for k in range(4):
                first = (2 * (y ^ (k // 2)) + (x ^ (k % 2))) * TP_WIDTH
                for h in range(2):
                    for b in range(spread):
                        for yb in range(2):
                            to = first + (yb * spread + b) * size
                            at = h * TP_WIDTH + (b * 2 + yb) * size
                            target[h * rows : (h + 1) * rows, to : to + size] = pieces[k][
                                :, at : at + size
                            ].astype(F32)

        at_place(place, write)

    def unpack_heads(place, *refs):
        pieces, halves, weights = refs[:4], refs[4:8], refs[8:11]
        out = refs[11]
        rows = out.shape[0]
        half = rows // 2

        def write(y, x):
            for k in range(4):
                yy, xx = y ^ (k // 2), x ^ (k % 2)
                for index, target in enumerate(weights):
                    for a in range(planes):
                        to = (4 * a + 2 * yy + xx) * HEAD_DIM
                        at = index * TP_WIDTH + a * HEAD_DIM
                        target[:, to : to + HEAD_DIM] = pieces[k][:, at : at + HEAD_DIM].astype(F32)
        at_place(place, write)

        def write_out(top, x):
            near = halves[:2] if top == x else halves[2:]
            for which, source in ((top, near[0]), (1 - top, near[1])):
                for to, at, size in shuffled_blocks(out.shape[1]):
                    out[which * half : (which + 1) * half, at * size : (at + 1) * size] = (
                        source[:, to * size : (to + 1) * size].astype(F32)
                    )

        for top in range(2):
            for xx in range(2):
                pl.when((place[2] == top) & (place[1] == xx))(
                    lambda top=top, xx=xx: write_out(top, xx)
                )

    def on_device(
        images,
        captions,
        cap_lengths,
        norm1_gain,
        w_query,
        w_key,
        w_value,
        w_out,
        norm2_gain,
        w_text,
        w_cross_query,
        w_cross_key,
        w_cross_value,
        w_cross_out,
        norm3_gain,
        w_up,
        w_down,
        out_grad,
    ):
        d = lax.axis_index("dp")
        x = lax.axis_index("seq")
        y = (d // spread) % 2
        top = (d % spread) // half_spread
        place = jnp.stack([y, x, top]).astype(jnp.int32)
        own_images, own_tokens, d_model = images.shape
        own_slots = captions.shape[1]
        text_d = captions.shape[2]
        ff_rows = w_down.shape[0]
        slots = 2 * own_slots
        rows = w_query.shape[0]
        half = rows // 2
        wide = 3 * TP_WIDTH
        fused = rows % 128 == 0 and half_spread == 1

        gains = gather_small(jnp.stack([norm1_gain, norm2_gain, norm3_gain]), d)
        own, other, kept, passed = whole_call(
            pack_self,
            place,
            (w_query, w_key, w_value, w_out),
            [(rows, wide), (rows, wide), (half, d_model), (half, d_model)],
        )
        other, passed = swap(other, 1, 0), flip(passed, half_spread)
        (self_load,) = whole_call(
            join, place, (own, other, kept, passed), [(2 * rows, wide + TP_WIDTH)]
        )
        self_full = gather_weight(self_load)

        cross_own, cross_other, kept, passed = whole_call(
            pack_cross,
            place,
            (after(w_cross_query, self_load, gains), w_cross_key, w_cross_value)
            + (w_cross_out, w_text),
            [(rows, 5 * TP_WIDTH), (rows, 5 * TP_WIDTH), (half, d_model), (half, d_model)],
        )
        width = ff_rows // 2
        if width % 128 == 0:
            up_own, up_other = whole_call(
                pack_up, place, (after(w_up, kept),), [(rows, width * planes * spread)] * 2
            )
        else:

            def up_columns(yy):
                return jnp.concatenate(
                    [
                        lax.dynamic_slice_in_dim(
                            w_up, ((a * 2 + yy) * spread + b) * ff_rows + x * width, width, 1
                        )
                        for a in range(planes)
                        for b in range(spread)
                    ],
                    axis=1,
                )

            up_own, up_other = up_columns(y), up_columns(1 - y)
        image_rows, out_grad_rows, caption_rows, down_load = whole_call(
            prepare,
            place,
            (
                after(images, up_own).reshape(-1, d_model),
                out_grad.reshape(-1, d_model),
                captions.reshape(-1, text_d),
                w_down,
            ),
            [(own_images * own_tokens, d_model)] * 2
            + [(own_images * own_slots, text_d), (width, d_model)],
        )
        gains = shuffle(gains.astype(F32))
        cross_other, passed = swap(cross_other, 1, 0), flip(passed, half_spread)
        up_other = swap(up_other, 1, 0)
        image_all = gather_tokens(image_rows)
        (cross_load,) = whole_call(
            join, place, (cross_own, cross_other, kept, passed), [(2 * rows, 6 * TP_WIDTH)]
        )
        cross_full = gather_weight(cross_load)
        (up_load,) = whole_call(join, place, (up_own, up_other), [(2 * rows, up_own.shape[1])])
        up_full = gather_weight(up_load)
        down_full = gather_weight(after(down_load, up_load))
        caption_all = gather_direct(after(caption_rows, image_all[1], image_all[2]))
        self_full = after(self_full, up_load)

        def head_rows(columns):
            blocks = columns.reshape(planes, 2, half_spread, 4, half, TP_WIDTH)
            blocks = blocks.transpose(0, 2, 1, 4, 3, 5)
            return blocks.reshape(TP_WIDTH, d_model)

        qkv_full, out_full = self_full[:, :wide], head_rows(self_full[:, wide:])
        cquery_full = cross_full[:, :TP_WIDTH]
        cpair_full = cross_full[:, TP_WIDTH:wide]
        text_full = jnp.concatenate(
            [cross_full[:, wide : wide + TP_WIDTH], cross_full[:, wide + TP_WIDTH : -TP_WIDTH]],
            axis=0,
        )
        cout_full = head_rows(cross_full[:, -TP_WIDTH:])

        all_lengths = jnp.concatenate([cap_lengths, swap(cap_lengths, 1, 0)])
        position = jnp.arange(own_slots)
        slot = jnp.concatenate([x * own_slots + position, (1 - x) * own_slots + position])
        usable = (slot[None, :] < all_lengths[:, None]).astype(F32)
        usable = usable.reshape(2, own_images, 1, slots)

        def by_image(pieces):
            return [piece.reshape(own_images, -1, piece.shape[-1]) for piece in pieces]

        def by_row(pieces):
            return [piece.reshape(-1, piece.shape[-1]) for piece in pieces]

        def each(multiply, pieces, weight):
            return [rounded(multiply(piece, weight)) for piece in pieces]

        def all_rows(pieces):
            return jnp.concatenate(pieces, axis=0)

        stream = image_rows.astype(F32)
        normed1 = [rounded(layer_norm(piece.astype(F32), gains[0])) for piece in image_all]
        qkv = by_image(each(mm, normed1, qkv_full))
        self_mix = by_row(per_image(self_kernel, None, qkv, [(0, TP_WIDTH)]))
        self_mix = after_all(self_mix, *caption_all)
        after_self = stream + scatter_tokens(each(mm, self_mix, out_full))[0]

        quarter = 2 * y + x

        def swap_slots(values, ky, kx):
            blocks = swap(values, ky, kx).reshape(2, 2, -1, values.shape[-1])
            blocks = blocks[::-1] if ky else blocks
            blocks = blocks[:, ::-1] if kx else blocks
            return blocks.reshape(values.shape)

        caption_rows_shape = caption_rows.shape
        caption_rows = all_rows(caption_all)
        part_feat = rounded(mm(caption_rows, text_full))
        caption_feat = jnp.zeros((part_feat.shape[0], d_model), BF16)
        for ky in range(2):
            for kx in range(2):
                piece = swap_slots(part_feat, ky, kx) if ky or kx else part_feat
                caption_feat = lax.dynamic_update_slice(
                    caption_feat, piece, (0, (quarter ^ (2 * ky + kx)) * TP_WIDTH)
                )
        cpair = rounded(mm(caption_feat, cpair_full))
        cpair = by_image(list(cpair.reshape(4, -1, 2 * TP_WIDTH)))

        normed2 = gather_tokens(rounded(layer_norm(after_self, gains[1])))
        cquery = by_image(each(mm, normed2, cquery_full))
        cross_mix = by_row(per_image(cross_kernel, usable, cquery + cpair, [(0, TP_WIDTH)]))
        after_cross = after_self + scatter_tokens(each(mm, cross_mix, cout_full))[0]

        normed3 = gather_tokens(rounded(layer_norm(after_cross, gains[2])))
        out_grad_all = gather_tokens(after(out_grad_rows, *normed3))
        active, grad_hidden, normed3, out_grad_all = feed_forward(
            normed3, out_grad_all, up_full, down_full
        )

        def pieces_of(values):
            return list(values.reshape(4, -1, values.shape[-1]))

        grad_parts = each(mm_t, pieces_of(grad_hidden), up_full)
        grad_normed3, sent3 = scatter_tokens(grad_parts)
        out_grad_all = after(out_grad_all, *grad_parts)
        grad_down_part = rounded(outer(active, out_grad_all))
        half_down = reduce_weight(grad_down_part)
        grad_up_part = rounded(outer(normed3, after(grad_hidden, grad_down_part)))
        layer_part = each(mm, pieces_of(after(active, grad_up_part, *sent3)), down_full)
        grad_normed3 = after(grad_normed3, *layer_part)
        grad_stream, grad_norm3 = norm_back(after_cross, gains[2], grad_normed3)
        grad_after_cross = out_grad_rows.astype(F32) + grad_stream

        branch2 = gather_tokens(rounded(grad_after_cross))
        up_sums = reduce_weight(after(grad_up_part, half_down, *branch2))
        down_pieces = [half_down, swap(half_down, 0, 1)]
        layer_part = after_all(layer_part, *branch2)
        layer_sum = rounded(after_cross + scatter_tokens(layer_part)[0])
        (layer_out,) = whole_call(
            functools.partial(natural, 1), place, (layer_sum,), [layer_sum.shape]
        )
        grad_cross_mix = by_image(each(mm_t, branch2, cout_full))
        back = per_image(
            cross_back_kernel,
            usable,
            cquery + cpair + grad_cross_mix,
            [(0, TP_WIDTH), (4, 2 * TP_WIDTH)],
        )
        gcquery, gcpair = by_row(back[:4]), all_rows(by_row(back[4:]))
        gcquery = after_all(gcquery, layer_sum)
        grad_parts = each(mm_t, gcquery, cquery_full)
        grad_normed2, sent2 = scatter_tokens(grad_parts)
        gcquery = list(after(tuple(gcquery), *grad_parts))
        grad_stream, grad_norm2 = norm_back(after_self, gains[1], grad_normed2)
        grad_after_self = grad_after_cross + grad_stream
        branch1 = gather_tokens(rounded(grad_after_self))

        grad_feat_part = rounded(mm_t(gcpair, cpair_full))
        grad_feat = None
        for ky in range(2):
            for kx in range(2):
                piece = lax.dynamic_slice_in_dim(
                    grad_feat_part, (quarter ^ (2 * ky + kx)) * TP_WIDTH, TP_WIDTH, 1
                )
                if ky or kx:
                    piece = after(swap_slots(piece, ky, kx), branch1[0])
                    grad_feat = grad_feat + piece.astype(F32)
                else:
                    grad_feat = piece.astype(F32)
        grad_feat = rounded(grad_feat)

        def head_blocks(parts):
            blocks = parts.reshape(planes, half_spread, 2, half, 4, TP_WIDTH)
            return blocks.transpose(0, 2, 1, 4, 3, 5).reshape(-1, TP_WIDTH)

        if fused:
            grad_cross_part = cross_weights(
                normed2, branch2, after(caption_feat, *sent2), gcquery, gcpair, cross_mix
            )
            grad_text_part = text_weights(caption_all, grad_feat)
        else:
            grad_cross_part = jnp.concatenate(
                [
                    rounded(outer(all_rows(normed2), all_rows(gcquery))),
                    rounded(outer(caption_feat, gcpair)),
                    head_blocks(rounded(outer(all_rows(cross_mix), all_rows(branch2)))),
                ],
                axis=1,
            )
            grad_text_part = rounded(outer(caption_rows, grad_feat))
            grad_text_part = jnp.concatenate(
                [grad_text_part[:d_model], grad_text_part[d_model:]], axis=1
            )
        cross_sums = reduce_weight(after(grad_cross_part, up_sums, down_pieces[1]))
        def four(summed, columns):
            own = lax.dynamic_slice(summed, (y * rows, 0), (rows, columns))
            other = lax.dynamic_slice(summed, ((1 - y) * rows, 0), (rows, columns))
            return [own, swap(own, 0, 1), swap(other, 1, 0), swap(other, 1, 1)]

        up_pieces = four(up_sums, up_sums.shape[1])
        grad_self_mix = by_image(each(mm_t, branch1, out_full))
        gqkv = by_row(per_image(self_back_kernel, None, qkv + grad_self_mix, [(0, wide)]))
        text_sums = reduce_weight(after(grad_text_part, cross_sums, *gqkv))
        grad_parts = each(mm_t, gqkv, qkv_full)
        grad_normed1, sent1 = scatter_tokens(grad_parts)
        gqkv = after_all(gqkv, *sent1)
        if fused:
            grad_self_part = self_weights(normed1, branch1, gqkv, self_mix)
        else:
            grad_self_part = jnp.concatenate(
                [
                    rounded(outer(all_rows(normed1), all_rows(gqkv))),
                    head_blocks(rounded(outer(all_rows(self_mix), all_rows(branch1)))),
                ],
                axis=1,
            )
        self_sums = reduce_weight(after(grad_self_part, text_sums, grad_normed1, *up_pieces))
        grad_stream, grad_norm1 = norm_back(stream, gains[0], grad_normed1)
        (image_grad,) = whole_call(
            functools.partial(natural, 1), place, (grad_after_self + grad_stream,), [image_rows.shape], F32
        )

        caption_part = each(mm_t, pieces_of(after(grad_feat, grad_normed1)), text_full)
        (caption_grad,) = whole_call(
            functools.partial(natural, 2), place, (scatter_tokens(caption_part)[0],), [caption_rows_shape], F32
        )
        caption_grad = caption_grad.reshape(captions.shape)


        def head_pieces(columns):
            own = columns.reshape(4, half, TP_WIDTH).transpose(1, 0, 2).reshape(half, -1)
            pairs = [
                (2 * i + j, 2 * (i ^ half_spread) + 1 - j) for i in range(devices) for j in range(2)
            ]
            far = lax.ppermute(own, ("dp", "seq"), pairs)
            return [own, flip(own, half_spread), swap(own, 0, 1), far]

        (grad_down,) = whole_call(
            unpack_down, place, down_pieces, [(2 * width, d_model)], F32
        )
        (grad_up,) = whole_call(unpack_up, place, up_pieces, [w_up.shape], F32)
        cross_pieces = four(cross_sums, wide) + head_pieces(cross_sums[:, -TP_WIDTH:])
        grad_cross_query, grad_cross_key, grad_cross_value, grad_cross_out = whole_call(
            unpack_heads, place, cross_pieces, [w_query.shape] * 4, F32
        )
        text_pieces = four(text_sums, 2 * TP_WIDTH)
        (grad_text,) = whole_call(unpack_text, place, text_pieces, [w_text.shape], F32)
        self_sums = after(self_sums, *down_pieces, *up_pieces, *cross_pieces, *text_pieces)
        self_pieces = four(self_sums, wide) + head_pieces(self_sums[:, -TP_WIDTH:])
        grad_query, grad_key, grad_value, grad_out = whole_call(
            unpack_heads, place, self_pieces, [w_query.shape] * 4, F32
        )

        norm_sums = unshuffle(jnp.stack([grad_norm1, grad_norm2, grad_norm3]))
        norm_sums = reduce_small(norm_sums, d)
        return (
            layer_out.reshape(images.shape),
            image_grad.reshape(images.shape),
            caption_grad,
            norm_sums[0],
            grad_query,
            grad_key,
            grad_value,
            grad_out,
            norm_sums[1],
            grad_text,
            grad_cross_query,
            grad_cross_key,
            grad_cross_value,
            grad_cross_out,
            norm_sums[2],
            grad_up,
            grad_down,
        )

    return on_device


def solution(mesh):
    tokens = P("dp", "seq", None)
    rows = P("dp", None)
    vector = P("dp")
    in_specs = (
        (tokens, tokens, vector)
        + (vector, rows, rows, rows, rows)
        + (vector, rows, rows, rows, rows, rows)
        + (vector, rows, rows)
        + (tokens,)
    )
    out_specs = (
        (tokens, tokens, tokens)
        + (vector, rows, rows, rows, rows)
        + (vector, rows, rows, rows, rows, rows)
        + (vector, rows, rows)
    )
    return jax.shard_map(
        make(mesh.shape["dp"]), mesh=mesh, in_specs=in_specs, out_specs=out_specs, check_vma=False
    )
```

time: 1380 us -> 975 us (0.71)
  waiting for transfers between devices: 614 us -> 456 us
  local copies, waits for them, and re-layouts: 207 us -> 66.8 us
  Pallas kernels: 24.7 us -> 126 us
  blocking collectives: 96.2 us -> 0 us
  other arithmetic: 120 us -> 40 us
  matrix products: 210 us -> 145 us
  starting transfers between devices: 78.5 us -> 120 us
    ppermute x20 -> x7, waiting for transfers between devices: 174 us -> 7.66 us  [swap(): return lax.ppermute(values, ('dp', 'seq'), pairs)]
    ppermute x23 -> x37, waiting for transfers between devices: 70.9 us -> 184 us  [swap(): return lax.ppermute(values, 'seq', [(0, 1), (1, 0)])]
    pallas_call x4 -> x23, Pallas kernels: 24.7 us -> 126 us  [the longest x3 42.7 us: weight_call(): pl.pallas_call(kernel, grid=(blocks,), in_specs=specs, out_specs=pl.Block...]
    ppermute x25 -> x37, waiting for transfers between devices: 307 us -> 224 us  [swap(): return lax.ppermute(values, 'dp', [(d, d ^ spread) for d in range(devices)])]
    unnamed x254 -> x308, local copies, waits for them, and re-layouts: 87 us -> 30.9 us
    all_gather x1 -> x0, blocking collectives: 48.3 us -> none  [on_device(): lax.all_gather(jnp.stack([norm1_gain, norm2_gain, norm3_gain]), 'dp', axi...]
    psum x1 -> x0, blocking collectives: 47.9 us -> none  [on_device(): lax.psum(jnp.stack([grad_norm1, grad_norm2, grad_norm3]), ('dp', 'seq'))]
    reduce_scatter x7 -> x5, waiting for transfers between devices: 58.6 us -> 13.1 us  [reduce_weight(): lax.psum_scatter(parts, 'dp', scatter_dimension=0, tiled=True, axis_index...]
  transfers between devices with their start and end apart: 86 -> 104, of which waited for: 46 -> 61; matrix products, arithmetic and copies ran while one was open for 30% -> 20% of each run, Pallas kernels for 1% -> 10%
where the time goes in v2:
time: 975 us; the launch traced here: 970 us
  waiting for transfers between devices  456 us (47%)
  matrix products  145 us (15%)
  Pallas kernels  126 us (13%)
  starting transfers between devices  120 us (12%)
  local copies, waits for them, and re-layouts  66.8 us (7%)
  other arithmetic  40 us (4%)
  between operations  16.8 us (2%)
    ppermute x37, waiting for transfers between devices, swap(): return lax.ppermute(values, 'dp', [(d, d ^ spread) for d in range(devices)])  224 us
    ppermute x37, waiting for transfers between devices, swap(): return lax.ppermute(values, 'seq', [(0, 1), (1, 0)])  184 us
    dot_general x25, matrix products, mm_t(): lax.dot_general(left, right, (((1,), (1,)), ((), ())), preferred_element_...  66.7 us
    dot_general x22, matrix products, mm(): lax.dot_general(left, right, (((1,), (0,)), ((), ())), preferred_element_...  52.3 us
    ppermute x37, starting transfers between devices, swap(): return lax.ppermute(values, 'dp', [(d, d ^ spread) for d in range(devices)])  51.9 us
    pallas_call x3, Pallas kernels, weight_call(): pl.pallas_call(kernel, grid=(blocks,), in_specs=specs, out_specs=pl.Block...  42.7 us
    ppermute x37, starting transfers between devices, swap(): return lax.ppermute(values, 'seq', [(0, 1), (1, 0)])  40.3 us
    pallas_call x15, Pallas kernels, whole_call(): pl.pallas_call(kernel, in_specs=[pl.BlockSpec(memory_space=pltpu.SMEM)] +...  33.2 us
  transfers between devices with their start and end apart: 104, of which 61 were waited for; matrix products, arithmetic and copies ran while one was open for 20% of the time, Pallas kernels for 10%

profile of v2, /device:TPU:0, one launch (start us, length us, event | category | flops | bytes accessed | tf_op | source)
XLA Modules:
  0.0 969.6 jit_solution(14019196156460586224)
XLA Ops:
  17.0 7.6 collective-permute-done.other
  30.5 12.6 %collective-permute-done.19.other = bf16[128,2560]{1,0:T(8,128)(2,1)S(1)} collective-permute-done((bf16[128,2560]{1,0:T(8,128)(2,1)S(1)}, bf16[128,2560]{1,0:T(8,128)(2,1)S(1)}, u32[]{:S(2)}, u32[]{:S(2)}) %collective-permute-start.19) | collective-permute-done | bytes 655392 | tf_op jit(solution)/shard_map/ppermute | solution.py:301
  49.5 12.5 %collective-permute-done.3 = bf16[3,256]{1,0:T(4,128)(2,1)S(1)} collective-permute-done((bf16[3,256]{1,0:T(4,128)(2,1)S(1)}, bf16[3,256]{1,0:T(4,128)(2,1)S(1)}, u32[]{:S(2)}, u32[]{:S(2)}) %collective-permute-start.3) | collective-permute-done | bytes 1568 | tf_op jit(solution)/shard_map/ppermute | solution.py:306
  74.3 3.7 collective-permute-done.5
  81.9 21.5 %collective-permute-done.7 = bf16[256,2048]{1,0:T(8,128)(2,1)S(1)} collective-permute-done((bf16[256,2048]{1,0:T(8,128)(2,1)S(1)}, bf16[256,2048]{1,0:T(8,128)(2,1)S(1)}, u32[]{:S(2)}, u32[]{:S(2)}) %collective-permute-start.7) | collective-permute-done | bytes 1048608 | tf_op jit(solution)/shard_map/ppermute | solution.py:299
  111.6 51.1 %collective-permute-done.10 = bf16[128,2048]{1,0:T(8,128)(2,1)S(1)} collective-permute-done((bf16[128,2048]{1,0:T(8,128)(2,1)S(1)}, bf16[128,2048]{1,0:T(8,128)(2,1)S(1)}, u32[]{:S(2)}, u32[]{:S(2)}) %collective-permute-start.10) | collective-permute-done | bytes 524320 | tf_op jit(solution)/shard_map/ppermute | solution.py:301
  166.4 5.2 convolution_convert_fusion.22
  178.0 3.4 shard_map.311
  189.9 8.6 collective-permute-done.14
  202.0 20.3 %collective-permute-done.15 = bf16[256,2048]{1,0:T(8,128)(2,1)S(1)} collective-permute-done((bf16[256,2048]{1,0:T(8,128)(2,1)S(1)}, bf16[256,2048]{1,0:T(8,128)(2,1)S(1)}, u32[]{:S(2)}, u32[]{:S(2)}) %collective-permute-start.15) | collective-permute-done | bytes 1048608 | tf_op jit(solution)/shard_map/ppermute | solution.py:299
  227.8 19.4 %collective-permute-done.22.refs_2_ = bf16[256,2048]{1,0:T(8,128)(2,1)} collective-permute-done((bf16[256,2048]{1,0:T(8,128)(2,1)S(1)}, bf16[256,2048]{1,0:T(8,128)(2,1)}, u32[]{:S(2)}, u32[]{:S(2)}) %collective-permute-start.22) | collective-permute-done | bytes 1048608 | tf_op jit(solution)/shard_map/ppermute | solution.py:301
  253.5 6.5 collective-permute-done.23
  264.9 3.4 fusion.82
  268.6 6.7 constant_dynamic-update-slice_fusion.11
  292.4 4.3 collective-permute-done.26
  302.1 5.2 fusion.43
  314.6 11.8 %collective-permute-done.28 = bf16[128,2048]{1,0:T(8,128)(2,1)S(1)} collective-permute-done((bf16[128,2048]{1,0:T(8,128)(2,1)S(1)}, bf16[128,2048]{1,0:T(8,128)(2,1)S(1)}, u32[]{:S(2)}, u32[]{:S(2)}) %collective-permute-start.28) | collective-permute-done | bytes 524320 | tf_op jit(solution)/shard_map/ppermute | solution.py:301
  330.3 14.6 %collective-permute-done.29 = bf16[256,2048]{1,0:T(8,128)(2,1)S(1)} collective-permute-done((bf16[256,2048]{1,0:T(8,128)(2,1)S(1)}, bf16[256,2048]{1,0:T(8,128)(2,1)S(1)}, u32[]{:S(2)}, u32[]{:S(2)}) %collective-permute-start.29) | collective-permute-done | bytes 1048608 | tf_op jit(solution)/shard_map/ppermute | solution.py:299
  350.9 20.0 %collective-permute-done.33.refs_2_ = bf16[256,2048]{1,0:T(8,128)(2,1)S(1)} collective-permute-done((bf16[256,2048]{1,0:T(8,128)(2,1)S(1)}, bf16[256,2048]{1,0:T(8,128)(2,1)S(1)}, u32[]{:S(2)}, u32[]{:S(2)}) %collective-permute-start.33) | collective-permute-done | bytes 1048608 | tf_op jit(solution)/shard_map/ppermute | solution.py:301
  374.6 7.9 collective-permute-done.34
  382.6 4.4 collective-permute-done.35
  391.3 18.5 %collective-permute-done.37.refs_6_ = bf16[256,2048]{1,0:T(8,128)(2,1)S(1)} collective-permute-done((bf16[256,2048]{1,0:T(8,128)(2,1)S(1)}, bf16[256,2048]{1,0:T(8,128)(2,1)S(1)}, u32[]{:S(2)}, u32[]{:S(2)}) %collective-permute-start.37) | collective-permute-done | bytes 1048608 | tf_op jit(solution)/shard_map/ppermute | solution.py:301
  413.8 5.4 collective-permute-done.38
  422.2 27.2 %shard_map.314 = (bf16[1024,2048]{1,0:T(8,128)(2,1)}, bf16[1024,2048]{1,0:T(8,128)(2,1)}, bf16[1024,2048]{1,0:T(8,128)(2,1)}, bf16[1024,2048]{1,0:T(8,128)(2,1)}) custom-call(bf16[256,2048]{1,0:T(8,128)(2,1)} %copy-done.84, bf16[256,2048]{1,0:T(8,128)(2,1)} %copy-done.92, bf16[256,2048]{1,0:T(8,128)(2,1)} %copy-done.91, bf16[256,2048]{1,0:T(8,128)(2,1)} %copy-done.95, ...), custom_call_target="tpu_custom_call" | custom-call | tf_op jit(solution)/shard_map/pallas_call | solution.py:89
  449.4 7.2 convolution_convert_fusion.30
  456.7 3.3 convolution_convert_fusion.31
  466.9 11.6 %convolution_convert_fusion.1 = bf16[2048,2048]{1,0:T(8,128)(2,1)} fusion(bf16[1024,2048]{1,0:T(8,128)(2,1)S(1)} %copy-done.136, bf16[1024,2048]{1,0:T(8,128)(2,1)S(1)} %copy-done.139), kind=kOutput, calls=%fused_computation.1 | convolution fusion | flops 8594128896 | bytes 16777216 | tf_op jit(solution)/shard_map/dot_general | solution.py:41
  483.8 14.2 %convolution_convert_fusion = bf16[2048,2048]{1,0:T(8,128)(2,1)} fusion(bf16[1024,2048]{1,0:T(8,128)(2,1)} %get-tuple-element.174, bf16[1024,2048]{1,0:T(8,128)(2,1)} %get-tuple-element.178), kind=kOutput, calls=%fused_computation | convolution fusion | flops 8594128896 | bytes 16777216 | tf_op jit(solution)/shard_map/dot_general | solution.py:41
  505.3 7.5 convolution_convert_fusion.26
  512.8 3.4 convolution_convert_fusion.27
  516.1 3.4 convolution_convert_fusion.28
  519.5 3.4 convolution_convert_fusion.29
  529.6 18.7 %collective-permute-done.45.refs_6_ = bf16[256,2048]{1,0:T(8,128)(2,1)S(1)} collective-permute-done((bf16[256,2048]{1,0:T(8,128)(2,1)S(1)}, bf16[256,2048]{1,0:T(8,128)(2,1)S(1)}, u32[]{:S(2)}, u32[]{:S(2)}) %collective-permute-start.45) | collective-permute-done | bytes 1048608 | tf_op jit(solution)/shard_map/ppermute | solution.py:301
  551.2 6.5 collective-permute-done.46
  560.3 6.2 reduce-scatter.6.cloned.1.call-done.own
  571.1 8.6 collective-permute-done.48
  588.5 7.1 shard_map.316
  595.6 7.7 collective-permute-done.49
  611.1 3.4 convolution_convert_fusion.9
  619.3 6.6 collective-permute-done.52
  627.1 4.9 collective-permute-done.54
  633.3 16.1 %shard_map.322 = bf16[2048,2048]{1,0:T(8,128)(2,1)} custom-call(bf16[256,2048]{1,0:T(8,128)(2,1)} %copy-done.90, bf16[256,2048]{1,0:T(8,128)(2,1)} %collective-permute-done.21.refs_1_, bf16[256,2048]{1,0:T(8,128)(2,1)} %collective-permute-done.22.refs_2_, bf16[256,2048]{1,0:T(8,128)(2,1)} %constant_dynamic-update-slice_fusion.refs_3_, ...), custom_call_target="tpu_custom_call" | custom-call | tf_op jit(solution)/shard_map/pallas_call | solution.py:242
  649.6 7.0 reduce-scatter.8.cloned.1.call-done
  660.1 4.6 fusion.12
  668.5 14.9 %collective-permute-done.53 = bf16[256,2048]{1,0:T(8,128)(2,1)S(1)} collective-permute-done((bf16[256,2048]{1,0:T(8,128)(2,1)}, bf16[256,2048]{1,0:T(8,128)(2,1)S(1)}, u32[]{:S(2)}, u32[]{:S(2)}) %collective-permute-start.53) | collective-permute-done | bytes 1048608 | tf_op jit(solution)/shard_map/ppermute | solution.py:299
  690.9 3.8 collective-permute-done.64
  696.6 10.9 %collective-permute-done.65 = bf16[512,512]{1,0:T(8,128)(2,1)} collective-permute-done((bf16[512,512]{1,0:T(8,128)(2,1)S(1)}, bf16[512,512]{1,0:T(8,128)(2,1)}, u32[]{:S(2)}, u32[]{:S(2)}) %collective-permute-start.65) | collective-permute-done | bytes 524320 | tf_op jit(solution)/shard_map/ppermute | solution.py:301
  711.8 8.6 shard_map.321
  722.4 4.0 collective-permute-done.57.refs_6_
  741.0 9.5 shard_map.317
  751.7 5.5 convolution_convert_fusion.18
  757.2 4.8 convolution_convert_fusion.19
  769.9 6.1 collective-permute-done.60
  786.2 18.0 %shard_map.320 = bf16[2048,2048]{1,0:T(8,128)(2,1)} custom-call(bf16[256,2048]{1,0:T(8,128)(2,1)} %get-tuple-element.305.refs_0_, bf16[256,2048]{1,0:T(8,128)(2,1)} %get-tuple-element.304.refs_1_, bf16[256,2048]{1,0:T(8,128)(2,1)} %get-tuple-element.303.refs_2_, bf16[256,2048]{1,0:T(8,128)(2,1)} %get-tuple-element.302.refs_3_, ...), custom_call_target="tpu_custom_call" | custom-call | tf_op jit(solution)/shard_map/pallas_call | solution.py:242
  805.4 4.1 fusion.32
  809.5 5.3 collective-permute-done.77.refs_1_
  815.0 7.6 collective-permute-done.79.refs_3_
  826.6 3.8 convolution_convert_fusion.2
  835.9 6.4 collective-permute-start.72
  863.6 12.2 %collective-permute-done.84.refs_6_ = bf16[64,2048]{1,0:T(8,128)(2,1)S(1)} collective-permute-done((bf16[64,2048]{1,0:T(8,128)(2,1)S(1)}, bf16[64,2048]{1,0:T(8,128)(2,1)S(1)}, u32[]{:S(2)}, u32[]{:S(2)}) %collective-permute-start.84) | collective-permute-done | bytes 262176 | tf_op jit(solution)/shard_map/ppermute | solution.py:299
  882.7 7.1 collective-permute-done.80.refs_1_
  897.8 25.3 %collective-permute-done.86.refs_1_ = bf16[128,1024]{1,0:T(8,128)(2,1)S(1)} collective-permute-done((bf16[128,1024]{1,0:T(8,128)(2,1)S(1)}, bf16[128,1024]{1,0:T(8,128)(2,1)S(1)}, u32[]{:S(2)}, u32[]{:S(2)}) %collective-permute-start.86) | collective-permute-done | bytes 262176 | tf_op jit(solution)/shard_map/ppermute | solution.py:299
  939.9 3.7 shard_map.326
  950.8 8.9 collective-permute-done.89.refs_1_
  (710 shorter events, 329.3 us)
Async XLA Ops:
  7.2 159.2 %all-gather.5.cloned.1.call-start = ((), (), s32[]{:S(2)}) async-start(), calls=%async_computation.5 | async-start | bytes 9437184 | tf_op jit(solution)/shard_map/all_gather | solution.py:337
  26.1 238.8 %all-gather.7.cloned.1.call-start = ((), (), s32[]{:S(2)}) async-start(), calls=%async_computation.6 | async-start | bytes 14155776 | tf_op jit(solution)/shard_map/all_gather | solution.py:337
  44.9 377.2 %all-gather.11.cloned.1.call-start = ((), (), s32[]{:S(2)}) async-start(), calls=%async_computation.8 | async-start | bytes 9437184 | tf_op jit(solution)/shard_map/all_gather | solution.py:337
  47.4 21.6 %collective-permute-start.6 = (bf16[128,2048]{1,0:T(8,128)(2,1)}, bf16[128,2048]{1,0:T(8,128)(2,1)}, u32[]{:S(2)}, u32[]{:S(2)}) collective-permute-start(bf16[128,2048]{1,0:T(8,128)(2,1)} %get-tuple-element.142), channel_id=1, source_target_pairs={{0,4},{2,6},{4,0},{6,2},{8,12},{10,14},{12,8},{14,10},{16,20},{18,... | collective-permute-start | bytes 1572872 | tf_op jit(solution)/shard_map/ppermute | solution.py:301
  71.5 350.7 %all-gather.9.cloned.1.call-start = ((), (), s32[]{:S(2)}) async-start(), calls=%async_computation.7 | async-start | bytes 9437184 | tf_op jit(solution)/shard_map/all_gather | solution.py:337
  78.1 25.2 %collective-permute-start.7 = (bf16[256,2048]{1,0:T(8,128)(2,1)S(1)}, bf16[256,2048]{1,0:T(8,128)(2,1)S(1)}, u32[]{:S(2)}, u32[]{:S(2)}) collective-permute-start(bf16[256,2048]{1,0:T(8,128)(2,1)S(1)} %get-tuple-element.141), channel_id=1, source_target_pairs={{0,1},{1,0},{2,3},{3,2},{4,5},{5,4},{6,7},{7,6},{8,9},{9,8},{10,11... | collective-permute-start | bytes 3145736 | tf_op jit(solution)/shard_map/ppermute | solution.py:299
  79.7 24.9 %collective-permute-start.8 = (bf16[256,2048]{1,0:T(8,128)(2,1)S(1)}, bf16[256,2048]{1,0:T(8,128)(2,1)S(1)}, u32[]{:S(2)}, u32[]{:S(2)}) collective-permute-start(bf16[256,2048]{1,0:T(8,128)(2,1)S(1)} %get-tuple-element.141), channel_id=1, source_target_pairs={{0,4},{2,6},{4,0},{6,2},{8,12},{10,14},{12,8},{14,10},{16,20},{18,... | collective-permute-start | bytes 3145736 | tf_op jit(solution)/shard_map/ppermute | solution.py:301
  104.5 76.9 %collective-permute-start.11 = (bf16[128,4096]{1,0:T(8,128)(2,1)S(1)}, bf16[128,4096]{1,0:T(8,128)(2,1)}, u32[]{:S(2)}, u32[]{:S(2)}) collective-permute-start(bf16[128,4096]{1,0:T(8,128)(2,1)S(1)} %get-tuple-element.149.refs_0_.refs_4_), channel_id=1, source_target_pairs={{0,1},{1,0},{2,3},{3,2},{4,5},{5,4},{6,7},{7,6},{8,9},{9,8},{10,11... | collective-permute-start | bytes 3145736 | tf_op jit(solution)/shard_map/ppermute | solution.py:299
  105.1 76.3 %collective-permute-start.12 = (bf16[128,4096]{1,0:T(8,128)(2,1)S(1)}, bf16[128,4096]{1,0:T(8,128)(2,1)}, u32[]{:S(2)}, u32[]{:S(2)}) collective-permute-start(bf16[128,4096]{1,0:T(8,128)(2,1)S(1)} %get-tuple-element.149.refs_0_.refs_4_), channel_id=1, source_target_pairs={{0,4},{2,6},{4,0},{6,2},{8,12},{10,14},{12,8},{14,10},{16,20},{18,... | collective-permute-start | bytes 3145736 | tf_op jit(solution)/shard_map/ppermute | solution.py:301
  106.5 74.9 %collective-permute-start.13 = (bf16[128,4096]{1,0:T(8,128)(2,1)S(1)}, bf16[128,4096]{1,0:T(8,128)(2,1)}, u32[]{:S(2)}, u32[]{:S(2)}) collective-permute-start(bf16[128,4096]{1,0:T(8,128)(2,1)S(1)} %get-tuple-element.149.refs_0_.refs_4_), channel_id=1, source_target_pairs={{0,5},{1,4},{2,7},{3,6},{4,1},{5,0},{6,3},{7,2},{8,13},{9,12},{10,... | collective-permute-start | bytes 3145736 | tf_op jit(solution)/shard_map/ppermute | solution.py:303
  108.0 54.6 %collective-permute-start.10 = (bf16[128,2048]{1,0:T(8,128)(2,1)S(1)}, bf16[128,2048]{1,0:T(8,128)(2,1)S(1)}, u32[]{:S(2)}, u32[]{:S(2)}) collective-permute-start(bf16[128,2048]{1,0:T(8,128)(2,1)S(1)} %slice.343), channel_id=1, source_target_pairs={{0,4},{2,6},{4,0},{6,2},{8,12},{10,14},{12,8},{14,10},{16,20},{18,... | collective-permute-start | bytes 1572872 | tf_op jit(solution)/shard_map/ppermute | solution.py:301
  109.6 53.0 %collective-permute-start.9 = (bf16[128,2048]{1,0:T(8,128)(2,1)S(1)}, bf16[128,2048]{1,0:T(8,128)(2,1)S(1)}, u32[]{:S(2)}, u32[]{:S(2)}) collective-permute-start(bf16[128,2048]{1,0:T(8,128)(2,1)S(1)} %slice.342), channel_id=1, source_target_pairs={{0,1},{1,0},{2,3},{3,2},{4,5},{5,4},{6,7},{7,6},{8,9},{9,8},{10,11... | collective-permute-start | bytes 1572872 | tf_op jit(solution)/shard_map/ppermute | solution.py:299
  198.8 23.6 %collective-permute-start.15 = (bf16[256,2048]{1,0:T(8,128)(2,1)S(1)}, bf16[256,2048]{1,0:T(8,128)(2,1)S(1)}, u32[]{:S(2)}, u32[]{:S(2)}) collective-permute-start(bf16[256,2048]{1,0:T(8,128)(2,1)S(1)} %pad_maximum_fusion.2), channel_id=1, source_target_pairs={{0,1},{1,0},{2,3},{3,2},{4,5},{5,4},{6,7},{7,6},{8,9},{9,8},{10,11... | collective-permute-start | bytes 3145736 | tf_op jit(solution)/shard_map/ppermute | solution.py:299
  201.5 20.9 %collective-permute-start.17 = (bf16[256,2048]{1,0:T(8,128)(2,1)S(1)}, bf16[256,2048]{1,0:T(8,128)(2,1)S(1)}, u32[]{:S(2)}, u32[]{:S(2)}) collective-permute-start(bf16[256,2048]{1,0:T(8,128)(2,1)S(1)} %pad_maximum_fusion.3), channel_id=1, source_target_pairs={{0,4},{2,6},{4,0},{6,2},{8,12},{10,14},{12,8},{14,10},{16,20},{18,... | collective-permute-start | bytes 3145736 | tf_op jit(solution)/shard_map/ppermute | solution.py:301
  224.4 22.8 %collective-permute-start.22 = (bf16[256,2048]{1,0:T(8,128)(2,1)S(1)}, bf16[256,2048]{1,0:T(8,128)(2,1)}, u32[]{:S(2)}, u32[]{:S(2)}) collective-permute-start(bf16[256,2048]{1,0:T(8,128)(2,1)S(1)} %multiply_convert_fusion.1.refs_0_), channel_id=1, source_target_pairs={{0,4},{2,6},{4,0},{6,2},{8,12},{10,14},{12,8},{14,10},{16,20},{18,... | collective-permute-start | bytes 3145736 | tf_op jit(solution)/shard_map/ppermute | solution.py:301
  225.9 24.7 %collective-permute-start.21 = (bf16[256,2048]{1,0:T(8,128)(2,1)S(1)}, bf16[256,2048]{1,0:T(8,128)(2,1)}, u32[]{:S(2)}, u32[]{:S(2)}) collective-permute-start(bf16[256,2048]{1,0:T(8,128)(2,1)S(1)} %multiply_convert_fusion.1.refs_0_), channel_id=1, source_target_pairs={{0,1},{1,0},{2,3},{3,2},{4,5},{5,4},{6,7},{7,6},{8,9},{9,8},{10,11... | collective-permute-start | bytes 3145736 | tf_op jit(solution)/shard_map/ppermute | solution.py:299
  226.7 26.1 %collective-permute-start.18 = (s32[2]{0:T(128)S(1)}, s32[2]{0:T(128)S(1)}, u32[]{:S(2)}, u32[]{:S(2)}) collective-permute-start(s32[2]{0:T(128)S(1)} %copy-done.140), channel_id=1, source_target_pairs={{0,4},{2,6},{4,0},{6,2},{8,12},{10,14},{12,8},{14,10},{16,20},{18,... | collective-permute-start | bytes 32 | tf_op jit(solution)/shard_map/ppermute | solution.py:301
  252.9 313.5 %reduce-scatter.6.cloned.1.call-start = ((), (), s32[]{:S(2)}) async-start(), calls=%async_computation.9 | async-start | bytes 9437184 | tf_op jit(solution)/shard_map/reduce_scatter | solution.py:340
  276.1 20.5 %collective-permute-start.26 = (bf16[512,512]{1,0:T(8,128)(2,1)}, bf16[512,512]{1,0:T(8,128)(2,1)}, u32[]{:S(2)}, u32[]{:S(2)}) collective-permute-start(bf16[512,512]{1,0:T(8,128)(2,1)} %get-tuple-element.316), channel_id=1, source_target_pairs={{0,4},{2,6},{4,0},{6,2},{8,12},{10,14},{12,8},{14,10},{16,20},{18,... | collective-permute-start | bytes 1572872 | tf_op jit(solution)/shard_map/ppermute | solution.py:301
  276.3 21.4 %collective-permute-start.27 = (bf16[512,512]{1,0:T(8,128)(2,1)}, bf16[512,512]{1,0:T(8,128)(2,1)}, u32[]{:S(2)}, u32[]{:S(2)}) collective-permute-start(bf16[512,512]{1,0:T(8,128)(2,1)} %get-tuple-element.316), channel_id=1, source_target_pairs={{0,5},{1,4},{2,7},{3,6},{4,1},{5,0},{6,3},{7,2},{8,13},{9,12},{10,... | collective-permute-start | bytes 1572872 | tf_op jit(solution)/shard_map/ppermute | solution.py:303
  326.6 18.3 %collective-permute-start.29 = (bf16[256,2048]{1,0:T(8,128)(2,1)S(1)}, bf16[256,2048]{1,0:T(8,128)(2,1)S(1)}, u32[]{:S(2)}, u32[]{:S(2)}) collective-permute-start(bf16[256,2048]{1,0:T(8,128)(2,1)S(1)} %pad_maximum_fusion.4), channel_id=1, source_target_pairs={{0,1},{1,0},{2,3},{3,2},{4,5},{5,4},{6,7},{7,6},{8,9},{9,8},{10,11... | collective-permute-start | bytes 3145736 | tf_op jit(solution)/shard_map/ppermute | solution.py:299
  347.9 23.0 %collective-permute-start.33 = (bf16[256,2048]{1,0:T(8,128)(2,1)S(1)}, bf16[256,2048]{1,0:T(8,128)(2,1)S(1)}, u32[]{:S(2)}, u32[]{:S(2)}) collective-permute-start(bf16[256,2048]{1,0:T(8,128)(2,1)S(1)} %multiply_convert_fusion.refs_0_), channel_id=1, source_target_pairs={{0,4},{2,6},{4,0},{6,2},{8,12},{10,14},{12,8},{14,10},{16,20},{18,... | collective-permute-start | bytes 3145736 | tf_op jit(solution)/shard_map/ppermute | solution.py:301
  349.5 22.3 %collective-permute-start.32 = (bf16[256,2048]{1,0:T(8,128)(2,1)S(1)}, bf16[256,2048]{1,0:T(8,128)(2,1)S(1)}, u32[]{:S(2)}, u32[]{:S(2)}) collective-permute-start(bf16[256,2048]{1,0:T(8,128)(2,1)S(1)} %multiply_convert_fusion.refs_0_), channel_id=1, source_target_pairs={{0,1},{1,0},{2,3},{3,2},{4,5},{5,4},{6,7},{7,6},{8,9},{9,8},{10,11... | collective-permute-start | bytes 3145736 | tf_op jit(solution)/shard_map/ppermute | solution.py:299
  388.0 21.8 %collective-permute-start.37 = (bf16[256,2048]{1,0:T(8,128)(2,1)S(1)}, bf16[256,2048]{1,0:T(8,128)(2,1)S(1)}, u32[]{:S(2)}, u32[]{:S(2)}) collective-permute-start(bf16[256,2048]{1,0:T(8,128)(2,1)S(1)} %get-tuple-element.170.refs_4_), channel_id=1, source_target_pairs={{0,4},{2,6},{4,0},{6,2},{8,12},{10,14},{12,8},{14,10},{16,20},{18,... | collective-permute-start | bytes 3145736 | tf_op jit(solution)/shard_map/ppermute | solution.py:301
  390.5 20.4 %collective-permute-start.36 = (bf16[256,2048]{1,0:T(8,128)(2,1)S(1)}, bf16[256,2048]{1,0:T(8,128)(2,1)S(1)}, u32[]{:S(2)}, u32[]{:S(2)}) collective-permute-start(bf16[256,2048]{1,0:T(8,128)(2,1)S(1)} %get-tuple-element.170.refs_4_), channel_id=1, source_target_pairs={{0,1},{1,0},{2,3},{3,2},{4,5},{5,4},{6,7},{7,6},{8,9},{9,8},{10,11... | collective-permute-start | bytes 3145736 | tf_op jit(solution)/shard_map/ppermute | solution.py:299
  478.5 178.1 %reduce-scatter.8.cloned.1.call-start = ((), (), s32[]{:S(2)}) async-start(), calls=%async_computation.10 | async-start | bytes 9437184 | tf_op jit(solution)/shard_map/reduce_scatter | solution.py:340
  480.8 19.5 %collective-permute-start.41 = (bf16[128,2048]{1,0:T(8,128)(2,1)}, bf16[128,2048]{1,0:T(8,128)(2,1)}, u32[]{:S(2)}, u32[]{:S(2)}) collective-permute-start(bf16[128,2048]{1,0:T(8,128)(2,1)} %get-tuple-element.285), channel_id=1, source_target_pairs={{0,1},{1,0},{2,3},{3,2},{4,5},{5,4},{6,7},{7,6},{8,9},{9,8},{10,11... | collective-permute-start | bytes 1572872 | tf_op jit(solution)/shard_map/ppermute | solution.py:299
  481.9 20.5 %collective-permute-start.40 = (bf16[128,2048]{1,0:T(8,128)(2,1)}, bf16[128,2048]{1,0:T(8,128)(2,1)}, u32[]{:S(2)}, u32[]{:S(2)}) collective-permute-start(bf16[128,2048]{1,0:T(8,128)(2,1)} %get-tuple-element.286), channel_id=1, source_target_pairs={{0,4},{2,6},{4,0},{6,2},{8,12},{10,14},{12,8},{14,10},{16,20},{18,... | collective-permute-start | bytes 1572872 | tf_op jit(solution)/shard_map/ppermute | solution.py:301
  501.6 21.3 %collective-permute-start.43 = (bf16[256,2048]{1,0:T(8,128)(2,1)S(1)}, bf16[256,2048]{1,0:T(8,128)(2,1)S(1)}, u32[]{:S(2)}, u32[]{:S(2)}) collective-permute-start(bf16[256,2048]{1,0:T(8,128)(2,1)S(1)} %pad_maximum_fusion.8), channel_id=1, source_target_pairs={{0,4},{2,6},{4,0},{6,2},{8,12},{10,14},{12,8},{14,10},{16,20},{18,... | collective-permute-start | bytes 3145736 | tf_op jit(solution)/shard_map/ppermute | solution.py:301
  504.1 18.8 %collective-permute-start.42 = (bf16[256,2048]{1,0:T(8,128)(2,1)S(1)}, bf16[256,2048]{1,0:T(8,128)(2,1)S(1)}, u32[]{:S(2)}, u32[]{:S(2)}) collective-permute-start(bf16[256,2048]{1,0:T(8,128)(2,1)S(1)} %pad_maximum_fusion.7), channel_id=1, source_target_pairs={{0,1},{1,0},{2,3},{3,2},{4,5},{5,4},{6,7},{7,6},{8,9},{9,8},{10,11... | collective-permute-start | bytes 3145736 | tf_op jit(solution)/shard_map/ppermute | solution.py:299
  527.9 20.4 %collective-permute-start.45 = (bf16[256,2048]{1,0:T(8,128)(2,1)S(1)}, bf16[256,2048]{1,0:T(8,128)(2,1)S(1)}, u32[]{:S(2)}, u32[]{:S(2)}) collective-permute-start(bf16[256,2048]{1,0:T(8,128)(2,1)S(1)} %get-tuple-element.259.refs_4_), channel_id=1, source_target_pairs={{0,4},{2,6},{4,0},{6,2},{8,12},{10,14},{12,8},{14,10},{16,20},{18,... | collective-permute-start | bytes 3145736 | tf_op jit(solution)/shard_map/ppermute | solution.py:301
  528.8 20.5 %collective-permute-start.44 = (bf16[256,2048]{1,0:T(8,128)(2,1)S(1)}, bf16[256,2048]{1,0:T(8,128)(2,1)S(1)}, u32[]{:S(2)}, u32[]{:S(2)}) collective-permute-start(bf16[256,2048]{1,0:T(8,128)(2,1)S(1)} %get-tuple-element.259.refs_4_), channel_id=1, source_target_pairs={{0,1},{1,0},{2,3},{3,2},{4,5},{5,4},{6,7},{7,6},{8,9},{9,8},{10,11... | collective-permute-start | bytes 3145736 | tf_op jit(solution)/shard_map/ppermute | solution.py:299
  566.5 185.0 %reduce-scatter.10.cloned.1.call-start = ((), (), s32[]{:S(2)}) async-start(), calls=%async_computation.11 | async-start | bytes 9437184 | tf_op jit(solution)/shard_map/reduce_scatter | solution.py:340
  580.0 23.4 %collective-permute-start.49 = (bf16[256,2048]{1,0:T(8,128)(2,1)S(1)}, bf16[256,2048]{1,0:T(8,128)(2,1)S(1)}, u32[]{:S(2)}, u32[]{:S(2)}) collective-permute-start(bf16[256,2048]{1,0:T(8,128)(2,1)S(1)} %pad_maximum_fusion.9), channel_id=1, source_target_pairs={{0,1},{1,0},{2,3},{3,2},{4,5},{5,4},{6,7},{7,6},{8,9},{9,8},{10,11... | collective-permute-start | bytes 3145736 | tf_op jit(solution)/shard_map/ppermute | solution.py:299
  582.6 20.8 %collective-permute-start.51 = (bf16[256,2048]{1,0:T(8,128)(2,1)S(1)}, bf16[256,2048]{1,0:T(8,128)(2,1)S(1)}, u32[]{:S(2)}, u32[]{:S(2)}) collective-permute-start(bf16[256,2048]{1,0:T(8,128)(2,1)S(1)} %pad_maximum_fusion.10), channel_id=1, source_target_pairs={{0,4},{2,6},{4,0},{6,2},{8,12},{10,14},{12,8},{14,10},{16,20},{18,... | collective-permute-start | bytes 3145736 | tf_op jit(solution)/shard_map/ppermute | solution.py:301
  618.3 31.3 %collective-permute-start.76 = (bf16[256,2048]{1,0:T(8,128)(2,1)S(1)}, bf16[256,2048]{1,0:T(8,128)(2,1)S(1)}, u32[]{:S(2)}, u32[]{:S(2)}) collective-permute-start(bf16[256,2048]{1,0:T(8,128)(2,1)S(1)} %copy-done.20), channel_id=1, source_target_pairs={{0,1},{1,0},{2,3},{3,2},{4,5},{5,4},{6,7},{7,6},{8,9},{9,8},{10,11... | collective-permute-start | bytes 3145736 | tf_op jit(solution)/shard_map/ppermute | solution.py:299
  656.6 166.0 %reduce-scatter.12.cloned.1.call-start = ((), (), s32[]{:S(2)}) async-start(), calls=%async_computation.12 | async-start | bytes 4718592 | tf_op jit(solution)/shard_map/reduce_scatter | solution.py:340
  657.1 26.4 %collective-permute-start.53 = (bf16[256,2048]{1,0:T(8,128)(2,1)}, bf16[256,2048]{1,0:T(8,128)(2,1)S(1)}, u32[]{:S(2)}, u32[]{:S(2)}) collective-permute-start(bf16[256,2048]{1,0:T(8,128)(2,1)} %pad_maximum_fusion.11), channel_id=1, source_target_pairs={{0,1},{1,0},{2,3},{3,2},{4,5},{5,4},{6,7},{7,6},{8,9},{9,8},{10,11... | collective-permute-start | bytes 3145736 | tf_op jit(solution)/shard_map/ppermute | solution.py:299
  658.6 26.3 %collective-permute-start.55 = (bf16[256,2048]{1,0:T(8,128)(2,1)}, bf16[256,2048]{1,0:T(8,128)(2,1)S(1)}, u32[]{:S(2)}, u32[]{:S(2)}) collective-permute-start(bf16[256,2048]{1,0:T(8,128)(2,1)} %pad_maximum_fusion.12), channel_id=1, source_target_pairs={{0,4},{2,6},{4,0},{6,2},{8,12},{10,14},{12,8},{14,10},{16,20},{18,... | collective-permute-start | bytes 3145736 | tf_op jit(solution)/shard_map/ppermute | solution.py:301
  664.9 29.7 %collective-permute-start.64 = (bf16[512,512]{1,0:T(8,128)(2,1)S(1)}, bf16[512,512]{1,0:T(8,128)(2,1)S(1)}, u32[]{:S(2)}, u32[]{:S(2)}) collective-permute-start(bf16[512,512]{1,0:T(8,128)(2,1)S(1)} %get-tuple-element.268), channel_id=1, source_target_pairs={{0,1},{1,0},{2,3},{3,2},{4,5},{5,4},{6,7},{7,6},{8,9},{9,8},{10,11... | collective-permute-start | bytes 1572872 | tf_op jit(solution)/shard_map/ppermute | solution.py:299
  665.6 41.9 %collective-permute-start.65 = (bf16[512,512]{1,0:T(8,128)(2,1)S(1)}, bf16[512,512]{1,0:T(8,128)(2,1)}, u32[]{:S(2)}, u32[]{:S(2)}) collective-permute-start(bf16[512,512]{1,0:T(8,128)(2,1)S(1)} %get-tuple-element.270), channel_id=1, source_target_pairs={{0,4},{2,6},{4,0},{6,2},{8,12},{10,14},{12,8},{14,10},{16,20},{18,... | collective-permute-start | bytes 1572872 | tf_op jit(solution)/shard_map/ppermute | solution.py:301
  666.1 42.5 %collective-permute-start.66 = (bf16[512,512]{1,0:T(8,128)(2,1)S(1)}, bf16[512,512]{1,0:T(8,128)(2,1)}, u32[]{:S(2)}, u32[]{:S(2)}) collective-permute-start(bf16[512,512]{1,0:T(8,128)(2,1)S(1)} %get-tuple-element.269), channel_id=1, source_target_pairs={{0,5},{1,4},{2,7},{3,6},{4,1},{5,0},{6,3},{7,2},{8,13},{9,12},{10,... | collective-permute-start | bytes 1572872 | tf_op jit(solution)/shard_map/ppermute | solution.py:303
  688.9 37.5 %collective-permute-start.57 = (bf16[256,2048]{1,0:T(8,128)(2,1)}, bf16[256,2048]{1,0:T(8,128)(2,1)}, u32[]{:S(2)}, u32[]{:S(2)}) collective-permute-start(bf16[256,2048]{1,0:T(8,128)(2,1)} %get-tuple-element.257.refs_4_), channel_id=1, source_target_pairs={{0,4},{2,6},{4,0},{6,2},{8,12},{10,14},{12,8},{14,10},{16,20},{18,... | collective-permute-start | bytes 3145736 | tf_op jit(solution)/shard_map/ppermute | solution.py:301
  690.4 37.7 %collective-permute-start.56 = (bf16[256,2048]{1,0:T(8,128)(2,1)}, bf16[256,2048]{1,0:T(8,128)(2,1)}, u32[]{:S(2)}, u32[]{:S(2)}) collective-permute-start(bf16[256,2048]{1,0:T(8,128)(2,1)} %get-tuple-element.257.refs_4_), channel_id=1, source_target_pairs={{0,1},{1,0},{2,3},{3,2},{4,5},{5,4},{6,7},{7,6},{8,9},{9,8},{10,11... | collective-permute-start | bytes 3145736 | tf_op jit(solution)/shard_map/ppermute | solution.py:299
  751.5 173.7 %reduce-scatter.14.cloned.1.call-start = ((), (), s32[]{:S(2)}) async-start(), calls=%async_computation.13 | async-start | bytes 9437184 | tf_op jit(solution)/shard_map/reduce_scatter | solution.py:340
  777.3 26.9 %collective-permute-start.61 = (bf16[256,2048]{1,0:T(8,128)(2,1)}, bf16[256,2048]{1,0:T(8,128)(2,1)}, u32[]{:S(2)}, u32[]{:S(2)}) collective-permute-start(bf16[256,2048]{1,0:T(8,128)(2,1)} %pad_maximum_fusion.13), channel_id=1, source_target_pairs={{0,1},{1,0},{2,3},{3,2},{4,5},{5,4},{6,7},{7,6},{8,9},{9,8},{10,11... | collective-permute-start | bytes 3145736 | tf_op jit(solution)/shard_map/ppermute | solution.py:299
  781.6 23.8 %collective-permute-start.63 = (bf16[256,2048]{1,0:T(8,128)(2,1)}, bf16[256,2048]{1,0:T(8,128)(2,1)}, u32[]{:S(2)}, u32[]{:S(2)}) collective-permute-start(bf16[256,2048]{1,0:T(8,128)(2,1)} %pad_maximum_fusion.14), channel_id=1, source_target_pairs={{0,4},{2,6},{4,0},{6,2},{8,12},{10,14},{12,8},{14,10},{16,20},{18,... | collective-permute-start | bytes 3145736 | tf_op jit(solution)/shard_map/ppermute | solution.py:301
  782.5 32.3 %collective-permute-start.77 = (bf16[128,2048]{1,0:T(8,128)(2,1)S(1)}, bf16[128,2048]{1,0:T(8,128)(2,1)S(1)}, u32[]{:S(2)}, u32[]{:S(2)}) collective-permute-start(bf16[128,2048]{1,0:T(8,128)(2,1)S(1)} %get-tuple-element.276.refs_0_), channel_id=1, source_target_pairs={{0,1},{1,0},{2,3},{3,2},{4,5},{5,4},{6,7},{7,6},{8,9},{9,8},{10,11... | collective-permute-start | bytes 1572872 | tf_op jit(solution)/shard_map/ppermute | solution.py:299
  784.0 31.0 %collective-permute-start.78 = (bf16[128,2048]{1,0:T(8,128)(2,1)}, bf16[128,2048]{1,0:T(8,128)(2,1)}, u32[]{:S(2)}, u32[]{:S(2)}) collective-permute-start(bf16[128,2048]{1,0:T(8,128)(2,1)} %get-tuple-element.275), channel_id=1, source_target_pairs={{0,4},{2,6},{4,0},{6,2},{8,12},{10,14},{12,8},{14,10},{16,20},{18,... | collective-permute-start | bytes 1572872 | tf_op jit(solution)/shard_map/ppermute | solution.py:301
  786.1 36.5 %collective-permute-start.79 = (bf16[128,2048]{1,0:T(8,128)(2,1)}, bf16[128,2048]{1,0:T(8,128)(2,1)}, u32[]{:S(2)}, u32[]{:S(2)}) collective-permute-start(bf16[128,2048]{1,0:T(8,128)(2,1)} %get-tuple-element.275), channel_id=1, source_target_pairs={{0,5},{1,4},{2,7},{3,6},{4,1},{5,0},{6,3},{7,2},{8,13},{9,12},{10,... | collective-permute-start | bytes 1572872 | tf_op jit(solution)/shard_map/ppermute | solution.py:303
  856.7 35.8 %collective-permute-start.81 = (bf16[128,1536]{1,0:T(8,128)(2,1)S(1)}, bf16[128,1536]{1,0:T(8,128)(2,1)S(1)}, u32[]{:S(2)}, u32[]{:S(2)}) collective-permute-start(bf16[128,1536]{1,0:T(8,128)(2,1)S(1)} %get-tuple-element.273), channel_id=1, source_target_pairs={{0,4},{2,6},{4,0},{6,2},{8,12},{10,14},{12,8},{14,10},{16,20},{18,... | collective-permute-start | bytes 1179656 | tf_op jit(solution)/shard_map/ppermute | solution.py:301
  858.6 35.0 %collective-permute-start.82 = (bf16[128,1536]{1,0:T(8,128)(2,1)S(1)}, bf16[128,1536]{1,0:T(8,128)(2,1)S(1)}, u32[]{:S(2)}, u32[]{:S(2)}) collective-permute-start(bf16[128,1536]{1,0:T(8,128)(2,1)S(1)} %get-tuple-element.273), channel_id=1, source_target_pairs={{0,5},{1,4},{2,7},{3,6},{4,1},{5,0},{6,3},{7,2},{8,13},{9,12},{10,... | collective-permute-start | bytes 1179656 | tf_op jit(solution)/shard_map/ppermute | solution.py:303
  860.3 20.2 %collective-permute-start.85 = (bf16[64,2048]{1,0:T(8,128)(2,1)S(1)}, bf16[64,2048]{1,0:T(8,128)(2,1)S(1)}, u32[]{:S(2)}, u32[]{:S(2)}) collective-permute-start(bf16[64,2048]{1,0:T(8,128)(2,1)S(1)} %bitcast.204), channel_id=1, source_target_pairs={{0,3},{1,2},{2,1},{3,0},{4,7},{5,6},{6,5},{7,4},{8,11},{9,10},{10,... | collective-permute-start | bytes 786440 | tf_op jit(solution)/shard_map/ppermute | solution.py:852
  861.7 28.2 %collective-permute-start.80 = (bf16[128,1536]{1,0:T(8,128)(2,1)S(1)}, bf16[128,1536]{1,0:T(8,128)(2,1)S(1)}, u32[]{:S(2)}, u32[]{:S(2)}) collective-permute-start(bf16[128,1536]{1,0:T(8,128)(2,1)S(1)} %get-tuple-element.274.refs_0_), channel_id=1, source_target_pairs={{0,1},{1,0},{2,3},{3,2},{4,5},{5,4},{6,7},{7,6},{8,9},{9,8},{10,11... | collective-permute-start | bytes 1179656 | tf_op jit(solution)/shard_map/ppermute | solution.py:299
  876.6 53.5 %collective-permute-start.68 = (bf16[128,4096]{1,0:T(8,128)(2,1)}, bf16[128,4096]{1,0:T(8,128)(2,1)}, u32[]{:S(2)}, u32[]{:S(2)}) collective-permute-start(bf16[128,4096]{1,0:T(8,128)(2,1)} %pad_maximum_fusion.16), channel_id=1, source_target_pairs={{0,1},{1,0},{2,3},{3,2},{4,5},{5,4},{6,7},{7,6},{8,9},{9,8},{10,11... | collective-permute-start | bytes 3145736 | tf_op jit(solution)/shard_map/ppermute | solution.py:299
  881.2 49.5 %collective-permute-start.70 = (bf16[128,4096]{1,0:T(8,128)(2,1)}, bf16[128,4096]{1,0:T(8,128)(2,1)}, u32[]{:S(2)}, u32[]{:S(2)}) collective-permute-start(bf16[128,4096]{1,0:T(8,128)(2,1)} %pad_maximum_fusion.17), channel_id=1, source_target_pairs={{0,4},{2,6},{4,0},{6,2},{8,12},{10,14},{12,8},{14,10},{16,20},{18,... | collective-permute-start | bytes 3145736 | tf_op jit(solution)/shard_map/ppermute | solution.py:301
  890.6 33.2 %collective-permute-start.87 = (bf16[128,1024]{1,0:T(8,128)(2,1)S(1)}, bf16[128,1024]{1,0:T(8,128)(2,1)S(1)}, u32[]{:S(2)}, u32[]{:S(2)}) collective-permute-start(bf16[128,1024]{1,0:T(8,128)(2,1)S(1)} %get-tuple-element.295), channel_id=1, source_target_pairs={{0,4},{2,6},{4,0},{6,2},{8,12},{10,14},{12,8},{14,10},{16,20},{18,... | collective-permute-start | bytes 786440 | tf_op jit(solution)/shard_map/ppermute | solution.py:301
  892.5 32.0 %collective-permute-start.88 = (bf16[128,1024]{1,0:T(8,128)(2,1)S(1)}, bf16[128,1024]{1,0:T(8,128)(2,1)S(1)}, u32[]{:S(2)}, u32[]{:S(2)}) collective-permute-start(bf16[128,1024]{1,0:T(8,128)(2,1)S(1)} %get-tuple-element.295), channel_id=1, source_target_pairs={{0,5},{1,4},{2,7},{3,6},{4,1},{5,0},{6,3},{7,2},{8,13},{9,12},{10,... | collective-permute-start | bytes 786440 | tf_op jit(solution)/shard_map/ppermute | solution.py:303
  894.4 28.7 %collective-permute-start.86 = (bf16[128,1024]{1,0:T(8,128)(2,1)S(1)}, bf16[128,1024]{1,0:T(8,128)(2,1)S(1)}, u32[]{:S(2)}, u32[]{:S(2)}) collective-permute-start(bf16[128,1024]{1,0:T(8,128)(2,1)S(1)} %get-tuple-element.296.refs_0_), channel_id=1, source_target_pairs={{0,1},{1,0},{2,3},{3,2},{4,5},{5,4},{6,7},{7,6},{8,9},{9,8},{10,11... | collective-permute-start | bytes 786440 | tf_op jit(solution)/shard_map/ppermute | solution.py:299
  927.2 32.5 %collective-permute-start.90 = (bf16[128,1536]{1,0:T(8,128)(2,1)S(1)}, bf16[128,1536]{1,0:T(8,128)(2,1)S(1)}, u32[]{:S(2)}, u32[]{:S(2)}) collective-permute-start(bf16[128,1536]{1,0:T(8,128)(2,1)S(1)} %get-tuple-element.271), channel_id=1, source_target_pairs={{0,4},{2,6},{4,0},{6,2},{8,12},{10,14},{12,8},{14,10},{16,20},{18,... | collective-permute-start | bytes 1179656 | tf_op jit(solution)/shard_map/ppermute | solution.py:301
  928.9 30.7 %collective-permute-start.91 = (bf16[128,1536]{1,0:T(8,128)(2,1)S(1)}, bf16[128,1536]{1,0:T(8,128)(2,1)S(1)}, u32[]{:S(2)}, u32[]{:S(2)}) collective-permute-start(bf16[128,1536]{1,0:T(8,128)(2,1)S(1)} %get-tuple-element.271), channel_id=1, source_target_pairs={{0,5},{1,4},{2,7},{3,6},{4,1},{5,0},{6,3},{7,2},{8,13},{9,12},{10,... | collective-permute-start | bytes 1179656 | tf_op jit(solution)/shard_map/ppermute | solution.py:303
  930.1 18.8 %collective-permute-start.93 = (bf16[64,2048]{1,0:T(8,128)(2,1)S(1)}, bf16[64,2048]{1,0:T(8,128)(2,1)S(1)}, u32[]{:S(2)}, u32[]{:S(2)}) collective-permute-start(bf16[64,2048]{1,0:T(8,128)(2,1)S(1)} %bitcast.207), channel_id=1, source_target_pairs={{0,1},{1,0},{2,3},{3,2},{4,5},{5,4},{6,7},{7,6},{8,9},{9,8},{10,11... | collective-permute-start | bytes 786440 | tf_op jit(solution)/shard_map/ppermute | solution.py:299
  930.8 20.1 %collective-permute-start.94 = (bf16[64,2048]{1,0:T(8,128)(2,1)S(1)}, bf16[64,2048]{1,0:T(8,128)(2,1)S(1)}, u32[]{:S(2)}, u32[]{:S(2)}) collective-permute-start(bf16[64,2048]{1,0:T(8,128)(2,1)S(1)} %bitcast.208), channel_id=1, source_target_pairs={{0,3},{1,2},{2,1},{3,0},{4,7},{5,6},{6,5},{7,4},{8,11},{9,10},{10,... | collective-permute-start | bytes 786440 | tf_op jit(solution)/shard_map/ppermute | solution.py:852
  931.4 28.3 %collective-permute-start.89 = (bf16[128,1536]{1,0:T(8,128)(2,1)S(1)}, bf16[128,1536]{1,0:T(8,128)(2,1)S(1)}, u32[]{:S(2)}, u32[]{:S(2)}) collective-permute-start(bf16[128,1536]{1,0:T(8,128)(2,1)S(1)} %get-tuple-element.272.refs_0_), channel_id=1, source_target_pairs={{0,1},{1,0},{2,3},{3,2},{4,5},{5,4},{6,7},{7,6},{8,9},{9,8},{10,11... | collective-permute-start | bytes 1179656 | tf_op jit(solution)/shard_map/ppermute | solution.py:299
  (196 other events, 2741.8 us)
Sparse Core Ops, SparseCore 0:
  26.3 83.8 all-gather.4
  112.4 115.1 all-gather.6
  229.7 80.3 all-gather.10
  312.2 80.5 all-gather.8
  478.6 87.7 reduce-scatter.5
  568.6 87.9 reduce-scatter.7
  658.9 87.9 reduce-scatter.9
  751.6 52.6 reduce-scatter.11
  822.8 95.0 reduce-scatter.13

commit v3 on v2

--- a/solution.py
+++ b/solution.py
@@ -60,45 +60,63 @@
     return result, jnp.sum(grad_normed * unit, axis=tuple(range(values.ndim - 1)))
 
 
-def feed_forward_kernel(*refs):
-    normed_refs, grad_refs = refs[:4], refs[4:8]
-    up, down, active_ref, grad_hidden_ref, normed, out_grad = refs[8:]
-    rows = normed_refs[0].shape[0]
+def join_once(pieces, target):
+    rows = pieces[0].shape[0]
 
     @pl.when(pl.program_id(0) == 0)
     def _():
         for k in range(4):
-            normed[k * rows : (k + 1) * rows, :] = normed_refs[k][...]
-            out_grad[k * rows : (k + 1) * rows, :] = grad_refs[k][...]
-
-    for part in range(2):
-        here = slice(2 * part * rows, 2 * (part + 1) * rows)
+            target[k * rows : (k + 1) * rows, :] = pieces[k][...]
+
+
+def halves(rows):
+    return [slice(part * rows // 2, (part + 1) * rows // 2) for part in range(2)]
+
+
+def forward_kernel(*refs):
+    up, active, slope, normed = refs[4:]
+    join_once(refs[:4], normed)
+    for here in halves(normed.shape[0]):
         hidden = mm(normed[here, :], up[...])
         half = 0.5 * (1.0 + lax.erf(hidden * (0.5**0.5)))
-        active_ref[here, :] = rounded(hidden * half)
+        active[here, :] = rounded(hidden * half)
+        slope[here, :] = half + hidden * (
+            jnp.exp(-0.5 * hidden * hidden) * (0.5 / jnp.pi) ** 0.5
+        )
+
+
+def backward_kernel(*refs):
+    down, slope, grad_hidden, out_grad = refs[4:]
+    join_once(refs[:4], out_grad)
+    for here in halves(out_grad.shape[0]):
         grad_active = rounded(mm_t(out_grad[here, :], down[...])).astype(F32)
-        slope = half + hidden * (jnp.exp(-0.5 * hidden * hidden) * (0.5 / jnp.pi) ** 0.5)
-        grad_hidden_ref[here, :] = rounded(slope * grad_active)
-
-
-def feed_forward(normed, out_grad, up, down, block=256):
-    rows, d_model = normed[0].shape
-    hidden = up.shape[1]
+        grad_hidden[here, :] = rounded(slope[here, :] * grad_active)
+
+
+def hidden_call(kernel, pieces, weight, weight_block, more, dtypes, block=256):
+    rows, d_model = pieces[0].shape
+    hidden = weight.size // d_model
     whole = pl.BlockSpec((rows, d_model), lambda i: (0, 0), pipeline_mode=pl.Buffered(1))
-    result = jax.ShapeDtypeStruct((4 * rows, hidden), BF16)
+    column = pl.BlockSpec((4 * rows, block), lambda i: (0, i))
     return pl.pallas_call(
-        feed_forward_kernel,
+        kernel,
         grid=(hidden // block,),
-        in_specs=[whole] * 8
-        + [
-            pl.BlockSpec((d_model, block), lambda i: (0, i)),
-            pl.BlockSpec((block, d_model), lambda i: (i, 0)),
-        ],
-        out_specs=[pl.BlockSpec((4 * rows, block), lambda i: (0, i))] * 2
-        + [pl.BlockSpec((4 * rows, d_model), lambda i: (0, 0))] * 2,
-        out_shape=[result, result] + [jax.ShapeDtypeStruct((4 * rows, d_model), BF16)] * 2,
+        in_specs=[whole] * 4 + [weight_block] + [column] * len(more),
+        out_specs=[column] * len(dtypes) + [pl.BlockSpec((4 * rows, d_model), lambda i: (0, 0))],
+        out_shape=[jax.ShapeDtypeStruct((4 * rows, hidden), dtype) for dtype in dtypes]
+        + [jax.ShapeDtypeStruct((4 * rows, d_model), BF16)],
         compiler_params=pltpu.CompilerParams(vmem_limit_bytes=56 * 1024 * 1024),
-    )(*normed, *out_grad, up, down)
+    )(*pieces, weight, *more)
+
+
+def ffn_forward(normed, up, block=256):
+    spec = pl.BlockSpec((up.shape[0], block), lambda i: (0, i))
+    return hidden_call(forward_kernel, normed, up, spec, [], [BF16, F32], block)
+
+
+def ffn_backward(out_grad, down, slope, block=256):
+    spec = pl.BlockSpec((block, down.shape[1]), lambda i: (i, 0))
+    return hidden_call(backward_kernel, out_grad, down, spec, [slope], [BF16], block)
 
 
 def soft(queries, keys, usable):
@@ -148,24 +166,28 @@
             put(gpairs, ky, key_at + head, outer(grad_raw, query_rows))
 
 
+def pieces_in(ref):
+    return [ref.at[k] for k in range(4)]
+
+
 def self_kernel(*refs):
-    attend_body(refs[:4], refs[:4], TP_HEADS, 2 * TP_HEADS, None, refs[4:])
+    attend_body(refs[:4], refs[:4], TP_HEADS, 2 * TP_HEADS, None, pieces_in(refs[4]))
 
 
 def self_back_kernel(*refs):
+    target = pieces_in(refs[8])
     attend_back_body(
-        refs[:4], refs[:4], TP_HEADS, 2 * TP_HEADS, None, refs[4:8], refs[8:], refs[8:]
+        refs[:4], refs[:4], TP_HEADS, 2 * TP_HEADS, None, refs[4:8], target, target
     )
 
 
 def cross_kernel(usable, *refs):
-    attend_body(refs[:4], refs[4:8], 0, TP_HEADS, usable, refs[8:])
+    attend_body(refs[:4], refs[4:8], 0, TP_HEADS, usable, pieces_in(refs[8]))
 
 
 def cross_back_kernel(usable, *refs):
-    attend_back_body(
-        refs[:4], refs[4:8], 0, TP_HEADS, usable, refs[8:12], refs[12:16], refs[16:]
-    )
+    targets = [pieces_in(ref) for ref in refs[12:]]
+    attend_back_body(refs[:4], refs[4:8], 0, TP_HEADS, usable, refs[8:12], *targets)
 
 
 def per_image(kernel, usable, pieces, widths):
@@ -174,22 +196,23 @@
     def block(shape):
         return pl.BlockSpec((1,) + tuple(shape[1:]), lambda i: (i, 0, 0))
 
-    shapes = [
-        pieces[like].shape[:2] + (width,) for like, width in widths for _ in range(4)
-    ]
+    shapes = [(4,) + pieces[like].shape[:2] + (width,) for like, width in widths]
     in_specs = [block(piece.shape) for piece in pieces]
     if usable is not None:
         slots = usable.shape[-1]
         in_specs = [pl.BlockSpec((2, 1, 1, slots), lambda i: (0, i, 0, 0))] + in_specs
         pieces = [usable] + list(pieces)
-    return pl.pallas_call(
+    results = pl.pallas_call(
         kernel,
         grid=(images,),
         in_specs=in_specs,
-        out_specs=[block(shape) for shape in shapes],
+        out_specs=[
+            pl.BlockSpec((4, 1) + tuple(shape[2:]), lambda i: (0, i, 0, 0)) for shape in shapes
+        ],
         out_shape=[jax.ShapeDtypeStruct(shape, BF16) for shape in shapes],
         compiler_params=pltpu.CompilerParams(vmem_limit_bytes=48 * 1024 * 1024),
     )(*pieces)
+    return [result.reshape(-1, result.shape[-1]) for result in results]
 
 
 def whole_call(kernel, place, args, shapes, dtype=BF16):
@@ -208,7 +231,7 @@
 
 
 def put_head_rows(target, column, mix, grads):
-    full = outer(joined(mix), joined(grads))
+    full = outer(mix[...], joined(grads))
     half = full.shape[0] // 2
     kept = jnp.where(pl.program_id(0) % 2 == 0, full[:half], full[half:]).astype(BF16)
     for j in range(4):
@@ -216,17 +239,18 @@
 
 
 def self_weights_kernel(*refs):
-    normed, branch, gqkv, mix, target = refs[:4], refs[4:8], refs[8:12], refs[12:16], refs[16]
+    normed, branch = refs[:4], refs[4:8]
+    gqkv, mix, target = refs[8:]
     wide = 3 * TP_WIDTH
-    target[:, :wide] = outer(joined(normed), joined(gqkv)).astype(BF16)
+    target[:, :wide] = outer(joined(normed), gqkv[...]).astype(BF16)
     put_head_rows(target, wide, mix, branch)
 
 
 def cross_weights_kernel(*refs):
-    normed, branch, gquery, mix = refs[:4], refs[4:8], refs[8:12], refs[12:16]
-    feat, gpair, target = refs[16:]
+    normed, branch = refs[:4], refs[4:8]
+    gquery, mix, feat, gpair, target = refs[8:]
     wide = TP_WIDTH
-    target[:, :wide] = outer(joined(normed), joined(gquery)).astype(BF16)
+    target[:, :wide] = outer(joined(normed), gquery[...]).astype(BF16)
     target[:, wide : 3 * wide] = outer(feat[...], gpair[...]).astype(BF16)
     put_head_rows(target, 3 * wide, mix, branch)
 
@@ -261,9 +285,9 @@
     tokens, d_model = normed[0].shape
     rows = d_model // blocks
     specs = [column_block(tokens, rows, lambda i: i)] * 4
-    specs += [whole_block(a) for a in branch + gqkv]
-    specs += [column_block(tokens, HEAD_DIM, lambda i: i // 2)] * 4
-    args = (*normed, *branch, *gqkv, *mix)
+    specs += [whole_block(a) for a in branch + [gqkv]]
+    specs += [column_block(4 * tokens, HEAD_DIM, lambda i: i // 2)]
+    args = (*normed, *branch, gqkv, mix)
     return weight_call(self_weights_kernel, d_model, 4 * TP_WIDTH, args, specs, blocks)
 
 
@@ -271,10 +295,10 @@
     tokens, d_model = normed[0].shape
     rows = d_model // blocks
     specs = [column_block(tokens, rows, lambda i: i)] * 4
-    specs += [whole_block(a) for a in branch + gquery]
-    specs += [column_block(tokens, HEAD_DIM, lambda i: i // 2)] * 4
+    specs += [whole_block(a) for a in branch + [gquery]]
+    specs += [column_block(4 * tokens, HEAD_DIM, lambda i: i // 2)]
     specs += [column_block(feat.shape[0], rows, lambda i: i), whole_block(gpair)]
-    args = (*normed, *branch, *gquery, *mix, feat, gpair)
+    args = (*normed, *branch, gquery, mix, feat, gpair)
     return weight_call(cross_weights_kernel, d_model, 4 * TP_WIDTH, args, specs, blocks)
 
 
@@ -315,11 +339,16 @@
         blocks = values.reshape(lead + (planes, spread, 2, -1))
         return jnp.swapaxes(blocks, -3, -2).reshape(values.shape)
 
-    def gather_tokens(own):
+    def gather_near(own):
+        return swap(own, 0, 1), swap(own, 1, 0)
+
+    def gather_far(own, over_x, over_y):
         half = own.shape[0] // 2
-        over_x, over_y = swap(own, 0, 1), swap(own, 1, 0)
         far = jnp.concatenate([swap(over_y[:half], 0, 1), swap(over_x[half:], 1, 0)], axis=0)
         return [own, over_x, over_y, far]
+
+    def gather_tokens(own):
+        return gather_far(own, *gather_near(own))
 
     def gather_direct(own):
         return [own, swap(own, 0, 1), swap(own, 1, 0), swap(own, 1, 1)]
@@ -327,11 +356,12 @@
     def scatter_tokens(parts):
         here, to_x, to_y, far = lax.optimization_barrier(tuple(parts))
         half = here.shape[0] // 2
-        by_x, by_y = swap(far[:half], 0, 1), swap(far[half:], 1, 0)
+        first = (far[:half], far[half:])
+        by_x, by_y = swap(first[0], 0, 1), swap(first[1], 1, 0)
         to_y = jnp.concatenate([rounded(to_y[:half].astype(F32) + by_x), to_y[half:]], axis=0)
         to_x = jnp.concatenate([to_x[:half], rounded(to_x[half:].astype(F32) + by_y)], axis=0)
         total = here.astype(F32) + swap(to_x, 0, 1).astype(F32)
-        return total + swap(to_y, 1, 0).astype(F32), (to_x, to_y)
+        return total + swap(to_y, 1, 0).astype(F32), first, (to_x, to_y)
 
     def gather_weight(payload):
         return lax.all_gather(payload, "dp", axis=0, tiled=True, axis_index_groups=groups)
@@ -485,6 +515,19 @@
         for yy in range(2):
             for xx in range(2):
                 pl.when((place[0] == yy) & (place[1] == xx))(lambda yy=yy, xx=xx: write(yy, xx))
+
+    def split(place, summed, own, other, *head):
+        rows, columns = own.shape
+        first = pl.multiple_of(place[0] * rows, rows)
+        second = pl.multiple_of((1 - place[0]) * rows, rows)
+        own[...] = summed[pl.ds(first, rows), :columns]
+        other[...] = summed[pl.ds(second, rows), :columns]
+        for target in head:
+            half = target.shape[0]
+            for j in range(4):
+                target[:, j * TP_WIDTH : (j + 1) * TP_WIDTH] = summed[
+                    j * half : (j + 1) * half, columns:
+                ]
 
     def unpack_down(place, own, other, target):
         width = own.shape[0]
@@ -597,7 +640,6 @@
         wide = 3 * TP_WIDTH
         fused = rows % 128 == 0 and half_spread == 1
 
-        gains = gather_small(jnp.stack([norm1_gain, norm2_gain, norm3_gain]), d)
         own, other, kept, passed = whole_call(
             pack_self,
             place,
@@ -613,7 +655,7 @@
         cross_own, cross_other, kept, passed = whole_call(
             pack_cross,
             place,
-            (after(w_cross_query, self_load, gains), w_cross_key, w_cross_value)
+            (after(w_cross_query, self_load), w_cross_key, w_cross_value)
             + (w_cross_out, w_text),
             [(rows, 5 * TP_WIDTH), (rows, 5 * TP_WIDTH), (half, d_model), (half, d_model)],
         )
@@ -649,7 +691,6 @@
             [(own_images * own_tokens, d_model)] * 2
             + [(own_images * own_slots, text_d), (width, d_model)],
         )
-        gains = shuffle(gains.astype(F32))
         cross_other, passed = swap(cross_other, 1, 0), flip(passed, half_spread)
         up_other = swap(up_other, 1, 0)
         image_all = gather_tokens(image_rows)
@@ -657,10 +698,14 @@
             join, place, (cross_own, cross_other, kept, passed), [(2 * rows, 6 * TP_WIDTH)]
         )
         cross_full = gather_weight(cross_load)
+        gains = jnp.stack([norm1_gain, norm2_gain, norm3_gain])
+        gains = gather_small(after(gains, image_all[1], image_all[2]), d)
+        gains = shuffle(gains.astype(F32))
+        up_other = after(up_other, image_all[1], image_all[2])
         (up_load,) = whole_call(join, place, (up_own, up_other), [(2 * rows, up_own.shape[1])])
         up_full = gather_weight(up_load)
         down_full = gather_weight(after(down_load, up_load))
-        caption_all = gather_direct(after(caption_rows, image_all[1], image_all[2]))
+        caption_all = gather_direct(after(caption_rows, *image_all))
         self_full = after(self_full, up_load)
 
         def head_rows(columns):
@@ -689,6 +734,12 @@
         def by_row(pieces):
             return [piece.reshape(-1, piece.shape[-1]) for piece in pieces]
 
+        def all_at_once(multiply, values, weight):
+            return pieces_of(rounded(multiply(values, weight)))
+
+        def pieces_of(values):
+            return list(values.reshape(4, -1, values.shape[-1]))
+
         def each(multiply, pieces, weight):
             return [rounded(multiply(piece, weight)) for piece in pieces]
 
@@ -698,9 +749,9 @@
         stream = image_rows.astype(F32)
         normed1 = [rounded(layer_norm(piece.astype(F32), gains[0])) for piece in image_all]
         qkv = by_image(each(mm, normed1, qkv_full))
-        self_mix = by_row(per_image(self_kernel, None, qkv, [(0, TP_WIDTH)]))
-        self_mix = after_all(self_mix, *caption_all)
-        after_self = stream + scatter_tokens(each(mm, self_mix, out_full))[0]
+        (self_mix,) = per_image(self_kernel, None, qkv, [(0, TP_WIDTH)])
+        self_mix = after(self_mix, *caption_all)
+        after_self = stream + scatter_tokens(all_at_once(mm, self_mix, out_full))[0]
 
         quarter = 2 * y + x
 
@@ -725,25 +776,23 @@
 
         normed2 = gather_tokens(rounded(layer_norm(after_self, gains[1])))
         cquery = by_image(each(mm, normed2, cquery_full))
-        cross_mix = by_row(per_image(cross_kernel, usable, cquery + cpair, [(0, TP_WIDTH)]))
-        after_cross = after_self + scatter_tokens(each(mm, cross_mix, cout_full))[0]
+        (cross_mix,) = per_image(cross_kernel, usable, cquery + cpair, [(0, TP_WIDTH)])
+        after_cross = after_self + scatter_tokens(all_at_once(mm, cross_mix, cout_full))[0]
 
         normed3 = gather_tokens(rounded(layer_norm(after_cross, gains[2])))
-        out_grad_all = gather_tokens(after(out_grad_rows, *normed3))
-        active, grad_hidden, normed3, out_grad_all = feed_forward(
-            normed3, out_grad_all, up_full, down_full
-        )
-
-        def pieces_of(values):
-            return list(values.reshape(4, -1, values.shape[-1]))
-
-        grad_parts = each(mm_t, pieces_of(grad_hidden), up_full)
-        grad_normed3, sent3 = scatter_tokens(grad_parts)
+        out_grad_rows = after(out_grad_rows, *normed3)
+        out_grad_near = gather_near(out_grad_rows)
+        active, slope, normed3 = ffn_forward(normed3, up_full)
+        out_grad_all = gather_far(out_grad_rows, *after_all(out_grad_near, active))
+        grad_hidden, out_grad_all = ffn_backward(out_grad_all, down_full, slope)
+
+        grad_parts = all_at_once(mm_t, grad_hidden, up_full)
+        grad_normed3, _, sent3 = scatter_tokens(grad_parts)
         out_grad_all = after(out_grad_all, *grad_parts)
         grad_down_part = rounded(outer(active, out_grad_all))
         half_down = reduce_weight(grad_down_part)
         grad_up_part = rounded(outer(normed3, after(grad_hidden, grad_down_part)))
-        layer_part = each(mm, pieces_of(after(active, grad_up_part, *sent3)), down_full)
+        layer_part = all_at_once(mm, after(active, grad_up_part, *sent3), down_full)
         grad_normed3 = after(grad_normed3, *layer_part)
         grad_stream, grad_norm3 = norm_back(after_cross, gains[2], grad_normed3)
         grad_after_cross = out_grad_rows.astype(F32) + grad_stream
@@ -757,17 +806,16 @@
             functools.partial(natural, 1), place, (layer_sum,), [layer_sum.shape]
         )
         grad_cross_mix = by_image(each(mm_t, branch2, cout_full))
-        back = per_image(
+        gcquery, gcpair = per_image(
             cross_back_kernel,
             usable,
             cquery + cpair + grad_cross_mix,
             [(0, TP_WIDTH), (4, 2 * TP_WIDTH)],
         )
-        gcquery, gcpair = by_row(back[:4]), all_rows(by_row(back[4:]))
-        gcquery = after_all(gcquery, layer_sum)
-        grad_parts = each(mm_t, gcquery, cquery_full)
-        grad_normed2, sent2 = scatter_tokens(grad_parts)
-        gcquery = list(after(tuple(gcquery), *grad_parts))
+        gcquery = after(gcquery, layer_sum)
+        grad_parts = all_at_once(mm_t, gcquery, cquery_full)
+        grad_normed2, first2, _ = scatter_tokens(grad_parts)
+        gcquery = after(gcquery, *grad_parts)
         grad_stream, grad_norm2 = norm_back(after_self, gains[1], grad_normed2)
         grad_after_self = grad_after_cross + grad_stream
         branch1 = gather_tokens(rounded(grad_after_self))
@@ -792,15 +840,15 @@
 
         if fused:
             grad_cross_part = cross_weights(
-                normed2, branch2, after(caption_feat, *sent2), gcquery, gcpair, cross_mix
+                normed2, branch2, after(caption_feat, *first2), gcquery, gcpair, cross_mix
             )
             grad_text_part = text_weights(caption_all, grad_feat)
         else:
             grad_cross_part = jnp.concatenate(
                 [
-                    rounded(outer(all_rows(normed2), all_rows(gcquery))),
+                    rounded(outer(all_rows(normed2), gcquery)),
                     rounded(outer(caption_feat, gcpair)),
-                    head_blocks(rounded(outer(all_rows(cross_mix), all_rows(branch2)))),
+                    head_blocks(rounded(outer(cross_mix, all_rows(branch2)))),
                 ],
                 axis=1,
             )
@@ -808,68 +856,76 @@
             grad_text_part = jnp.concatenate(
                 [grad_text_part[:d_model], grad_text_part[d_model:]], axis=1
             )
-        cross_sums = reduce_weight(after(grad_cross_part, up_sums, down_pieces[1]))
-        def four(summed, columns):
-            own = lax.dynamic_slice(summed, (y * rows, 0), (rows, columns))
-            other = lax.dynamic_slice(summed, ((1 - y) * rows, 0), (rows, columns))
+        cross_sums = reduce_weight(after(grad_cross_part, up_sums, grad_normed2))
+        def four(summed):
+            shape = (rows, summed.shape[1])
+            own, other = whole_call(split, place, (summed,), [shape, shape])
             return [own, swap(own, 0, 1), swap(other, 1, 0), swap(other, 1, 1)]
 
-        up_pieces = four(up_sums, up_sums.shape[1])
+        up_pieces = four(up_sums)
         grad_self_mix = by_image(each(mm_t, branch1, out_full))
-        gqkv = by_row(per_image(self_back_kernel, None, qkv + grad_self_mix, [(0, wide)]))
-        text_sums = reduce_weight(after(grad_text_part, cross_sums, *gqkv))
-        grad_parts = each(mm_t, gqkv, qkv_full)
-        grad_normed1, sent1 = scatter_tokens(grad_parts)
-        gqkv = after_all(gqkv, *sent1)
+        (gqkv,) = per_image(self_back_kernel, None, qkv + grad_self_mix, [(0, wide)])
+        grad_parts = all_at_once(mm_t, after(gqkv, down_pieces[1]), qkv_full)
+        text_sums = reduce_weight(after(grad_text_part, cross_sums, *grad_parts))
+        grad_normed1, _, sent1 = scatter_tokens(grad_parts)
+        gqkv = after(gqkv, *sent1)
         if fused:
             grad_self_part = self_weights(normed1, branch1, gqkv, self_mix)
         else:
             grad_self_part = jnp.concatenate(
                 [
-                    rounded(outer(all_rows(normed1), all_rows(gqkv))),
-                    head_blocks(rounded(outer(all_rows(self_mix), all_rows(branch1)))),
+                    rounded(outer(all_rows(normed1), gqkv)),
+                    head_blocks(rounded(outer(self_mix, all_rows(branch1)))),
                 ],
                 axis=1,
             )
-        self_sums = reduce_weight(after(grad_self_part, text_sums, grad_normed1, *up_pieces))
+        self_sums = reduce_weight(after(grad_self_part, text_sums, grad_normed1))
         grad_stream, grad_norm1 = norm_back(stream, gains[0], grad_normed1)
         (image_grad,) = whole_call(
             functools.partial(natural, 1), place, (grad_after_self + grad_stream,), [image_rows.shape], F32
         )
 
-        caption_part = each(mm_t, pieces_of(after(grad_feat, grad_normed1)), text_full)
+        caption_part = all_at_once(mm_t, grad_feat, text_full)
+        caption_sum = scatter_tokens(after_all(caption_part, grad_normed1, *up_pieces))[0]
         (caption_grad,) = whole_call(
-            functools.partial(natural, 2), place, (scatter_tokens(caption_part)[0],), [caption_rows_shape], F32
+            functools.partial(natural, 2), place, (caption_sum,), [caption_rows_shape], F32
         )
         caption_grad = caption_grad.reshape(captions.shape)
 
 
-        def head_pieces(columns):
-            own = columns.reshape(4, half, TP_WIDTH).transpose(1, 0, 2).reshape(half, -1)
+        def seven(summed):
+            shape = (rows, wide)
+            own, other, head = whole_call(
+                split, place, (summed,), [shape, shape, (half, d_model)]
+            )
             pairs = [
                 (2 * i + j, 2 * (i ^ half_spread) + 1 - j) for i in range(devices) for j in range(2)
             ]
-            far = lax.ppermute(own, ("dp", "seq"), pairs)
-            return [own, flip(own, half_spread), swap(own, 0, 1), far]
+            pieces = [own, swap(own, 0, 1), swap(other, 1, 0), swap(other, 1, 1)]
+            far = lax.ppermute(head, ("dp", "seq"), pairs)
+            return pieces + [head, flip(head, half_spread), swap(head, 0, 1), far]
 
         (grad_down,) = whole_call(
             unpack_down, place, down_pieces, [(2 * width, d_model)], F32
         )
         (grad_up,) = whole_call(unpack_up, place, up_pieces, [w_up.shape], F32)
-        cross_pieces = four(cross_sums, wide) + head_pieces(cross_sums[:, -TP_WIDTH:])
+        cross_pieces = seven(cross_sums)
         grad_cross_query, grad_cross_key, grad_cross_value, grad_cross_out = whole_call(
             unpack_heads, place, cross_pieces, [w_query.shape] * 4, F32
         )
-        text_pieces = four(text_sums, 2 * TP_WIDTH)
+        text_pieces = four(text_sums)
         (grad_text,) = whole_call(unpack_text, place, text_pieces, [w_text.shape], F32)
-        self_sums = after(self_sums, *down_pieces, *up_pieces, *cross_pieces, *text_pieces)
-        self_pieces = four(self_sums, wide) + head_pieces(self_sums[:, -TP_WIDTH:])
+        norm_sums = jnp.stack([grad_norm1, grad_norm2, grad_norm3])
+        norm_sums = unshuffle(after(norm_sums, *caption_part))
+        norm_sums = reduce_small(norm_sums, d)
+        self_sums = after(
+            self_sums, grad_down, grad_up, grad_cross_query, grad_text, norm_sums, layer_out
+        )
+        self_pieces = seven(self_sums)
         grad_query, grad_key, grad_value, grad_out = whole_call(
             unpack_heads, place, self_pieces, [w_query.shape] * 4, F32
         )
 
-        norm_sums = unshuffle(jnp.stack([grad_norm1, grad_norm2, grad_norm3]))
-        norm_sums = reduce_small(norm_sums, d)
         return (
             layer_out.reshape(images.shape),
             image_grad.reshape(images.shape),

time: 975 us -> 956 us (0.981)
  starting transfers between devices: 120 us -> 92.7 us
  matrix products: 145 us -> 119 us
  local copies, waits for them, and re-layouts: 66.8 us -> 84.6 us
    ppermute x37, waiting for transfers between devices: 184 us -> 137 us  [swap(): return lax.ppermute(values, 'seq', [(0, 1), (1, 0)])]
    ppermute x7, waiting for transfers between devices: 7.66 us -> 35.1 us  [swap(): return lax.ppermute(values, ('dp', 'seq'), pairs)]
    dot_general x25 -> x13, matrix products: 66.7 us -> 46.8 us  [mm_t(): lax.dot_general(left, right, (((1,), (1,)), ((), ())), preferred_element_...]
    reduce_scatter x5, waiting for transfers between devices: 13.1 us -> 29 us  [reduce_weight(): lax.psum_scatter(parts, 'dp', scatter_dimension=0, tiled=True, axis_index...]
    ppermute x37, starting transfers between devices: 51.9 us -> 37.4 us  [swap(): return lax.ppermute(values, 'dp', [(d, d ^ spread) for d in range(devices)])]
    ppermute x37, waiting for transfers between devices: 224 us -> 238 us  [swap(): return lax.ppermute(values, 'dp', [(d, d ^ spread) for d in range(devices)])]
    ppermute x12, waiting for transfers between devices: 23 us -> 9.71 us  [flip(): return lax.ppermute(values, 'dp', [(d, d ^ bit) for d in range(devices)])]
    another operation x0 -> x7, local copies, waits for them, and re-layouts: none -> 10.2 us  [pieces_of(): return list(values.reshape(4, -1, values.shape[-1]))]
  transfers between devices with their start and end apart: 104 -> 104, of which waited for: 61 -> 68; matrix products, arithmetic and copies ran while one was open for 20% -> 21% of each run, Pallas kernels for 10% -> 12%
where the time goes in v3:
time: 956 us; the launch traced here: 949 us
  waiting for transfers between devices  457 us (48%)
  Pallas kernels  132 us (14%)
  matrix products  119 us (12%)
  starting transfers between devices  92.7 us (10%)
  local copies, waits for them, and re-layouts  84.6 us (9%)
  other arithmetic  47.9 us (5%)
  between operations  16.3 us (2%)
    ppermute x37, waiting for transfers between devices, swap(): return lax.ppermute(values, 'dp', [(d, d ^ spread) for d in range(devices)])  238 us
    ppermute x37, waiting for transfers between devices, swap(): return lax.ppermute(values, 'seq', [(0, 1), (1, 0)])  137 us
    dot_general x13, matrix products, mm_t(): lax.dot_general(left, right, (((1,), (1,)), ((), ())), preferred_element_...  46.8 us
    dot_general x13, matrix products, mm(): lax.dot_general(left, right, (((1,), (0,)), ((), ())), preferred_element_...  46.3 us
    pallas_call x3, Pallas kernels, weight_call(): pl.pallas_call(kernel, grid=(blocks,), in_specs=specs, out_specs=pl.Block...  42.5 us
    ppermute x37, starting transfers between devices, swap(): return lax.ppermute(values, 'dp', [(d, d ^ spread) for d in range(devices)])  37.4 us
    ppermute x37, starting transfers between devices, swap(): return lax.ppermute(values, 'seq', [(0, 1), (1, 0)])  36.8 us
    ppermute x7, waiting for transfers between devices, swap(): return lax.ppermute(values, ('dp', 'seq'), pairs)  35.1 us
  transfers between devices with their start and end apart: 104, of which 68 were waited for; matrix products, arithmetic and copies ran while one was open for 21% of the time, Pallas kernels for 12%

profile of v3, /device:TPU:0, one launch (start us, length us, event | category | flops | bytes accessed | tf_op | source)
XLA Modules:
  0.0 949.3 jit_solution(7697857673674042334)
XLA Ops:
  17.0 7.6 collective-permute-done.other
  30.5 12.6 %collective-permute-done.19.other = bf16[128,2560]{1,0:T(8,128)(2,1)S(1)} collective-permute-done((bf16[128,2560]{1,0:T(8,128)(2,1)S(1)}, bf16[128,2560]{1,0:T(8,128)(2,1)S(1)}, u32[]{:S(2)}, u32[]{:S(2)}) %collective-permute-start.19) | collective-permute-done | bytes 655392 | tf_op jit(solution)/shard_map/ppermute | solution.py:325
  48.5 4.0 shard_map.309
  56.8 22.0 %collective-permute-done.3 = bf16[256,2048]{1,0:T(8,128)(2,1)} collective-permute-done((bf16[256,2048]{1,0:T(8,128)(2,1)S(1)}, bf16[256,2048]{1,0:T(8,128)(2,1)}, u32[]{:S(2)}, u32[]{:S(2)}) %collective-permute-start.3) | collective-permute-done | bytes 1048608 | tf_op jit(solution)/shard_map/ppermute | solution.py:325
  82.0 5.3 collective-permute-done.8.other
  109.1 9.2 collective-permute-done.10
  123.6 4.0 fusion.57
  127.6 5.1 fusion.33
  138.9 3.4 shard_map.311
  142.4 4.2 collective-permute-done.13.refs_3_.refs_7_
  146.5 19.2 %collective-permute-done.12.refs_2_.refs_6_ = bf16[128,4096]{1,0:T(8,128)(2,1)} collective-permute-done((bf16[128,4096]{1,0:T(8,128)(2,1)S(1)}, bf16[128,4096]{1,0:T(8,128)(2,1)}, u32[]{:S(2)}, u32[]{:S(2)}) %collective-permute-start.12) | collective-permute-done | bytes 1048608 | tf_op jit(solution)/shard_map/ppermute | solution.py:325
  175.0 11.4 %collective-permute-done.16 = bf16[128,2048]{1,0:T(8,128)(2,1)S(1)} collective-permute-done((bf16[128,2048]{1,0:T(8,128)(2,1)S(1)}, bf16[128,2048]{1,0:T(8,128)(2,1)S(1)}, u32[]{:S(2)}, u32[]{:S(2)}) %collective-permute-start.16) | collective-permute-done | bytes 524320 | tf_op jit(solution)/shard_map/ppermute | solution.py:323
  188.8 22.0 %collective-permute-done.17 = bf16[256,2048]{1,0:T(8,128)(2,1)S(1)} collective-permute-done((bf16[256,2048]{1,0:T(8,128)(2,1)S(1)}, bf16[256,2048]{1,0:T(8,128)(2,1)S(1)}, u32[]{:S(2)}, u32[]{:S(2)}) %collective-permute-start.17) | collective-permute-done | bytes 1048608 | tf_op jit(solution)/shard_map/ppermute | solution.py:325
  217.0 21.0 %collective-permute-done.22.refs_2_ = bf16[256,2048]{1,0:T(8,128)(2,1)} collective-permute-done((bf16[256,2048]{1,0:T(8,128)(2,1)S(1)}, bf16[256,2048]{1,0:T(8,128)(2,1)}, u32[]{:S(2)}, u32[]{:S(2)}) %collective-permute-start.22) | collective-permute-done | bytes 1048608 | tf_op jit(solution)/shard_map/ppermute | solution.py:325
  244.2 7.1 collective-permute-done.23
  259.0 6.7 constant_dynamic-update-slice_fusion.13
  294.2 4.6 fusion.64
  308.3 8.3 collective-permute-done.30
  318.1 3.9 collective-permute-done.28
  322.3 17.3 %collective-permute-done.31 = bf16[256,2048]{1,0:T(8,128)(2,1)S(1)} collective-permute-done((bf16[256,2048]{1,0:T(8,128)(2,1)S(1)}, bf16[256,2048]{1,0:T(8,128)(2,1)S(1)}, u32[]{:S(2)}, u32[]{:S(2)}) %collective-permute-start.31) | collective-permute-done | bytes 1048608 | tf_op jit(solution)/shard_map/ppermute | solution.py:325
  342.8 20.9 %collective-permute-done.33.refs_2_ = bf16[256,2048]{1,0:T(8,128)(2,1)S(1)} collective-permute-done((bf16[256,2048]{1,0:T(8,128)(2,1)S(1)}, bf16[256,2048]{1,0:T(8,128)(2,1)S(1)}, u32[]{:S(2)}, u32[]{:S(2)}) %collective-permute-start.33) | collective-permute-done | bytes 1048608 | tf_op jit(solution)/shard_map/ppermute | solution.py:325
  366.3 8.3 collective-permute-done.34
  374.7 3.9 collective-permute-done.35
  379.9 17.6 %shard_map.314 = (bf16[1024,2048]{1,0:T(8,128)(2,1)}, f32[1024,2048]{1,0:T(8,128)}, bf16[1024,2048]{1,0:T(8,128)(2,1)}) custom-call(bf16[256,2048]{1,0:T(8,128)(2,1)} %copy-done.61, bf16[256,2048]{1,0:T(8,128)(2,1)} %copy-done.79, bf16[256,2048]{1,0:T(8,128)(2,1)} %copy-done.77, bf16[256,2048]{1,0:T(8,128)(2,1)} %copy-done.80, ...), custom_call_target="tpu_custom_call" | custom-call | tf_op jit(solution)/shard_map/pallas_call | solution.py:101
  401.9 8.6 collective-permute-done.38
  411.7 15.9 %shard_map.315 = (bf16[1024,2048]{1,0:T(8,128)(2,1)}, bf16[1024,2048]{1,0:T(8,128)(2,1)}) custom-call(bf16[256,2048]{1,0:T(8,128)(2,1)} %copy-done.3, bf16[256,2048]{1,0:T(8,128)(2,1)} %collective-permute-done.36.refs_1_, bf16[256,2048]{1,0:T(8,128)(2,1)} %copy-done.78, bf16[256,2048]{1,0:T(8,128)(2,1)} %pad_maximum_fusion.9.refs_3_, ...), custom_call_target="tpu_custom_call" | custom-call | tf_op jit(solution)/shard_map/pallas_call | solution.py:101
  427.7 12.7 %convolution_convert_fusion.6 = bf16[1024,2048]{1,0:T(8,128)(2,1)S(1)} fusion(bf16[1024,2048]{1,0:T(8,128)(2,1)} %get-tuple-element.162, bf16[2048,2048]{1,0:T(8,128)(2,1)} %all-gather.9.cloned.1.call-done.refs_4_), kind=kOutput, calls=%fused_computation.15 | convolution fusion | flops 8592031744 | bytes 16777216 | tf_op jit(solution)/shard_map/dot_general | solution.py:37
  444.6 11.3 %convolution_convert_fusion.1 = bf16[2048,2048]{1,0:T(8,128)(2,1)} fusion(bf16[1024,2048]{1,0:T(8,128)(2,1)S(1)} %copy-done.110, bf16[1024,2048]{1,0:T(8,128)(2,1)S(1)} %copy-done.112), kind=kOutput, calls=%fused_computation.1 | convolution fusion | flops 8594128896 | bytes 16777216 | tf_op jit(solution)/shard_map/dot_general | solution.py:41
  460.3 14.2 %convolution_convert_fusion = bf16[2048,2048]{1,0:T(8,128)(2,1)} fusion(bf16[1024,2048]{1,0:T(8,128)(2,1)} %get-tuple-element.151, bf16[1024,2048]{1,0:T(8,128)(2,1)} %get-tuple-element.162), kind=kOutput, calls=%fused_computation | convolution fusion | flops 8594128896 | bytes 16777216 | tf_op jit(solution)/shard_map/dot_general | solution.py:41
  480.9 11.3 %convolution_convert_fusion.5 = bf16[1024,2048]{1,0:T(8,128)(2,1)S(1)} fusion(bf16[1024,2048]{1,0:T(8,128)(2,1)S(1)} %copy-done.111, bf16[2048,2048]{1,0:T(8,128)(2,1)} %all-gather.11.cloned.1.call-done.refs_4_), kind=kOutput, calls=%fused_computation.14 | convolution fusion | flops 8592031744 | bytes 16777216 | tf_op jit(solution)/shard_map/dot_general | solution.py:33
  493.9 4.6 collective-permute-done.43
  506.0 17.8 %collective-permute-done.45.refs_6_ = bf16[256,2048]{1,0:T(8,128)(2,1)S(1)} collective-permute-done((bf16[256,2048]{1,0:T(8,128)(2,1)S(1)}, bf16[256,2048]{1,0:T(8,128)(2,1)S(1)}, u32[]{:S(2)}, u32[]{:S(2)}) %collective-permute-start.45) | collective-permute-done | bytes 1048608 | tf_op jit(solution)/shard_map/ppermute | solution.py:325
  527.3 5.8 collective-permute-done.46
  535.8 11.1 %reduce-scatter.6.cloned.1.call-done.own = bf16[256,2048]{1,0:T(8,128)(2,1)} async-done(((bf16[2048,2048]{1,0:T(8,128)(2,1)}), bf16[256,2048]{1,0:T(8,128)(2,1)}) %reduce-scatter.6.cloned.1.call-update) | async-done | bytes 1048592 | tf_op jit(solution)/shard_map/reduce_scatter | solution.py:370
  552.0 8.4 collective-permute-done.50
  568.9 7.1 shard_map.317
  576.1 8.1 collective-permute-done.51
  584.8 4.0 convolution_convert_fusion.4
  592.7 9.3 collective-permute-done.54
  606.3 16.2 %shard_map.324 = bf16[2048,2048]{1,0:T(8,128)(2,1)} custom-call(bf16[256,2048]{1,0:T(8,128)(2,1)} %copy-done.75, bf16[256,2048]{1,0:T(8,128)(2,1)} %collective-permute-done.21.refs_1_, bf16[256,2048]{1,0:T(8,128)(2,1)} %collective-permute-done.22.refs_2_, bf16[256,2048]{1,0:T(8,128)(2,1)} %constant_dynamic-update-slice_fusion.2.refs_3_, ...), custom_call_target="tpu_custom_call" | custom-call | tf_op jit(solution)/shard_map/pallas_call | solution.py:266
  627.8 4.1 multiply_reduce_fusion.1
  632.0 5.1 reduce-scatter.8.cloned.1.call-done.summed
  638.3 4.7 fusion.21
  652.8 6.2 collective-permute-done.65
  661.7 9.6 %collective-permute-done.67 = bf16[512,512]{1,0:T(8,128)(2,1)} collective-permute-done((bf16[512,512]{1,0:T(8,128)(2,1)}, bf16[512,512]{1,0:T(8,128)(2,1)}, u32[]{:S(2)}, u32[]{:S(2)}) %collective-permute-start.67) | collective-permute-done | bytes 524320 | tf_op jit(solution)/shard_map/ppermute | solution.py:327
  678.0 8.5 shard_map.323
  700.7 6.3 collective-permute-done.58
  709.9 9.5 %shard_map.318 = bf16[4,2,128,1536]{3,2,1,0:T(8,128)(2,1)} custom-call(bf16[2,128,1536]{2,1,0:T(8,128)(2,1)S(1)} %bitcast.128, bf16[2,128,1536]{2,1,0:T(8,128)(2,1)S(1)} %bitcast.126, bf16[2,128,1536]{2,1,0:T(8,128)(2,1)S(1)} %bitcast.124, bf16[2,128,1536]{2,1,0:T(8,128)(2,1)S(1)} %bitcast.122, bf16[2,128,512]{2,1,0:T(8,128)(2,1)S(1)} %bitcast.150, ...), custom_call_target="tpu_custom_call" | custom-call | tf_op jit(solution)/shard_map/pallas_call | solution.py:205
  719.4 5.3 collective-permute-done.60.other
  724.8 8.7 convolution_convert_fusion.3
  738.9 7.2 collective-permute-done.63
  751.6 17.8 %shard_map.322 = bf16[2048,2048]{1,0:T(8,128)(2,1)} custom-call(bf16[256,2048]{1,0:T(8,128)(2,1)} %get-tuple-element.306.refs_0_, bf16[256,2048]{1,0:T(8,128)(2,1)} %get-tuple-element.305.refs_1_, bf16[256,2048]{1,0:T(8,128)(2,1)} %get-tuple-element.304.refs_2_, bf16[256,2048]{1,0:T(8,128)(2,1)} %get-tuple-element.303.refs_3_, bf16[256,2048]{1,0:T(8,128)(2,1)} %copy-done.60, ...), custom_call_target="tpu_custom_call" | custom-call | tf_op jit(solution)/shard_map/pallas_call | solution.py:266
  770.2 4.2 fusion.53
  774.3 12.7 %reduce-scatter.12.cloned.1.call-done.summed = bf16[256,1024]{1,0:T(8,128)(2,1)} async-done(((bf16[2048,1024]{1,0:T(8,128)(2,1)}), bf16[256,1024]{1,0:T(8,128)(2,1)}) %reduce-scatter.12.cloned.1.call-update) | async-done | bytes 524304 | tf_op jit(solution)/shard_map/reduce_scatter | solution.py:370
  787.1 4.8 convolution_convert_fusion.2
  809.2 11.4 %collective-permute-done.70.refs_3_ = bf16[128,2048]{1,0:T(8,128)(2,1)S(1)} collective-permute-done((bf16[128,2048]{1,0:T(8,128)(2,1)S(1)}, bf16[128,2048]{1,0:T(8,128)(2,1)S(1)}, u32[]{:S(2)}, u32[]{:S(2)}) %collective-permute-start.70) | collective-permute-done | bytes 524320 | tf_op jit(solution)/shard_map/ppermute | solution.py:327
  820.7 8.9 collective-permute-done.69.refs_2_
  832.3 11.3 %collective-permute-done.71 = bf16[64,4096]{1,0:T(8,128)(2,1)S(1)} collective-permute-done((bf16[64,4096]{1,0:T(8,128)(2,1)S(1)}, bf16[64,4096]{1,0:T(8,128)(2,1)S(1)}, u32[]{:S(2)}, u32[]{:S(2)}) %collective-permute-start.71) | collective-permute-done | bytes 524320 | tf_op jit(solution)/shard_map/ppermute | solution.py:325
  855.8 4.9 collective-permute-done.84.refs_6_
  863.1 6.0 collective-permute-done.80.refs_1_
  871.2 6.6 collective-permute-done.82.refs_3_
  900.6 7.9 collective-permute-done.74
  912.0 4.9 collective-permute-done.94.refs_7_
  922.5 16.8 %collective-permute-done.89.refs_1_ = bf16[128,1536]{1,0:T(8,128)(2,1)S(1)} collective-permute-done((bf16[128,1536]{1,0:T(8,128)(2,1)S(1)}, bf16[128,1536]{1,0:T(8,128)(2,1)S(1)}, u32[]{:S(2)}, u32[]{:S(2)}) %collective-permute-start.89) | collective-permute-done | bytes 393248 | tf_op jit(solution)/shard_map/ppermute | solution.py:323
  (629 shorter events, 323.4 us)
Async XLA Ops:
  7.2 120.4 %all-gather.5.cloned.1.call-start = ((), (), s32[]{:S(2)}) async-start(), calls=%async_computation.5 | async-start | bytes 9437184 | tf_op jit(solution)/shard_map/all_gather | solution.py:367
  26.1 229.2 %all-gather.7.cloned.1.call-start = ((), (), s32[]{:S(2)}) async-start(), calls=%async_computation.6 | async-start | bytes 14155776 | tf_op jit(solution)/shard_map/all_gather | solution.py:367
  27.1 16.0 %collective-permute-start.19 = (bf16[128,2560]{1,0:T(8,128)(2,1)S(1)}, bf16[128,2560]{1,0:T(8,128)(2,1)S(1)}, u32[]{:S(2)}, u32[]{:S(2)}) collective-permute-start(bf16[128,2560]{1,0:T(8,128)(2,1)S(1)} %get-tuple-element.144), channel_id=1, source_target_pairs={{0,4},{2,6},{4,0},{6,2},{8,12},{10,14},{12,8},{14,10},{16,20},{18,... | collective-permute-start | bytes 1966088 | tf_op jit(solution)/shard_map/ppermute | solution.py:325
  44.9 335.0 %all-gather.9.cloned.1.call-start = ((), (), s32[]{:S(2)}) async-start(), calls=%async_computation.7 | async-start | bytes 9437184 | tf_op jit(solution)/shard_map/all_gather | solution.py:367
  52.5 26.3 %collective-permute-start.3 = (bf16[256,2048]{1,0:T(8,128)(2,1)S(1)}, bf16[256,2048]{1,0:T(8,128)(2,1)}, u32[]{:S(2)}, u32[]{:S(2)}) collective-permute-start(bf16[256,2048]{1,0:T(8,128)(2,1)S(1)} %get-tuple-element.131), channel_id=1, source_target_pairs={{0,4},{2,6},{4,0},{6,2},{8,12},{10,14},{12,8},{14,10},{16,20},{18,... | collective-permute-start | bytes 3145736 | tf_op jit(solution)/shard_map/ppermute | solution.py:325
  54.0 33.4 %collective-permute-start.2 = (bf16[256,2048]{1,0:T(8,128)(2,1)S(1)}, bf16[256,2048]{1,0:T(8,128)(2,1)}, u32[]{:S(2)}, u32[]{:S(2)}) collective-permute-start(bf16[256,2048]{1,0:T(8,128)(2,1)S(1)} %get-tuple-element.131), channel_id=1, source_target_pairs={{0,1},{1,0},{2,3},{3,2},{4,5},{5,4},{6,7},{7,6},{8,9},{9,8},{10,11... | collective-permute-start | bytes 3145736 | tf_op jit(solution)/shard_map/ppermute | solution.py:323
  55.5 31.9 %collective-permute-start.8 = (bf16[128,2048]{1,0:T(8,128)(2,1)}, bf16[128,2048]{1,0:T(8,128)(2,1)S(1)}, u32[]{:S(2)}, u32[]{:S(2)}) collective-permute-start(bf16[128,2048]{1,0:T(8,128)(2,1)} %copy-done.47), channel_id=1, source_target_pairs={{0,4},{2,6},{4,0},{6,2},{8,12},{10,14},{12,8},{14,10},{16,20},{18,... | collective-permute-start | bytes 1572872 | tf_op jit(solution)/shard_map/ppermute | solution.py:325
  80.6 27.3 %collective-permute-start.9 = (bf16[128,2048]{1,0:T(8,128)(2,1)}, bf16[128,2048]{1,0:T(8,128)(2,1)}, u32[]{:S(2)}, u32[]{:S(2)}) collective-permute-start(bf16[128,2048]{1,0:T(8,128)(2,1)} %slice.350), channel_id=1, source_target_pairs={{0,1},{1,0},{2,3},{3,2},{4,5},{5,4},{6,7},{7,6},{8,9},{9,8},{10,11... | collective-permute-start | bytes 1572872 | tf_op jit(solution)/shard_map/ppermute | solution.py:323
  90.4 321.3 %all-gather.11.cloned.1.call-start = ((), (), s32[]{:S(2)}) async-start(), calls=%async_computation.8 | async-start | bytes 9437184 | tf_op jit(solution)/shard_map/all_gather | solution.py:367
  119.4 27.2 %collective-permute-start.13 = (bf16[128,4096]{1,0:T(8,128)(2,1)S(1)}, bf16[128,4096]{1,0:T(8,128)(2,1)}, u32[]{:S(2)}, u32[]{:S(2)}) collective-permute-start(bf16[128,4096]{1,0:T(8,128)(2,1)S(1)} %get-tuple-element.137.refs_0_.refs_4_), channel_id=1, source_target_pairs={{0,5},{1,4},{2,7},{3,6},{4,1},{5,0},{6,3},{7,2},{8,13},{9,12},{10,... | collective-permute-start | bytes 3145736 | tf_op jit(solution)/shard_map/ppermute | solution.py:327
  121.9 43.8 %collective-permute-start.12 = (bf16[128,4096]{1,0:T(8,128)(2,1)S(1)}, bf16[128,4096]{1,0:T(8,128)(2,1)}, u32[]{:S(2)}, u32[]{:S(2)}) collective-permute-start(bf16[128,4096]{1,0:T(8,128)(2,1)S(1)} %get-tuple-element.137.refs_0_.refs_4_), channel_id=1, source_target_pairs={{0,4},{2,6},{4,0},{6,2},{8,12},{10,14},{12,8},{14,10},{16,20},{18,... | collective-permute-start | bytes 3145736 | tf_op jit(solution)/shard_map/ppermute | solution.py:325
  122.4 43.5 %collective-permute-start.11 = (bf16[128,4096]{1,0:T(8,128)(2,1)S(1)}, bf16[128,4096]{1,0:T(8,128)(2,1)}, u32[]{:S(2)}, u32[]{:S(2)}) collective-permute-start(bf16[128,4096]{1,0:T(8,128)(2,1)S(1)} %get-tuple-element.137.refs_0_.refs_4_), channel_id=1, source_target_pairs={{0,1},{1,0},{2,3},{3,2},{4,5},{5,4},{6,7},{7,6},{8,9},{9,8},{10,11... | collective-permute-start | bytes 3145736 | tf_op jit(solution)/shard_map/ppermute | solution.py:323
  186.6 24.2 %collective-permute-start.17 = (bf16[256,2048]{1,0:T(8,128)(2,1)S(1)}, bf16[256,2048]{1,0:T(8,128)(2,1)S(1)}, u32[]{:S(2)}, u32[]{:S(2)}) collective-permute-start(bf16[256,2048]{1,0:T(8,128)(2,1)S(1)} %pad_maximum_fusion.6), channel_id=1, source_target_pairs={{0,4},{2,6},{4,0},{6,2},{8,12},{10,14},{12,8},{14,10},{16,20},{18,... | collective-permute-start | bytes 3145736 | tf_op jit(solution)/shard_map/ppermute | solution.py:325
  188.5 24.1 %collective-permute-start.15 = (bf16[256,2048]{1,0:T(8,128)(2,1)S(1)}, bf16[256,2048]{1,0:T(8,128)(2,1)S(1)}, u32[]{:S(2)}, u32[]{:S(2)}) collective-permute-start(bf16[256,2048]{1,0:T(8,128)(2,1)S(1)} %pad_maximum_fusion.5), channel_id=1, source_target_pairs={{0,1},{1,0},{2,3},{3,2},{4,5},{5,4},{6,7},{7,6},{8,9},{9,8},{10,11... | collective-permute-start | bytes 3145736 | tf_op jit(solution)/shard_map/ppermute | solution.py:323
  214.7 23.4 %collective-permute-start.22 = (bf16[256,2048]{1,0:T(8,128)(2,1)S(1)}, bf16[256,2048]{1,0:T(8,128)(2,1)}, u32[]{:S(2)}, u32[]{:S(2)}) collective-permute-start(bf16[256,2048]{1,0:T(8,128)(2,1)S(1)} %multiply_convert_fusion.1.refs_0_), channel_id=1, source_target_pairs={{0,4},{2,6},{4,0},{6,2},{8,12},{10,14},{12,8},{14,10},{16,20},{18,... | collective-permute-start | bytes 3145736 | tf_op jit(solution)/shard_map/ppermute | solution.py:325
  215.0 25.3 %collective-permute-start.21 = (bf16[256,2048]{1,0:T(8,128)(2,1)S(1)}, bf16[256,2048]{1,0:T(8,128)(2,1)}, u32[]{:S(2)}, u32[]{:S(2)}) collective-permute-start(bf16[256,2048]{1,0:T(8,128)(2,1)S(1)} %multiply_convert_fusion.1.refs_0_), channel_id=1, source_target_pairs={{0,1},{1,0},{2,3},{3,2},{4,5},{5,4},{6,7},{7,6},{8,9},{9,8},{10,11... | collective-permute-start | bytes 3145736 | tf_op jit(solution)/shard_map/ppermute | solution.py:323
  216.6 27.1 %collective-permute-start.18 = (s32[2]{0:T(128)S(1)}, s32[2]{0:T(128)S(1)}, u32[]{:S(2)}, u32[]{:S(2)}) collective-permute-start(s32[2]{0:T(128)S(1)} %copy-done.113), channel_id=1, source_target_pairs={{0,4},{2,6},{4,0},{6,2},{8,12},{10,14},{12,8},{14,10},{16,20},{18,... | collective-permute-start | bytes 32 | tf_op jit(solution)/shard_map/ppermute | solution.py:325
  243.9 303.1 %reduce-scatter.6.cloned.1.call-start = ((), (), s32[]{:S(2)}) async-start(), calls=%async_computation.9 | async-start | bytes 9437184 | tf_op jit(solution)/shard_map/reduce_scatter | solution.py:370
  267.1 16.5 %collective-permute-start.25 = (bf16[512,512]{1,0:T(8,128)(2,1)}, bf16[512,512]{1,0:T(8,128)(2,1)}, u32[]{:S(2)}, u32[]{:S(2)}) collective-permute-start(bf16[512,512]{1,0:T(8,128)(2,1)} %get-tuple-element.317), channel_id=1, source_target_pairs={{0,1},{1,0},{2,3},{3,2},{4,5},{5,4},{6,7},{7,6},{8,9},{9,8},{10,11... | collective-permute-start | bytes 1572872 | tf_op jit(solution)/shard_map/ppermute | solution.py:323
  267.8 20.9 %collective-permute-start.27 = (bf16[512,512]{1,0:T(8,128)(2,1)}, bf16[512,512]{1,0:T(8,128)(2,1)}, u32[]{:S(2)}, u32[]{:S(2)}) collective-permute-start(bf16[512,512]{1,0:T(8,128)(2,1)} %get-tuple-element.317), channel_id=1, source_target_pairs={{0,5},{1,4},{2,7},{3,6},{4,1},{5,0},{6,3},{7,2},{8,13},{9,12},{10,... | collective-permute-start | bytes 1572872 | tf_op jit(solution)/shard_map/ppermute | solution.py:327
  316.8 22.8 %collective-permute-start.31 = (bf16[256,2048]{1,0:T(8,128)(2,1)S(1)}, bf16[256,2048]{1,0:T(8,128)(2,1)S(1)}, u32[]{:S(2)}, u32[]{:S(2)}) collective-permute-start(bf16[256,2048]{1,0:T(8,128)(2,1)S(1)} %pad_maximum_fusion.8), channel_id=1, source_target_pairs={{0,4},{2,6},{4,0},{6,2},{8,12},{10,14},{12,8},{14,10},{16,20},{18,... | collective-permute-start | bytes 3145736 | tf_op jit(solution)/shard_map/ppermute | solution.py:325
  322.2 17.3 %collective-permute-start.29 = (bf16[256,2048]{1,0:T(8,128)(2,1)S(1)}, bf16[256,2048]{1,0:T(8,128)(2,1)S(1)}, u32[]{:S(2)}, u32[]{:S(2)}) collective-permute-start(bf16[256,2048]{1,0:T(8,128)(2,1)S(1)} %pad_maximum_fusion.7), channel_id=1, source_target_pairs={{0,1},{1,0},{2,3},{3,2},{4,5},{5,4},{6,7},{7,6},{8,9},{9,8},{10,11... | collective-permute-start | bytes 3145736 | tf_op jit(solution)/shard_map/ppermute | solution.py:323
  341.6 22.0 %collective-permute-start.33 = (bf16[256,2048]{1,0:T(8,128)(2,1)S(1)}, bf16[256,2048]{1,0:T(8,128)(2,1)S(1)}, u32[]{:S(2)}, u32[]{:S(2)}) collective-permute-start(bf16[256,2048]{1,0:T(8,128)(2,1)S(1)} %multiply_convert_fusion.refs_0_), channel_id=1, source_target_pairs={{0,4},{2,6},{4,0},{6,2},{8,12},{10,14},{12,8},{14,10},{16,20},{18,... | collective-permute-start | bytes 3145736 | tf_op jit(solution)/shard_map/ppermute | solution.py:325
  341.9 24.2 %collective-permute-start.32 = (bf16[256,2048]{1,0:T(8,128)(2,1)S(1)}, bf16[256,2048]{1,0:T(8,128)(2,1)S(1)}, u32[]{:S(2)}, u32[]{:S(2)}) collective-permute-start(bf16[256,2048]{1,0:T(8,128)(2,1)S(1)} %multiply_convert_fusion.refs_0_), channel_id=1, source_target_pairs={{0,1},{1,0},{2,3},{3,2},{4,5},{5,4},{6,7},{7,6},{8,9},{9,8},{10,11... | collective-permute-start | bytes 3145736 | tf_op jit(solution)/shard_map/ppermute | solution.py:323
  378.6 21.2 %collective-permute-start.37 = (bf16[256,2048]{1,0:T(8,128)(2,1)S(1)}, bf16[256,2048]{1,0:T(8,128)(2,1)S(1)}, u32[]{:S(2)}, u32[]{:S(2)}) collective-permute-start(bf16[256,2048]{1,0:T(8,128)(2,1)S(1)} %get-tuple-element.153.refs_0_), channel_id=1, source_target_pairs={{0,4},{2,6},{4,0},{6,2},{8,12},{10,14},{12,8},{14,10},{16,20},{18,... | collective-permute-start | bytes 3145736 | tf_op jit(solution)/shard_map/ppermute | solution.py:325
  379.6 20.2 %collective-permute-start.36 = (bf16[256,2048]{1,0:T(8,128)(2,1)S(1)}, bf16[256,2048]{1,0:T(8,128)(2,1)}, u32[]{:S(2)}, u32[]{:S(2)}) collective-permute-start(bf16[256,2048]{1,0:T(8,128)(2,1)S(1)} %get-tuple-element.153.refs_0_), channel_id=1, source_target_pairs={{0,1},{1,0},{2,3},{3,2},{4,5},{5,4},{6,7},{7,6},{8,9},{9,8},{10,11... | collective-permute-start | bytes 3145736 | tf_op jit(solution)/shard_map/ppermute | solution.py:323
  456.0 181.1 %reduce-scatter.8.cloned.1.call-start = ((), (), s32[]{:S(2)}) async-start(), calls=%async_computation.10 | async-start | bytes 9437184 | tf_op jit(solution)/shard_map/reduce_scatter | solution.py:370
  458.3 19.4 %collective-permute-start.41 = (bf16[128,2048]{1,0:T(8,128)(2,1)}, bf16[128,2048]{1,0:T(8,128)(2,1)}, u32[]{:S(2)}, u32[]{:S(2)}) collective-permute-start(bf16[128,2048]{1,0:T(8,128)(2,1)} %get-tuple-element.288), channel_id=1, source_target_pairs={{0,1},{1,0},{2,3},{3,2},{4,5},{5,4},{6,7},{7,6},{8,9},{9,8},{10,11... | collective-permute-start | bytes 1572872 | tf_op jit(solution)/shard_map/ppermute | solution.py:323
  477.2 16.8 %collective-permute-start.42 = (bf16[256,2048]{1,0:T(8,128)(2,1)S(1)}, bf16[256,2048]{1,0:T(8,128)(2,1)S(1)}, u32[]{:S(2)}, u32[]{:S(2)}) collective-permute-start(bf16[256,2048]{1,0:T(8,128)(2,1)S(1)} %pad_maximum_fusion.10), channel_id=1, source_target_pairs={{0,1},{1,0},{2,3},{3,2},{4,5},{5,4},{6,7},{7,6},{8,9},{9,8},{10,11... | collective-permute-start | bytes 3145736 | tf_op jit(solution)/shard_map/ppermute | solution.py:323
  479.3 19.2 %collective-permute-start.43 = (bf16[256,2048]{1,0:T(8,128)(2,1)S(1)}, bf16[256,2048]{1,0:T(8,128)(2,1)S(1)}, u32[]{:S(2)}, u32[]{:S(2)}) collective-permute-start(bf16[256,2048]{1,0:T(8,128)(2,1)S(1)} %pad_maximum_fusion.11), channel_id=1, source_target_pairs={{0,4},{2,6},{4,0},{6,2},{8,12},{10,14},{12,8},{14,10},{16,20},{18,... | collective-permute-start | bytes 3145736 | tf_op jit(solution)/shard_map/ppermute | solution.py:325
  502.5 21.3 %collective-permute-start.45 = (bf16[256,2048]{1,0:T(8,128)(2,1)S(1)}, bf16[256,2048]{1,0:T(8,128)(2,1)S(1)}, u32[]{:S(2)}, u32[]{:S(2)}) collective-permute-start(bf16[256,2048]{1,0:T(8,128)(2,1)S(1)} %get-tuple-element.240.refs_4_), channel_id=1, source_target_pairs={{0,4},{2,6},{4,0},{6,2},{8,12},{10,14},{12,8},{14,10},{16,20},{18,... | collective-permute-start | bytes 3145736 | tf_op jit(solution)/shard_map/ppermute | solution.py:325
  504.1 20.7 %collective-permute-start.44 = (bf16[256,2048]{1,0:T(8,128)(2,1)S(1)}, bf16[256,2048]{1,0:T(8,128)(2,1)S(1)}, u32[]{:S(2)}, u32[]{:S(2)}) collective-permute-start(bf16[256,2048]{1,0:T(8,128)(2,1)S(1)} %get-tuple-element.240.refs_4_), channel_id=1, source_target_pairs={{0,1},{1,0},{2,3},{3,2},{4,5},{5,4},{6,7},{7,6},{8,9},{9,8},{10,11... | collective-permute-start | bytes 3145736 | tf_op jit(solution)/shard_map/ppermute | solution.py:323
  547.0 188.3 %reduce-scatter.10.cloned.1.call-start = ((), (), s32[]{:S(2)}) async-start(), calls=%async_computation.11 | async-start | bytes 9437184 | tf_op jit(solution)/shard_map/reduce_scatter | solution.py:370
  560.7 23.6 %collective-permute-start.51 = (bf16[256,2048]{1,0:T(8,128)(2,1)S(1)}, bf16[256,2048]{1,0:T(8,128)(2,1)S(1)}, u32[]{:S(2)}, u32[]{:S(2)}) collective-permute-start(bf16[256,2048]{1,0:T(8,128)(2,1)S(1)} %pad_maximum_fusion.13), channel_id=1, source_target_pairs={{0,4},{2,6},{4,0},{6,2},{8,12},{10,14},{12,8},{14,10},{16,20},{18,... | collective-permute-start | bytes 3145736 | tf_op jit(solution)/shard_map/ppermute | solution.py:325
  563.6 20.6 %collective-permute-start.49 = (bf16[256,2048]{1,0:T(8,128)(2,1)S(1)}, bf16[256,2048]{1,0:T(8,128)(2,1)S(1)}, u32[]{:S(2)}, u32[]{:S(2)}) collective-permute-start(bf16[256,2048]{1,0:T(8,128)(2,1)S(1)} %pad_maximum_fusion.12), channel_id=1, source_target_pairs={{0,1},{1,0},{2,3},{3,2},{4,5},{5,4},{6,7},{7,6},{8,9},{9,8},{10,11... | collective-permute-start | bytes 3145736 | tf_op jit(solution)/shard_map/ppermute | solution.py:323
  603.2 22.2 %collective-permute-start.55 = (bf16[256,2048]{1,0:T(8,128)(2,1)}, bf16[256,2048]{1,0:T(8,128)(2,1)}, u32[]{:S(2)}, u32[]{:S(2)}) collective-permute-start(bf16[256,2048]{1,0:T(8,128)(2,1)} %pad_maximum_fusion.15), channel_id=1, source_target_pairs={{0,4},{2,6},{4,0},{6,2},{8,12},{10,14},{12,8},{14,10},{16,20},{18,... | collective-permute-start | bytes 3145736 | tf_op jit(solution)/shard_map/ppermute | solution.py:325
  605.9 21.9 %collective-permute-start.53 = (bf16[256,2048]{1,0:T(8,128)(2,1)}, bf16[256,2048]{1,0:T(8,128)(2,1)}, u32[]{:S(2)}, u32[]{:S(2)}) collective-permute-start(bf16[256,2048]{1,0:T(8,128)(2,1)} %pad_maximum_fusion.14), channel_id=1, source_target_pairs={{0,1},{1,0},{2,3},{3,2},{4,5},{5,4},{6,7},{7,6},{8,9},{9,8},{10,11... | collective-permute-start | bytes 3145736 | tf_op jit(solution)/shard_map/ppermute | solution.py:323
  637.1 150.0 %reduce-scatter.12.cloned.1.call-start = ((), (), s32[]{:S(2)}) async-start(), calls=%async_computation.12 | async-start | bytes 4718592 | tf_op jit(solution)/shard_map/reduce_scatter | solution.py:370
  645.7 25.7 %collective-permute-start.67 = (bf16[512,512]{1,0:T(8,128)(2,1)}, bf16[512,512]{1,0:T(8,128)(2,1)}, u32[]{:S(2)}, u32[]{:S(2)}) collective-permute-start(bf16[512,512]{1,0:T(8,128)(2,1)} %get-tuple-element.278), channel_id=1, source_target_pairs={{0,5},{1,4},{2,7},{3,6},{4,1},{5,0},{6,3},{7,2},{8,13},{9,12},{10,... | collective-permute-start | bytes 1572872 | tf_op jit(solution)/shard_map/ppermute | solution.py:327
  647.1 26.4 %collective-permute-start.66 = (bf16[512,512]{1,0:T(8,128)(2,1)}, bf16[512,512]{1,0:T(8,128)(2,1)}, u32[]{:S(2)}, u32[]{:S(2)}) collective-permute-start(bf16[512,512]{1,0:T(8,128)(2,1)} %get-tuple-element.279), channel_id=1, source_target_pairs={{0,4},{2,6},{4,0},{6,2},{8,12},{10,14},{12,8},{14,10},{16,20},{18,... | collective-permute-start | bytes 1572872 | tf_op jit(solution)/shard_map/ppermute | solution.py:325
  649.9 42.2 %collective-permute-start.57 = (bf16[256,2048]{1,0:T(8,128)(2,1)S(1)}, bf16[256,2048]{1,0:T(8,128)(2,1)S(1)}, u32[]{:S(2)}, u32[]{:S(2)}) collective-permute-start(bf16[256,2048]{1,0:T(8,128)(2,1)S(1)} %get-tuple-element.237.refs_4_), channel_id=1, source_target_pairs={{0,4},{2,6},{4,0},{6,2},{8,12},{10,14},{12,8},{14,10},{16,20},{18,... | collective-permute-start | bytes 3145736 | tf_op jit(solution)/shard_map/ppermute | solution.py:325
  651.3 42.3 %collective-permute-start.56 = (bf16[256,2048]{1,0:T(8,128)(2,1)S(1)}, bf16[256,2048]{1,0:T(8,128)(2,1)}, u32[]{:S(2)}, u32[]{:S(2)}) collective-permute-start(bf16[256,2048]{1,0:T(8,128)(2,1)S(1)} %get-tuple-element.237.refs_4_), channel_id=1, source_target_pairs={{0,1},{1,0},{2,3},{3,2},{4,5},{5,4},{6,7},{7,6},{8,9},{9,8},{10,11... | collective-permute-start | bytes 3145736 | tf_op jit(solution)/shard_map/ppermute | solution.py:323
  697.6 27.1 %collective-permute-start.60 = (bf16[256,2048]{1,0:T(8,128)(2,1)S(1)}, bf16[256,2048]{1,0:T(8,128)(2,1)S(1)}, u32[]{:S(2)}, u32[]{:S(2)}) collective-permute-start(bf16[256,2048]{1,0:T(8,128)(2,1)S(1)} %copy-done.17), channel_id=1, source_target_pairs={{0,1},{1,0},{2,3},{3,2},{4,5},{5,4},{6,7},{7,6},{8,9},{9,8},{10,11... | collective-permute-start | bytes 3145736 | tf_op jit(solution)/shard_map/ppermute | solution.py:323
  735.3 155.9 %reduce-scatter.14.cloned.1.call-start = ((), (), s32[]{:S(2)}) async-start(), calls=%async_computation.13 | async-start | bytes 9437184 | tf_op jit(solution)/shard_map/reduce_scatter | solution.py:370
  747.3 22.8 %collective-permute-start.64 = (bf16[256,2048]{1,0:T(8,128)(2,1)}, bf16[256,2048]{1,0:T(8,128)(2,1)}, u32[]{:S(2)}, u32[]{:S(2)}) collective-permute-start(bf16[256,2048]{1,0:T(8,128)(2,1)} %pad_maximum_fusion.17), channel_id=1, source_target_pairs={{0,4},{2,6},{4,0},{6,2},{8,12},{10,14},{12,8},{14,10},{16,20},{18,... | collective-permute-start | bytes 3145736 | tf_op jit(solution)/shard_map/ppermute | solution.py:325
  751.5 18.6 %collective-permute-start.62 = (bf16[256,2048]{1,0:T(8,128)(2,1)}, bf16[256,2048]{1,0:T(8,128)(2,1)}, u32[]{:S(2)}, u32[]{:S(2)}) collective-permute-start(bf16[256,2048]{1,0:T(8,128)(2,1)} %pad_maximum_fusion.16), channel_id=1, source_target_pairs={{0,1},{1,0},{2,3},{3,2},{4,5},{5,4},{6,7},{7,6},{8,9},{9,8},{10,11... | collective-permute-start | bytes 3145736 | tf_op jit(solution)/shard_map/ppermute | solution.py:323
  806.6 23.0 %collective-permute-start.69 = (bf16[128,2048]{1,0:T(8,128)(2,1)S(1)}, bf16[128,2048]{1,0:T(8,128)(2,1)S(1)}, u32[]{:S(2)}, u32[]{:S(2)}) collective-permute-start(bf16[128,2048]{1,0:T(8,128)(2,1)S(1)} %get-tuple-element.194), channel_id=1, source_target_pairs={{0,4},{2,6},{4,0},{6,2},{8,12},{10,14},{12,8},{14,10},{16,20},{18,... | collective-permute-start | bytes 1572872 | tf_op jit(solution)/shard_map/ppermute | solution.py:325
  807.2 22.4 %collective-permute-start.68 = (bf16[128,2048]{1,0:T(8,128)(2,1)S(1)}, bf16[128,2048]{1,0:T(8,128)(2,1)S(1)}, u32[]{:S(2)}, u32[]{:S(2)}) collective-permute-start(bf16[128,2048]{1,0:T(8,128)(2,1)S(1)} %get-tuple-element.193.refs_0_), channel_id=1, source_target_pairs={{0,1},{1,0},{2,3},{3,2},{4,5},{5,4},{6,7},{7,6},{8,9},{9,8},{10,11... | collective-permute-start | bytes 1572872 | tf_op jit(solution)/shard_map/ppermute | solution.py:323
  808.4 22.7 %collective-permute-start.78 = (f32[3,256]{1,0:T(4,128)S(1)}, f32[3,256]{1,0:T(4,128)S(1)}, u32[]{:S(2)}, u32[]{:S(2)}) collective-permute-start(f32[3,256]{1,0:T(4,128)S(1)} %slice_select_fusion.2), channel_id=1, source_target_pairs={{0,4},{2,6},{4,0},{6,2},{8,12},{10,14},{12,8},{14,10},{16,20},{18,... | collective-permute-start | bytes 9224 | tf_op jit(solution)/shard_map/ppermute | solution.py:330
  831.1 19.9 %collective-permute-start.79 = (f32[3,128]{1,0:T(4,128)S(1)}, f32[3,128]{1,0:T(4,128)S(1)}, u32[]{:S(2)}, u32[]{:S(2)}) collective-permute-start(f32[3,128]{1,0:T(4,128)S(1)} %slice_select_fusion.3), channel_id=1, source_target_pairs={{0,2},{2,0},{4,6},{6,4},{8,10},{10,8},{12,14},{14,12},{16,18},{18,... | collective-permute-start | bytes 4616 | tf_op jit(solution)/shard_map/ppermute | solution.py:330
  848.4 20.8 %collective-permute-start.80 = (bf16[128,1536]{1,0:T(8,128)(2,1)S(1)}, bf16[128,1536]{1,0:T(8,128)(2,1)S(1)}, u32[]{:S(2)}, u32[]{:S(2)}) collective-permute-start(bf16[128,1536]{1,0:T(8,128)(2,1)S(1)} %get-tuple-element.210.refs_0_), channel_id=1, source_target_pairs={{0,1},{1,0},{2,3},{3,2},{4,5},{5,4},{6,7},{7,6},{8,9},{9,8},{10,11... | collective-permute-start | bytes 1179656 | tf_op jit(solution)/shard_map/ppermute | solution.py:323
  851.0 26.8 %collective-permute-start.82 = (bf16[128,1536]{1,0:T(8,128)(2,1)S(1)}, bf16[128,1536]{1,0:T(8,128)(2,1)S(1)}, u32[]{:S(2)}, u32[]{:S(2)}) collective-permute-start(bf16[128,1536]{1,0:T(8,128)(2,1)S(1)} %get-tuple-element.211), channel_id=1, source_target_pairs={{0,5},{1,4},{2,7},{3,6},{4,1},{5,0},{6,3},{7,2},{8,13},{9,12},{10,... | collective-permute-start | bytes 1179656 | tf_op jit(solution)/shard_map/ppermute | solution.py:327
  855.1 24.0 %collective-permute-start.81 = (bf16[128,1536]{1,0:T(8,128)(2,1)S(1)}, bf16[128,1536]{1,0:T(8,128)(2,1)S(1)}, u32[]{:S(2)}, u32[]{:S(2)}) collective-permute-start(bf16[128,1536]{1,0:T(8,128)(2,1)S(1)} %get-tuple-element.211), channel_id=1, source_target_pairs={{0,4},{2,6},{4,0},{6,2},{8,12},{10,14},{12,8},{14,10},{16,20},{18,... | collective-permute-start | bytes 1179656 | tf_op jit(solution)/shard_map/ppermute | solution.py:325
  860.7 28.1 %collective-permute-start.88 = (bf16[128,1024]{1,0:T(8,128)(2,1)S(1)}, bf16[128,1024]{1,0:T(8,128)(2,1)S(1)}, u32[]{:S(2)}, u32[]{:S(2)}) collective-permute-start(bf16[128,1024]{1,0:T(8,128)(2,1)S(1)} %get-tuple-element.215), channel_id=1, source_target_pairs={{0,5},{1,4},{2,7},{3,6},{4,1},{5,0},{6,3},{7,2},{8,13},{9,12},{10,... | collective-permute-start | bytes 786440 | tf_op jit(solution)/shard_map/ppermute | solution.py:327
  862.0 26.8 %collective-permute-start.87 = (bf16[128,1024]{1,0:T(8,128)(2,1)S(1)}, bf16[128,1024]{1,0:T(8,128)(2,1)S(1)}, u32[]{:S(2)}, u32[]{:S(2)}) collective-permute-start(bf16[128,1024]{1,0:T(8,128)(2,1)S(1)} %get-tuple-element.215), channel_id=1, source_target_pairs={{0,4},{2,6},{4,0},{6,2},{8,12},{10,14},{12,8},{14,10},{16,20},{18,... | collective-permute-start | bytes 786440 | tf_op jit(solution)/shard_map/ppermute | solution.py:325
  869.1 19.7 %collective-permute-start.86 = (bf16[128,1024]{1,0:T(8,128)(2,1)S(1)}, bf16[128,1024]{1,0:T(8,128)(2,1)S(1)}, u32[]{:S(2)}, u32[]{:S(2)}) collective-permute-start(bf16[128,1024]{1,0:T(8,128)(2,1)S(1)} %get-tuple-element.214.refs_0_), channel_id=1, source_target_pairs={{0,1},{1,0},{2,3},{3,2},{4,5},{5,4},{6,7},{7,6},{8,9},{9,8},{10,11... | collective-permute-start | bytes 786440 | tf_op jit(solution)/shard_map/ppermute | solution.py:323
  877.8 30.7 %collective-permute-start.74 = (bf16[128,4096]{1,0:T(8,128)(2,1)}, bf16[128,4096]{1,0:T(8,128)(2,1)S(1)}, u32[]{:S(2)}, u32[]{:S(2)}) collective-permute-start(bf16[128,4096]{1,0:T(8,128)(2,1)} %pad_maximum_fusion.19), channel_id=1, source_target_pairs={{0,4},{2,6},{4,0},{6,2},{8,12},{10,14},{12,8},{14,10},{16,20},{18,... | collective-permute-start | bytes 3145736 | tf_op jit(solution)/shard_map/ppermute | solution.py:325
  879.1 32.2 %collective-permute-start.72 = (bf16[128,4096]{1,0:T(8,128)(2,1)}, bf16[128,4096]{1,0:T(8,128)(2,1)S(1)}, u32[]{:S(2)}, u32[]{:S(2)}) collective-permute-start(bf16[128,4096]{1,0:T(8,128)(2,1)} %pad_maximum_fusion.18), channel_id=1, source_target_pairs={{0,1},{1,0},{2,3},{3,2},{4,5},{5,4},{6,7},{7,6},{8,9},{9,8},{10,11... | collective-permute-start | bytes 3145736 | tf_op jit(solution)/shard_map/ppermute | solution.py:323
  893.0 23.9 %collective-permute-start.94 = (bf16[64,2048]{1,0:T(8,128)(2,1)S(1)}, bf16[64,2048]{1,0:T(8,128)(2,1)S(1)}, u32[]{:S(2)}, u32[]{:S(2)}) collective-permute-start(bf16[64,2048]{1,0:T(8,128)(2,1)S(1)} %get-tuple-element.219.refs_4_), channel_id=1, source_target_pairs={{0,3},{1,2},{2,1},{3,0},{4,7},{5,6},{6,5},{7,4},{8,11},{9,10},{10,... | collective-permute-start | bytes 786440 | tf_op jit(solution)/shard_map/ppermute | solution.py:905
  899.4 23.1 %collective-permute-start.93 = (bf16[64,2048]{1,0:T(8,128)(2,1)S(1)}, bf16[64,2048]{1,0:T(8,128)(2,1)S(1)}, u32[]{:S(2)}, u32[]{:S(2)}) collective-permute-start(bf16[64,2048]{1,0:T(8,128)(2,1)S(1)} %get-tuple-element.219.refs_4_), channel_id=1, source_target_pairs={{0,1},{1,0},{2,3},{3,2},{4,5},{5,4},{6,7},{7,6},{8,9},{9,8},{10,11... | collective-permute-start | bytes 786440 | tf_op jit(solution)/shard_map/ppermute | solution.py:323
  900.5 22.0 %collective-permute-start.92 = (bf16[64,2048]{1,0:T(8,128)(2,1)S(1)}, bf16[64,2048]{1,0:T(8,128)(2,1)S(1)}, u32[]{:S(2)}, u32[]{:S(2)}) collective-permute-start(bf16[64,2048]{1,0:T(8,128)(2,1)S(1)} %get-tuple-element.219.refs_4_), channel_id=1, source_target_pairs={{0,2},{2,0},{4,6},{6,4},{8,10},{10,8},{12,14},{14,12},{16,18},{18,... | collective-permute-start | bytes 786440 | tf_op jit(solution)/shard_map/ppermute | solution.py:330
  908.5 30.9 %collective-permute-start.91 = (bf16[128,1536]{1,0:T(8,128)(2,1)S(1)}, bf16[128,1536]{1,0:T(8,128)(2,1)S(1)}, u32[]{:S(2)}, u32[]{:S(2)}) collective-permute-start(bf16[128,1536]{1,0:T(8,128)(2,1)S(1)} %get-tuple-element.218), channel_id=1, source_target_pairs={{0,5},{1,4},{2,7},{3,6},{4,1},{5,0},{6,3},{7,2},{8,13},{9,12},{10,... | collective-permute-start | bytes 1179656 | tf_op jit(solution)/shard_map/ppermute | solution.py:327
  911.3 28.1 %collective-permute-start.90 = (bf16[128,1536]{1,0:T(8,128)(2,1)S(1)}, bf16[128,1536]{1,0:T(8,128)(2,1)S(1)}, u32[]{:S(2)}, u32[]{:S(2)}) collective-permute-start(bf16[128,1536]{1,0:T(8,128)(2,1)S(1)} %get-tuple-element.218), channel_id=1, source_target_pairs={{0,4},{2,6},{4,0},{6,2},{8,12},{10,14},{12,8},{14,10},{16,20},{18,... | collective-permute-start | bytes 1179656 | tf_op jit(solution)/shard_map/ppermute | solution.py:325
  916.9 22.4 %collective-permute-start.89 = (bf16[128,1536]{1,0:T(8,128)(2,1)S(1)}, bf16[128,1536]{1,0:T(8,128)(2,1)S(1)}, u32[]{:S(2)}, u32[]{:S(2)}) collective-permute-start(bf16[128,1536]{1,0:T(8,128)(2,1)S(1)} %get-tuple-element.217.refs_0_), channel_id=1, source_target_pairs={{0,1},{1,0},{2,3},{3,2},{4,5},{5,4},{6,7},{7,6},{8,9},{9,8},{10,11... | collective-permute-start | bytes 1179656 | tf_op jit(solution)/shard_map/ppermute | solution.py:323
  (162 other events, 2486.2 us)
Sparse Core Ops, SparseCore 0:
  26.3 83.8 all-gather.4
  112.4 115.1 all-gather.6
  229.8 80.2 all-gather.8
  312.1 80.5 all-gather.10
  456.1 90.7 reduce-scatter.5
  549.1 87.9 reduce-scatter.7
  639.4 87.9 reduce-scatter.9
  735.4 51.6 reduce-scatter.11
  789.4 88.2 reduce-scatter.13

commit v4 on v3

--- a/solution.py
+++ b/solution.py
@@ -919,7 +919,7 @@
         norm_sums = unshuffle(after(norm_sums, *caption_part))
         norm_sums = reduce_small(norm_sums, d)
         self_sums = after(
-            self_sums, grad_down, grad_up, grad_cross_query, grad_text, norm_sums, layer_out
+            self_sums, grad_down, grad_up, norm_sums, layer_out, *cross_pieces, *text_pieces
         )
         self_pieces = seven(self_sums)
         grad_query, grad_key, grad_value, grad_out = whole_call(

time: 956 us -> 956 us (level)
    unnamed x249 -> x271, local copies, waits for them, and re-layouts: 30.7 us -> 32.6 us
  transfers between devices with their start and end apart: 104 -> 104, of which waited for: 68 -> 69; matrix products, arithmetic and copies ran while one was open for 21% -> 21% of each run, Pallas kernels for 12% -> 12%
where the time goes in v4:
time: 956 us; the launch traced here: 949 us
  waiting for transfers between devices  454 us (47%)
  Pallas kernels  132 us (14%)
  matrix products  119 us (12%)
  starting transfers between devices  91.7 us (10%)
  local copies, waits for them, and re-layouts  86.5 us (9%)
  other arithmetic  49.3 us (5%)
  between operations  16.4 us (2%)
    ppermute x37, waiting for transfers between devices, swap(): return lax.ppermute(values, 'dp', [(d, d ^ spread) for d in range(devices)])  236 us
    ppermute x37, waiting for transfers between devices, swap(): return lax.ppermute(values, 'seq', [(0, 1), (1, 0)])  135 us
    dot_general x13, matrix products, mm_t(): lax.dot_general(left, right, (((1,), (1,)), ((), ())), preferred_element_...  46.8 us
    dot_general x13, matrix products, mm(): lax.dot_general(left, right, (((1,), (0,)), ((), ())), preferred_element_...  46.4 us
    pallas_call x3, Pallas kernels, weight_call(): pl.pallas_call(kernel, grid=(blocks,), in_specs=specs, out_specs=pl.Block...  42.4 us
    ppermute x37, starting transfers between devices, swap(): return lax.ppermute(values, 'dp', [(d, d ^ spread) for d in range(devices)])  37.2 us
    ppermute x7, waiting for transfers between devices, swap(): return lax.ppermute(values, ('dp', 'seq'), pairs)  36.8 us
    ppermute x37, starting transfers between devices, swap(): return lax.ppermute(values, 'seq', [(0, 1), (1, 0)])  35.6 us
  transfers between devices with their start and end apart: 104, of which 69 were waited for; matrix products, arithmetic and copies ran while one was open for 21% of the time, Pallas kernels for 12%

profile of v4, /device:TPU:0, one launch (start us, length us, event | category | flops | bytes accessed | tf_op | source)
XLA Modules:
  0.0 949.3 jit_solution(1913182322998610759)
XLA Ops:
  17.0 7.6 collective-permute-done.other
  30.5 12.6 %collective-permute-done.19.other = bf16[128,2560]{1,0:T(8,128)(2,1)S(1)} collective-permute-done((bf16[128,2560]{1,0:T(8,128)(2,1)S(1)}, bf16[128,2560]{1,0:T(8,128)(2,1)S(1)}, u32[]{:S(2)}, u32[]{:S(2)}) %collective-permute-start.19) | collective-permute-done | bytes 655392 | tf_op jit(solution)/shard_map/ppermute | solution.py:325
  48.5 4.0 shard_map.309
  56.8 22.0 %collective-permute-done.3 = bf16[256,2048]{1,0:T(8,128)(2,1)} collective-permute-done((bf16[256,2048]{1,0:T(8,128)(2,1)S(1)}, bf16[256,2048]{1,0:T(8,128)(2,1)}, u32[]{:S(2)}, u32[]{:S(2)}) %collective-permute-start.3) | collective-permute-done | bytes 1048608 | tf_op jit(solution)/shard_map/ppermute | solution.py:325
  82.0 5.3 collective-permute-done.8.other
  109.1 9.2 collective-permute-done.10
  123.6 4.0 fusion.57
  127.6 5.1 fusion.33
  142.4 4.2 collective-permute-done.13.refs_3_.refs_7_
  146.5 19.2 %collective-permute-done.12.refs_2_.refs_6_ = bf16[128,4096]{1,0:T(8,128)(2,1)} collective-permute-done((bf16[128,4096]{1,0:T(8,128)(2,1)S(1)}, bf16[128,4096]{1,0:T(8,128)(2,1)}, u32[]{:S(2)}, u32[]{:S(2)}) %collective-permute-start.12) | collective-permute-done | bytes 1048608 | tf_op jit(solution)/shard_map/ppermute | solution.py:325
  174.9 11.4 %collective-permute-done.16 = bf16[128,2048]{1,0:T(8,128)(2,1)S(1)} collective-permute-done((bf16[128,2048]{1,0:T(8,128)(2,1)S(1)}, bf16[128,2048]{1,0:T(8,128)(2,1)S(1)}, u32[]{:S(2)}, u32[]{:S(2)}) %collective-permute-start.16) | collective-permute-done | bytes 524320 | tf_op jit(solution)/shard_map/ppermute | solution.py:323
  188.8 22.0 %collective-permute-done.17 = bf16[256,2048]{1,0:T(8,128)(2,1)S(1)} collective-permute-done((bf16[256,2048]{1,0:T(8,128)(2,1)S(1)}, bf16[256,2048]{1,0:T(8,128)(2,1)S(1)}, u32[]{:S(2)}, u32[]{:S(2)}) %collective-permute-start.17) | collective-permute-done | bytes 1048608 | tf_op jit(solution)/shard_map/ppermute | solution.py:325
  217.0 21.0 %collective-permute-done.22.refs_2_ = bf16[256,2048]{1,0:T(8,128)(2,1)} collective-permute-done((bf16[256,2048]{1,0:T(8,128)(2,1)S(1)}, bf16[256,2048]{1,0:T(8,128)(2,1)}, u32[]{:S(2)}, u32[]{:S(2)}) %collective-permute-start.22) | collective-permute-done | bytes 1048608 | tf_op jit(solution)/shard_map/ppermute | solution.py:325
  244.2 7.1 collective-permute-done.23
  258.9 6.7 constant_dynamic-update-slice_fusion.13
  294.2 4.5 fusion.64
  308.2 8.3 collective-permute-done.30
  317.9 4.1 collective-permute-done.28
  322.3 17.3 %collective-permute-done.31 = bf16[256,2048]{1,0:T(8,128)(2,1)S(1)} collective-permute-done((bf16[256,2048]{1,0:T(8,128)(2,1)S(1)}, bf16[256,2048]{1,0:T(8,128)(2,1)S(1)}, u32[]{:S(2)}, u32[]{:S(2)}) %collective-permute-start.31) | collective-permute-done | bytes 1048608 | tf_op jit(solution)/shard_map/ppermute | solution.py:325
  342.6 21.2 %collective-permute-done.33.refs_2_ = bf16[256,2048]{1,0:T(8,128)(2,1)S(1)} collective-permute-done((bf16[256,2048]{1,0:T(8,128)(2,1)S(1)}, bf16[256,2048]{1,0:T(8,128)(2,1)S(1)}, u32[]{:S(2)}, u32[]{:S(2)}) %collective-permute-start.33) | collective-permute-done | bytes 1048608 | tf_op jit(solution)/shard_map/ppermute | solution.py:325
  366.5 8.3 collective-permute-done.34
  379.7 17.6 %shard_map.314 = (bf16[1024,2048]{1,0:T(8,128)(2,1)}, f32[1024,2048]{1,0:T(8,128)}, bf16[1024,2048]{1,0:T(8,128)(2,1)}) custom-call(bf16[256,2048]{1,0:T(8,128)(2,1)} %copy-done.71, bf16[256,2048]{1,0:T(8,128)(2,1)} %copy-done.89, bf16[256,2048]{1,0:T(8,128)(2,1)} %copy-done.87, bf16[256,2048]{1,0:T(8,128)(2,1)} %copy-done.90, ...), custom_call_target="tpu_custom_call" | custom-call | tf_op jit(solution)/shard_map/pallas_call | solution.py:101
  401.9 8.8 collective-permute-done.38
  411.8 15.9 %shard_map.315 = (bf16[1024,2048]{1,0:T(8,128)(2,1)}, bf16[1024,2048]{1,0:T(8,128)(2,1)}) custom-call(bf16[256,2048]{1,0:T(8,128)(2,1)} %copy-done.3, bf16[256,2048]{1,0:T(8,128)(2,1)} %collective-permute-done.36.refs_1_, bf16[256,2048]{1,0:T(8,128)(2,1)} %copy-done.88, bf16[256,2048]{1,0:T(8,128)(2,1)} %pad_maximum_fusion.9.refs_3_, ...), custom_call_target="tpu_custom_call" | custom-call | tf_op jit(solution)/shard_map/pallas_call | solution.py:101
  427.8 12.7 %convolution_convert_fusion.6 = bf16[1024,2048]{1,0:T(8,128)(2,1)S(1)} fusion(bf16[1024,2048]{1,0:T(8,128)(2,1)} %get-tuple-element.162, bf16[2048,2048]{1,0:T(8,128)(2,1)} %all-gather.9.cloned.1.call-done.refs_4_), kind=kOutput, calls=%fused_computation.15 | convolution fusion | flops 8592031744 | bytes 16777216 | tf_op jit(solution)/shard_map/dot_general | solution.py:37
  444.7 11.3 %convolution_convert_fusion.1 = bf16[2048,2048]{1,0:T(8,128)(2,1)} fusion(bf16[1024,2048]{1,0:T(8,128)(2,1)S(1)} %copy-done.121, bf16[1024,2048]{1,0:T(8,128)(2,1)S(1)} %copy-done.123), kind=kOutput, calls=%fused_computation.1 | convolution fusion | flops 8594128896 | bytes 16777216 | tf_op jit(solution)/shard_map/dot_general | solution.py:41
  460.7 14.7 %convolution_convert_fusion = bf16[2048,2048]{1,0:T(8,128)(2,1)} fusion(bf16[1024,2048]{1,0:T(8,128)(2,1)} %get-tuple-element.151, bf16[1024,2048]{1,0:T(8,128)(2,1)} %get-tuple-element.162), kind=kOutput, calls=%fused_computation | convolution fusion | flops 8594128896 | bytes 16777216 | tf_op jit(solution)/shard_map/dot_general | solution.py:41
  481.2 11.3 %convolution_convert_fusion.5 = bf16[1024,2048]{1,0:T(8,128)(2,1)S(1)} fusion(bf16[1024,2048]{1,0:T(8,128)(2,1)S(1)} %copy-done.122, bf16[2048,2048]{1,0:T(8,128)(2,1)} %all-gather.11.cloned.1.call-done.refs_4_), kind=kOutput, calls=%fused_computation.14 | convolution fusion | flops 8592031744 | bytes 16777216 | tf_op jit(solution)/shard_map/dot_general | solution.py:33
  494.2 4.6 collective-permute-done.43
  505.5 18.4 %collective-permute-done.45.refs_6_ = bf16[256,2048]{1,0:T(8,128)(2,1)S(1)} collective-permute-done((bf16[256,2048]{1,0:T(8,128)(2,1)S(1)}, bf16[256,2048]{1,0:T(8,128)(2,1)S(1)}, u32[]{:S(2)}, u32[]{:S(2)}) %collective-permute-start.45) | collective-permute-done | bytes 1048608 | tf_op jit(solution)/shard_map/ppermute | solution.py:325
  527.3 5.9 collective-permute-done.46
  535.8 11.1 %reduce-scatter.6.cloned.1.call-done.own = bf16[256,2048]{1,0:T(8,128)(2,1)} async-done(((bf16[2048,2048]{1,0:T(8,128)(2,1)}), bf16[256,2048]{1,0:T(8,128)(2,1)}) %reduce-scatter.6.cloned.1.call-update) | async-done | bytes 1048592 | tf_op jit(solution)/shard_map/reduce_scatter | solution.py:370
  551.9 8.4 collective-permute-done.50
  568.9 7.1 shard_map.317
  576.1 8.1 collective-permute-done.51
  584.8 4.0 convolution_convert_fusion.4
  592.7 9.2 collective-permute-done.54
  606.4 16.1 %shard_map.324 = bf16[2048,2048]{1,0:T(8,128)(2,1)} custom-call(bf16[256,2048]{1,0:T(8,128)(2,1)} %copy-done.85, bf16[256,2048]{1,0:T(8,128)(2,1)} %collective-permute-done.21.refs_1_, bf16[256,2048]{1,0:T(8,128)(2,1)} %collective-permute-done.22.refs_2_, bf16[256,2048]{1,0:T(8,128)(2,1)} %constant_dynamic-update-slice_fusion.2.refs_3_, ...), custom_call_target="tpu_custom_call" | custom-call | tf_op jit(solution)/shard_map/pallas_call | solution.py:266
  627.7 4.1 multiply_reduce_fusion.1
  631.9 5.2 reduce-scatter.8.cloned.1.call-done.summed
  638.3 4.7 fusion.21
  652.8 6.3 collective-permute-done.65
  661.7 9.6 %collective-permute-done.67 = bf16[512,512]{1,0:T(8,128)(2,1)} collective-permute-done((bf16[512,512]{1,0:T(8,128)(2,1)}, bf16[512,512]{1,0:T(8,128)(2,1)}, u32[]{:S(2)}, u32[]{:S(2)}) %collective-permute-start.67) | collective-permute-done | bytes 524320 | tf_op jit(solution)/shard_map/ppermute | solution.py:327
  678.0 8.5 shard_map.323
  700.7 6.3 collective-permute-done.58
  709.9 9.5 %shard_map.318 = bf16[4,2,128,1536]{3,2,1,0:T(8,128)(2,1)} custom-call(bf16[2,128,1536]{2,1,0:T(8,128)(2,1)S(1)} %bitcast.128, bf16[2,128,1536]{2,1,0:T(8,128)(2,1)S(1)} %bitcast.126, bf16[2,128,1536]{2,1,0:T(8,128)(2,1)S(1)} %bitcast.124, bf16[2,128,1536]{2,1,0:T(8,128)(2,1)S(1)} %bitcast.122, bf16[2,128,512]{2,1,0:T(8,128)(2,1)S(1)} %bitcast.150, ...), custom_call_target="tpu_custom_call" | custom-call | tf_op jit(solution)/shard_map/pallas_call | solution.py:205
  719.4 5.3 collective-permute-done.60.other
  724.7 8.7 convolution_convert_fusion.3
  738.9 7.1 collective-permute-done.63
  751.7 17.8 %shard_map.322 = bf16[2048,2048]{1,0:T(8,128)(2,1)} custom-call(bf16[256,2048]{1,0:T(8,128)(2,1)} %get-tuple-element.306.refs_0_, bf16[256,2048]{1,0:T(8,128)(2,1)} %get-tuple-element.305.refs_1_, bf16[256,2048]{1,0:T(8,128)(2,1)} %get-tuple-element.304.refs_2_, bf16[256,2048]{1,0:T(8,128)(2,1)} %get-tuple-element.303.refs_3_, bf16[256,2048]{1,0:T(8,128)(2,1)} %copy-done.70, ...), custom_call_target="tpu_custom_call" | custom-call | tf_op jit(solution)/shard_map/pallas_call | solution.py:266
  770.1 4.2 fusion.53
  774.3 12.7 %reduce-scatter.12.cloned.1.call-done.summed = bf16[256,1024]{1,0:T(8,128)(2,1)} async-done(((bf16[2048,1024]{1,0:T(8,128)(2,1)}), bf16[256,1024]{1,0:T(8,128)(2,1)}) %reduce-scatter.12.cloned.1.call-update) | async-done | bytes 524304 | tf_op jit(solution)/shard_map/reduce_scatter | solution.py:370
  787.1 4.8 convolution_convert_fusion.2
  809.3 11.5 %collective-permute-done.70.refs_3_ = bf16[128,2048]{1,0:T(8,128)(2,1)S(1)} collective-permute-done((bf16[128,2048]{1,0:T(8,128)(2,1)S(1)}, bf16[128,2048]{1,0:T(8,128)(2,1)S(1)}, u32[]{:S(2)}, u32[]{:S(2)}) %collective-permute-start.70) | collective-permute-done | bytes 524320 | tf_op jit(solution)/shard_map/ppermute | solution.py:327
  820.8 8.6 collective-permute-done.69.refs_2_
  832.2 11.3 %collective-permute-done.71 = bf16[64,4096]{1,0:T(8,128)(2,1)S(1)} collective-permute-done((bf16[64,4096]{1,0:T(8,128)(2,1)S(1)}, bf16[64,4096]{1,0:T(8,128)(2,1)S(1)}, u32[]{:S(2)}, u32[]{:S(2)}) %collective-permute-start.71) | collective-permute-done | bytes 524320 | tf_op jit(solution)/shard_map/ppermute | solution.py:325
  855.9 4.8 collective-permute-done.84.refs_6_
  863.0 6.3 collective-permute-done.82.refs_3_
  872.6 5.0 collective-permute-done.80.refs_1_
  884.7 4.1 collective-permute-done.86.refs_1_
  899.0 5.7 collective-permute-done.74
  906.1 5.4 collective-permute-done.72
  912.1 4.9 collective-permute-done.94.refs_7_
  927.4 12.0 %collective-permute-done.89.refs_1_ = bf16[128,1536]{1,0:T(8,128)(2,1)S(1)} collective-permute-done((bf16[128,1536]{1,0:T(8,128)(2,1)S(1)}, bf16[128,1536]{1,0:T(8,128)(2,1)S(1)}, u32[]{:S(2)}, u32[]{:S(2)}) %collective-permute-start.89) | collective-permute-done | bytes 393248 | tf_op jit(solution)/shard_map/ppermute | solution.py:323
  (651 shorter events, 328.2 us)
Async XLA Ops:
  7.2 120.4 %all-gather.5.cloned.1.call-start = ((), (), s32[]{:S(2)}) async-start(), calls=%async_computation.5 | async-start | bytes 9437184 | tf_op jit(solution)/shard_map/all_gather | solution.py:367
  26.1 229.2 %all-gather.7.cloned.1.call-start = ((), (), s32[]{:S(2)}) async-start(), calls=%async_computation.6 | async-start | bytes 14155776 | tf_op jit(solution)/shard_map/all_gather | solution.py:367
  44.9 334.8 %all-gather.9.cloned.1.call-start = ((), (), s32[]{:S(2)}) async-start(), calls=%async_computation.7 | async-start | bytes 9437184 | tf_op jit(solution)/shard_map/all_gather | solution.py:367
  52.5 26.3 %collective-permute-start.3 = (bf16[256,2048]{1,0:T(8,128)(2,1)S(1)}, bf16[256,2048]{1,0:T(8,128)(2,1)}, u32[]{:S(2)}, u32[]{:S(2)}) collective-permute-start(bf16[256,2048]{1,0:T(8,128)(2,1)S(1)} %get-tuple-element.131), channel_id=1, source_target_pairs={{0,4},{2,6},{4,0},{6,2},{8,12},{10,14},{12,8},{14,10},{16,20},{18,... | collective-permute-start | bytes 3145736 | tf_op jit(solution)/shard_map/ppermute | solution.py:325
  54.0 33.4 %collective-permute-start.2 = (bf16[256,2048]{1,0:T(8,128)(2,1)S(1)}, bf16[256,2048]{1,0:T(8,128)(2,1)}, u32[]{:S(2)}, u32[]{:S(2)}) collective-permute-start(bf16[256,2048]{1,0:T(8,128)(2,1)S(1)} %get-tuple-element.131), channel_id=1, source_target_pairs={{0,1},{1,0},{2,3},{3,2},{4,5},{5,4},{6,7},{7,6},{8,9},{9,8},{10,11... | collective-permute-start | bytes 3145736 | tf_op jit(solution)/shard_map/ppermute | solution.py:323
  55.5 31.9 %collective-permute-start.8 = (bf16[128,2048]{1,0:T(8,128)(2,1)}, bf16[128,2048]{1,0:T(8,128)(2,1)S(1)}, u32[]{:S(2)}, u32[]{:S(2)}) collective-permute-start(bf16[128,2048]{1,0:T(8,128)(2,1)} %copy-done.57), channel_id=1, source_target_pairs={{0,4},{2,6},{4,0},{6,2},{8,12},{10,14},{12,8},{14,10},{16,20},{18,... | collective-permute-start | bytes 1572872 | tf_op jit(solution)/shard_map/ppermute | solution.py:325
  80.6 27.3 %collective-permute-start.9 = (bf16[128,2048]{1,0:T(8,128)(2,1)}, bf16[128,2048]{1,0:T(8,128)(2,1)}, u32[]{:S(2)}, u32[]{:S(2)}) collective-permute-start(bf16[128,2048]{1,0:T(8,128)(2,1)} %slice.350), channel_id=1, source_target_pairs={{0,1},{1,0},{2,3},{3,2},{4,5},{5,4},{6,7},{7,6},{8,9},{9,8},{10,11... | collective-permute-start | bytes 1572872 | tf_op jit(solution)/shard_map/ppermute | solution.py:323
  90.4 321.4 %all-gather.11.cloned.1.call-start = ((), (), s32[]{:S(2)}) async-start(), calls=%async_computation.8 | async-start | bytes 9437184 | tf_op jit(solution)/shard_map/all_gather | solution.py:367
  119.4 27.2 %collective-permute-start.13 = (bf16[128,4096]{1,0:T(8,128)(2,1)S(1)}, bf16[128,4096]{1,0:T(8,128)(2,1)}, u32[]{:S(2)}, u32[]{:S(2)}) collective-permute-start(bf16[128,4096]{1,0:T(8,128)(2,1)S(1)} %get-tuple-element.137.refs_0_.refs_4_), channel_id=1, source_target_pairs={{0,5},{1,4},{2,7},{3,6},{4,1},{5,0},{6,3},{7,2},{8,13},{9,12},{10,... | collective-permute-start | bytes 3145736 | tf_op jit(solution)/shard_map/ppermute | solution.py:327
  121.9 43.8 %collective-permute-start.12 = (bf16[128,4096]{1,0:T(8,128)(2,1)S(1)}, bf16[128,4096]{1,0:T(8,128)(2,1)}, u32[]{:S(2)}, u32[]{:S(2)}) collective-permute-start(bf16[128,4096]{1,0:T(8,128)(2,1)S(1)} %get-tuple-element.137.refs_0_.refs_4_), channel_id=1, source_target_pairs={{0,4},{2,6},{4,0},{6,2},{8,12},{10,14},{12,8},{14,10},{16,20},{18,... | collective-permute-start | bytes 3145736 | tf_op jit(solution)/shard_map/ppermute | solution.py:325
  122.4 43.5 %collective-permute-start.11 = (bf16[128,4096]{1,0:T(8,128)(2,1)S(1)}, bf16[128,4096]{1,0:T(8,128)(2,1)}, u32[]{:S(2)}, u32[]{:S(2)}) collective-permute-start(bf16[128,4096]{1,0:T(8,128)(2,1)S(1)} %get-tuple-element.137.refs_0_.refs_4_), channel_id=1, source_target_pairs={{0,1},{1,0},{2,3},{3,2},{4,5},{5,4},{6,7},{7,6},{8,9},{9,8},{10,11... | collective-permute-start | bytes 3145736 | tf_op jit(solution)/shard_map/ppermute | solution.py:323
  186.6 24.2 %collective-permute-start.17 = (bf16[256,2048]{1,0:T(8,128)(2,1)S(1)}, bf16[256,2048]{1,0:T(8,128)(2,1)S(1)}, u32[]{:S(2)}, u32[]{:S(2)}) collective-permute-start(bf16[256,2048]{1,0:T(8,128)(2,1)S(1)} %pad_maximum_fusion.6), channel_id=1, source_target_pairs={{0,4},{2,6},{4,0},{6,2},{8,12},{10,14},{12,8},{14,10},{16,20},{18,... | collective-permute-start | bytes 3145736 | tf_op jit(solution)/shard_map/ppermute | solution.py:325
  188.4 24.1 %collective-permute-start.15 = (bf16[256,2048]{1,0:T(8,128)(2,1)S(1)}, bf16[256,2048]{1,0:T(8,128)(2,1)S(1)}, u32[]{:S(2)}, u32[]{:S(2)}) collective-permute-start(bf16[256,2048]{1,0:T(8,128)(2,1)S(1)} %pad_maximum_fusion.5), channel_id=1, source_target_pairs={{0,1},{1,0},{2,3},{3,2},{4,5},{5,4},{6,7},{7,6},{8,9},{9,8},{10,11... | collective-permute-start | bytes 3145736 | tf_op jit(solution)/shard_map/ppermute | solution.py:323
  214.6 23.4 %collective-permute-start.22 = (bf16[256,2048]{1,0:T(8,128)(2,1)S(1)}, bf16[256,2048]{1,0:T(8,128)(2,1)}, u32[]{:S(2)}, u32[]{:S(2)}) collective-permute-start(bf16[256,2048]{1,0:T(8,128)(2,1)S(1)} %multiply_convert_fusion.1.refs_0_), channel_id=1, source_target_pairs={{0,4},{2,6},{4,0},{6,2},{8,12},{10,14},{12,8},{14,10},{16,20},{18,... | collective-permute-start | bytes 3145736 | tf_op jit(solution)/shard_map/ppermute | solution.py:325
  214.9 25.3 %collective-permute-start.21 = (bf16[256,2048]{1,0:T(8,128)(2,1)S(1)}, bf16[256,2048]{1,0:T(8,128)(2,1)}, u32[]{:S(2)}, u32[]{:S(2)}) collective-permute-start(bf16[256,2048]{1,0:T(8,128)(2,1)S(1)} %multiply_convert_fusion.1.refs_0_), channel_id=1, source_target_pairs={{0,1},{1,0},{2,3},{3,2},{4,5},{5,4},{6,7},{7,6},{8,9},{9,8},{10,11... | collective-permute-start | bytes 3145736 | tf_op jit(solution)/shard_map/ppermute | solution.py:323
  216.5 27.1 %collective-permute-start.18 = (s32[2]{0:T(128)S(1)}, s32[2]{0:T(128)S(1)}, u32[]{:S(2)}, u32[]{:S(2)}) collective-permute-start(s32[2]{0:T(128)S(1)} %copy-done.124), channel_id=1, source_target_pairs={{0,4},{2,6},{4,0},{6,2},{8,12},{10,14},{12,8},{14,10},{16,20},{18,... | collective-permute-start | bytes 32 | tf_op jit(solution)/shard_map/ppermute | solution.py:325
  243.8 303.1 %reduce-scatter.6.cloned.1.call-start = ((), (), s32[]{:S(2)}) async-start(), calls=%async_computation.9 | async-start | bytes 9437184 | tf_op jit(solution)/shard_map/reduce_scatter | solution.py:370
  267.0 16.5 %collective-permute-start.25 = (bf16[512,512]{1,0:T(8,128)(2,1)}, bf16[512,512]{1,0:T(8,128)(2,1)}, u32[]{:S(2)}, u32[]{:S(2)}) collective-permute-start(bf16[512,512]{1,0:T(8,128)(2,1)} %get-tuple-element.317), channel_id=1, source_target_pairs={{0,1},{1,0},{2,3},{3,2},{4,5},{5,4},{6,7},{7,6},{8,9},{9,8},{10,11... | collective-permute-start | bytes 1572872 | tf_op jit(solution)/shard_map/ppermute | solution.py:323
  267.8 20.9 %collective-permute-start.27 = (bf16[512,512]{1,0:T(8,128)(2,1)}, bf16[512,512]{1,0:T(8,128)(2,1)}, u32[]{:S(2)}, u32[]{:S(2)}) collective-permute-start(bf16[512,512]{1,0:T(8,128)(2,1)} %get-tuple-element.317), channel_id=1, source_target_pairs={{0,5},{1,4},{2,7},{3,6},{4,1},{5,0},{6,3},{7,2},{8,13},{9,12},{10,... | collective-permute-start | bytes 1572872 | tf_op jit(solution)/shard_map/ppermute | solution.py:327
  316.8 22.8 %collective-permute-start.31 = (bf16[256,2048]{1,0:T(8,128)(2,1)S(1)}, bf16[256,2048]{1,0:T(8,128)(2,1)S(1)}, u32[]{:S(2)}, u32[]{:S(2)}) collective-permute-start(bf16[256,2048]{1,0:T(8,128)(2,1)S(1)} %pad_maximum_fusion.8), channel_id=1, source_target_pairs={{0,4},{2,6},{4,0},{6,2},{8,12},{10,14},{12,8},{14,10},{16,20},{18,... | collective-permute-start | bytes 3145736 | tf_op jit(solution)/shard_map/ppermute | solution.py:325
  322.2 17.3 %collective-permute-start.29 = (bf16[256,2048]{1,0:T(8,128)(2,1)S(1)}, bf16[256,2048]{1,0:T(8,128)(2,1)S(1)}, u32[]{:S(2)}, u32[]{:S(2)}) collective-permute-start(bf16[256,2048]{1,0:T(8,128)(2,1)S(1)} %pad_maximum_fusion.7), channel_id=1, source_target_pairs={{0,1},{1,0},{2,3},{3,2},{4,5},{5,4},{6,7},{7,6},{8,9},{9,8},{10,11... | collective-permute-start | bytes 3145736 | tf_op jit(solution)/shard_map/ppermute | solution.py:323
  341.6 22.3 %collective-permute-start.33 = (bf16[256,2048]{1,0:T(8,128)(2,1)S(1)}, bf16[256,2048]{1,0:T(8,128)(2,1)S(1)}, u32[]{:S(2)}, u32[]{:S(2)}) collective-permute-start(bf16[256,2048]{1,0:T(8,128)(2,1)S(1)} %multiply_convert_fusion.refs_0_), channel_id=1, source_target_pairs={{0,4},{2,6},{4,0},{6,2},{8,12},{10,14},{12,8},{14,10},{16,20},{18,... | collective-permute-start | bytes 3145736 | tf_op jit(solution)/shard_map/ppermute | solution.py:325
  341.9 23.9 %collective-permute-start.32 = (bf16[256,2048]{1,0:T(8,128)(2,1)S(1)}, bf16[256,2048]{1,0:T(8,128)(2,1)S(1)}, u32[]{:S(2)}, u32[]{:S(2)}) collective-permute-start(bf16[256,2048]{1,0:T(8,128)(2,1)S(1)} %multiply_convert_fusion.refs_0_), channel_id=1, source_target_pairs={{0,1},{1,0},{2,3},{3,2},{4,5},{5,4},{6,7},{7,6},{8,9},{9,8},{10,11... | collective-permute-start | bytes 3145736 | tf_op jit(solution)/shard_map/ppermute | solution.py:323
  378.6 21.3 %collective-permute-start.37 = (bf16[256,2048]{1,0:T(8,128)(2,1)S(1)}, bf16[256,2048]{1,0:T(8,128)(2,1)S(1)}, u32[]{:S(2)}, u32[]{:S(2)}) collective-permute-start(bf16[256,2048]{1,0:T(8,128)(2,1)S(1)} %get-tuple-element.153.refs_0_), channel_id=1, source_target_pairs={{0,4},{2,6},{4,0},{6,2},{8,12},{10,14},{12,8},{14,10},{16,20},{18,... | collective-permute-start | bytes 3145736 | tf_op jit(solution)/shard_map/ppermute | solution.py:325
  379.6 20.4 %collective-permute-start.36 = (bf16[256,2048]{1,0:T(8,128)(2,1)S(1)}, bf16[256,2048]{1,0:T(8,128)(2,1)}, u32[]{:S(2)}, u32[]{:S(2)}) collective-permute-start(bf16[256,2048]{1,0:T(8,128)(2,1)S(1)} %get-tuple-element.153.refs_0_), channel_id=1, source_target_pairs={{0,1},{1,0},{2,3},{3,2},{4,5},{5,4},{6,7},{7,6},{8,9},{9,8},{10,11... | collective-permute-start | bytes 3145736 | tf_op jit(solution)/shard_map/ppermute | solution.py:323
  456.1 181.0 %reduce-scatter.8.cloned.1.call-start = ((), (), s32[]{:S(2)}) async-start(), calls=%async_computation.10 | async-start | bytes 9437184 | tf_op jit(solution)/shard_map/reduce_scatter | solution.py:370
  458.4 19.7 %collective-permute-start.41 = (bf16[128,2048]{1,0:T(8,128)(2,1)}, bf16[128,2048]{1,0:T(8,128)(2,1)}, u32[]{:S(2)}, u32[]{:S(2)}) collective-permute-start(bf16[128,2048]{1,0:T(8,128)(2,1)} %get-tuple-element.288), channel_id=1, source_target_pairs={{0,1},{1,0},{2,3},{3,2},{4,5},{5,4},{6,7},{7,6},{8,9},{9,8},{10,11... | collective-permute-start | bytes 1572872 | tf_op jit(solution)/shard_map/ppermute | solution.py:323
  460.4 16.3 %collective-permute-start.40 = (bf16[128,2048]{1,0:T(8,128)(2,1)}, bf16[128,2048]{1,0:T(8,128)(2,1)}, u32[]{:S(2)}, u32[]{:S(2)}) collective-permute-start(bf16[128,2048]{1,0:T(8,128)(2,1)} %get-tuple-element.289), channel_id=1, source_target_pairs={{0,4},{2,6},{4,0},{6,2},{8,12},{10,14},{12,8},{14,10},{16,20},{18,... | collective-permute-start | bytes 1572872 | tf_op jit(solution)/shard_map/ppermute | solution.py:325
  478.1 16.2 %collective-permute-start.42 = (bf16[256,2048]{1,0:T(8,128)(2,1)S(1)}, bf16[256,2048]{1,0:T(8,128)(2,1)S(1)}, u32[]{:S(2)}, u32[]{:S(2)}) collective-permute-start(bf16[256,2048]{1,0:T(8,128)(2,1)S(1)} %pad_maximum_fusion.10), channel_id=1, source_target_pairs={{0,1},{1,0},{2,3},{3,2},{4,5},{5,4},{6,7},{7,6},{8,9},{9,8},{10,11... | collective-permute-start | bytes 3145736 | tf_op jit(solution)/shard_map/ppermute | solution.py:323
  479.5 19.3 %collective-permute-start.43 = (bf16[256,2048]{1,0:T(8,128)(2,1)S(1)}, bf16[256,2048]{1,0:T(8,128)(2,1)S(1)}, u32[]{:S(2)}, u32[]{:S(2)}) collective-permute-start(bf16[256,2048]{1,0:T(8,128)(2,1)S(1)} %pad_maximum_fusion.11), channel_id=1, source_target_pairs={{0,4},{2,6},{4,0},{6,2},{8,12},{10,14},{12,8},{14,10},{16,20},{18,... | collective-permute-start | bytes 3145736 | tf_op jit(solution)/shard_map/ppermute | solution.py:325
  502.8 21.1 %collective-permute-start.45 = (bf16[256,2048]{1,0:T(8,128)(2,1)S(1)}, bf16[256,2048]{1,0:T(8,128)(2,1)S(1)}, u32[]{:S(2)}, u32[]{:S(2)}) collective-permute-start(bf16[256,2048]{1,0:T(8,128)(2,1)S(1)} %get-tuple-element.240.refs_4_), channel_id=1, source_target_pairs={{0,4},{2,6},{4,0},{6,2},{8,12},{10,14},{12,8},{14,10},{16,20},{18,... | collective-permute-start | bytes 3145736 | tf_op jit(solution)/shard_map/ppermute | solution.py:325
  504.4 20.5 %collective-permute-start.44 = (bf16[256,2048]{1,0:T(8,128)(2,1)S(1)}, bf16[256,2048]{1,0:T(8,128)(2,1)S(1)}, u32[]{:S(2)}, u32[]{:S(2)}) collective-permute-start(bf16[256,2048]{1,0:T(8,128)(2,1)S(1)} %get-tuple-element.240.refs_4_), channel_id=1, source_target_pairs={{0,1},{1,0},{2,3},{3,2},{4,5},{5,4},{6,7},{7,6},{8,9},{9,8},{10,11... | collective-permute-start | bytes 3145736 | tf_op jit(solution)/shard_map/ppermute | solution.py:323
  547.0 188.2 %reduce-scatter.10.cloned.1.call-start = ((), (), s32[]{:S(2)}) async-start(), calls=%async_computation.11 | async-start | bytes 9437184 | tf_op jit(solution)/shard_map/reduce_scatter | solution.py:370
  560.6 23.6 %collective-permute-start.51 = (bf16[256,2048]{1,0:T(8,128)(2,1)S(1)}, bf16[256,2048]{1,0:T(8,128)(2,1)S(1)}, u32[]{:S(2)}, u32[]{:S(2)}) collective-permute-start(bf16[256,2048]{1,0:T(8,128)(2,1)S(1)} %pad_maximum_fusion.13), channel_id=1, source_target_pairs={{0,4},{2,6},{4,0},{6,2},{8,12},{10,14},{12,8},{14,10},{16,20},{18,... | collective-permute-start | bytes 3145736 | tf_op jit(solution)/shard_map/ppermute | solution.py:325
  563.6 20.6 %collective-permute-start.49 = (bf16[256,2048]{1,0:T(8,128)(2,1)S(1)}, bf16[256,2048]{1,0:T(8,128)(2,1)S(1)}, u32[]{:S(2)}, u32[]{:S(2)}) collective-permute-start(bf16[256,2048]{1,0:T(8,128)(2,1)S(1)} %pad_maximum_fusion.12), channel_id=1, source_target_pairs={{0,1},{1,0},{2,3},{3,2},{4,5},{5,4},{6,7},{7,6},{8,9},{9,8},{10,11... | collective-permute-start | bytes 3145736 | tf_op jit(solution)/shard_map/ppermute | solution.py:323
  603.1 22.2 %collective-permute-start.55 = (bf16[256,2048]{1,0:T(8,128)(2,1)}, bf16[256,2048]{1,0:T(8,128)(2,1)}, u32[]{:S(2)}, u32[]{:S(2)}) collective-permute-start(bf16[256,2048]{1,0:T(8,128)(2,1)} %pad_maximum_fusion.15), channel_id=1, source_target_pairs={{0,4},{2,6},{4,0},{6,2},{8,12},{10,14},{12,8},{14,10},{16,20},{18,... | collective-permute-start | bytes 3145736 | tf_op jit(solution)/shard_map/ppermute | solution.py:325
  605.8 21.9 %collective-permute-start.53 = (bf16[256,2048]{1,0:T(8,128)(2,1)}, bf16[256,2048]{1,0:T(8,128)(2,1)}, u32[]{:S(2)}, u32[]{:S(2)}) collective-permute-start(bf16[256,2048]{1,0:T(8,128)(2,1)} %pad_maximum_fusion.14), channel_id=1, source_target_pairs={{0,1},{1,0},{2,3},{3,2},{4,5},{5,4},{6,7},{7,6},{8,9},{9,8},{10,11... | collective-permute-start | bytes 3145736 | tf_op jit(solution)/shard_map/ppermute | solution.py:323
  637.1 149.9 %reduce-scatter.12.cloned.1.call-start = ((), (), s32[]{:S(2)}) async-start(), calls=%async_computation.12 | async-start | bytes 4718592 | tf_op jit(solution)/shard_map/reduce_scatter | solution.py:370
  645.6 25.7 %collective-permute-start.67 = (bf16[512,512]{1,0:T(8,128)(2,1)}, bf16[512,512]{1,0:T(8,128)(2,1)}, u32[]{:S(2)}, u32[]{:S(2)}) collective-permute-start(bf16[512,512]{1,0:T(8,128)(2,1)} %get-tuple-element.278), channel_id=1, source_target_pairs={{0,5},{1,4},{2,7},{3,6},{4,1},{5,0},{6,3},{7,2},{8,13},{9,12},{10,... | collective-permute-start | bytes 1572872 | tf_op jit(solution)/shard_map/ppermute | solution.py:327
  647.1 26.4 %collective-permute-start.66 = (bf16[512,512]{1,0:T(8,128)(2,1)}, bf16[512,512]{1,0:T(8,128)(2,1)}, u32[]{:S(2)}, u32[]{:S(2)}) collective-permute-start(bf16[512,512]{1,0:T(8,128)(2,1)} %get-tuple-element.279), channel_id=1, source_target_pairs={{0,4},{2,6},{4,0},{6,2},{8,12},{10,14},{12,8},{14,10},{16,20},{18,... | collective-permute-start | bytes 1572872 | tf_op jit(solution)/shard_map/ppermute | solution.py:325
  649.9 42.1 %collective-permute-start.57 = (bf16[256,2048]{1,0:T(8,128)(2,1)S(1)}, bf16[256,2048]{1,0:T(8,128)(2,1)S(1)}, u32[]{:S(2)}, u32[]{:S(2)}) collective-permute-start(bf16[256,2048]{1,0:T(8,128)(2,1)S(1)} %get-tuple-element.237.refs_4_), channel_id=1, source_target_pairs={{0,4},{2,6},{4,0},{6,2},{8,12},{10,14},{12,8},{14,10},{16,20},{18,... | collective-permute-start | bytes 3145736 | tf_op jit(solution)/shard_map/ppermute | solution.py:325
  651.3 42.2 %collective-permute-start.56 = (bf16[256,2048]{1,0:T(8,128)(2,1)S(1)}, bf16[256,2048]{1,0:T(8,128)(2,1)}, u32[]{:S(2)}, u32[]{:S(2)}) collective-permute-start(bf16[256,2048]{1,0:T(8,128)(2,1)S(1)} %get-tuple-element.237.refs_4_), channel_id=1, source_target_pairs={{0,1},{1,0},{2,3},{3,2},{4,5},{5,4},{6,7},{7,6},{8,9},{9,8},{10,11... | collective-permute-start | bytes 3145736 | tf_op jit(solution)/shard_map/ppermute | solution.py:323
  697.6 27.1 %collective-permute-start.60 = (bf16[256,2048]{1,0:T(8,128)(2,1)S(1)}, bf16[256,2048]{1,0:T(8,128)(2,1)S(1)}, u32[]{:S(2)}, u32[]{:S(2)}) collective-permute-start(bf16[256,2048]{1,0:T(8,128)(2,1)S(1)} %copy-done.17), channel_id=1, source_target_pairs={{0,1},{1,0},{2,3},{3,2},{4,5},{5,4},{6,7},{7,6},{8,9},{9,8},{10,11... | collective-permute-start | bytes 3145736 | tf_op jit(solution)/shard_map/ppermute | solution.py:323
  735.2 154.3 %reduce-scatter.14.cloned.1.call-start = ((), (), s32[]{:S(2)}) async-start(), calls=%async_computation.13 | async-start | bytes 9437184 | tf_op jit(solution)/shard_map/reduce_scatter | solution.py:370
  747.3 22.8 %collective-permute-start.64 = (bf16[256,2048]{1,0:T(8,128)(2,1)}, bf16[256,2048]{1,0:T(8,128)(2,1)}, u32[]{:S(2)}, u32[]{:S(2)}) collective-permute-start(bf16[256,2048]{1,0:T(8,128)(2,1)} %pad_maximum_fusion.17), channel_id=1, source_target_pairs={{0,4},{2,6},{4,0},{6,2},{8,12},{10,14},{12,8},{14,10},{16,20},{18,... | collective-permute-start | bytes 3145736 | tf_op jit(solution)/shard_map/ppermute | solution.py:325
  751.6 18.5 %collective-permute-start.62 = (bf16[256,2048]{1,0:T(8,128)(2,1)}, bf16[256,2048]{1,0:T(8,128)(2,1)}, u32[]{:S(2)}, u32[]{:S(2)}) collective-permute-start(bf16[256,2048]{1,0:T(8,128)(2,1)} %pad_maximum_fusion.16), channel_id=1, source_target_pairs={{0,1},{1,0},{2,3},{3,2},{4,5},{5,4},{6,7},{7,6},{8,9},{9,8},{10,11... | collective-permute-start | bytes 3145736 | tf_op jit(solution)/shard_map/ppermute | solution.py:323
  806.6 22.8 %collective-permute-start.69 = (bf16[128,2048]{1,0:T(8,128)(2,1)S(1)}, bf16[128,2048]{1,0:T(8,128)(2,1)S(1)}, u32[]{:S(2)}, u32[]{:S(2)}) collective-permute-start(bf16[128,2048]{1,0:T(8,128)(2,1)S(1)} %get-tuple-element.194), channel_id=1, source_target_pairs={{0,4},{2,6},{4,0},{6,2},{8,12},{10,14},{12,8},{14,10},{16,20},{18,... | collective-permute-start | bytes 1572872 | tf_op jit(solution)/shard_map/ppermute | solution.py:325
  807.2 22.3 %collective-permute-start.68 = (bf16[128,2048]{1,0:T(8,128)(2,1)S(1)}, bf16[128,2048]{1,0:T(8,128)(2,1)S(1)}, u32[]{:S(2)}, u32[]{:S(2)}) collective-permute-start(bf16[128,2048]{1,0:T(8,128)(2,1)S(1)} %get-tuple-element.193.refs_0_), channel_id=1, source_target_pairs={{0,1},{1,0},{2,3},{3,2},{4,5},{5,4},{6,7},{7,6},{8,9},{9,8},{10,11... | collective-permute-start | bytes 1572872 | tf_op jit(solution)/shard_map/ppermute | solution.py:323
  808.5 22.6 %collective-permute-start.78 = (f32[3,256]{1,0:T(4,128)S(1)}, f32[3,256]{1,0:T(4,128)S(1)}, u32[]{:S(2)}, u32[]{:S(2)}) collective-permute-start(f32[3,256]{1,0:T(4,128)S(1)} %slice_select_fusion.2), channel_id=1, source_target_pairs={{0,4},{2,6},{4,0},{6,2},{8,12},{10,14},{12,8},{14,10},{16,20},{18,... | collective-permute-start | bytes 9224 | tf_op jit(solution)/shard_map/ppermute | solution.py:330
  831.1 20.4 %collective-permute-start.79 = (f32[3,128]{1,0:T(4,128)S(1)}, f32[3,128]{1,0:T(4,128)S(1)}, u32[]{:S(2)}, u32[]{:S(2)}) collective-permute-start(f32[3,128]{1,0:T(4,128)S(1)} %slice_select_fusion.3), channel_id=1, source_target_pairs={{0,2},{2,0},{4,6},{6,4},{8,10},{10,8},{12,14},{14,12},{16,18},{18,... | collective-permute-start | bytes 4616 | tf_op jit(solution)/shard_map/ppermute | solution.py:330
  848.3 20.9 %collective-permute-start.82 = (bf16[128,1536]{1,0:T(8,128)(2,1)S(1)}, bf16[128,1536]{1,0:T(8,128)(2,1)S(1)}, u32[]{:S(2)}, u32[]{:S(2)}) collective-permute-start(bf16[128,1536]{1,0:T(8,128)(2,1)S(1)} %get-tuple-element.211), channel_id=1, source_target_pairs={{0,5},{1,4},{2,7},{3,6},{4,1},{5,0},{6,3},{7,2},{8,13},{9,12},{10,... | collective-permute-start | bytes 1179656 | tf_op jit(solution)/shard_map/ppermute | solution.py:327
  851.5 20.5 %collective-permute-start.81 = (bf16[128,1536]{1,0:T(8,128)(2,1)S(1)}, bf16[128,1536]{1,0:T(8,128)(2,1)S(1)}, u32[]{:S(2)}, u32[]{:S(2)}) collective-permute-start(bf16[128,1536]{1,0:T(8,128)(2,1)S(1)} %get-tuple-element.211), channel_id=1, source_target_pairs={{0,4},{2,6},{4,0},{6,2},{8,12},{10,14},{12,8},{14,10},{16,20},{18,... | collective-permute-start | bytes 1179656 | tf_op jit(solution)/shard_map/ppermute | solution.py:325
  855.1 22.5 %collective-permute-start.80 = (bf16[128,1536]{1,0:T(8,128)(2,1)S(1)}, bf16[128,1536]{1,0:T(8,128)(2,1)S(1)}, u32[]{:S(2)}, u32[]{:S(2)}) collective-permute-start(bf16[128,1536]{1,0:T(8,128)(2,1)S(1)} %get-tuple-element.210.refs_0_), channel_id=1, source_target_pairs={{0,1},{1,0},{2,3},{3,2},{4,5},{5,4},{6,7},{7,6},{8,9},{9,8},{10,11... | collective-permute-start | bytes 1179656 | tf_op jit(solution)/shard_map/ppermute | solution.py:323
  860.7 22.6 %collective-permute-start.88 = (bf16[128,1024]{1,0:T(8,128)(2,1)S(1)}, bf16[128,1024]{1,0:T(8,128)(2,1)S(1)}, u32[]{:S(2)}, u32[]{:S(2)}) collective-permute-start(bf16[128,1024]{1,0:T(8,128)(2,1)S(1)} %get-tuple-element.214), channel_id=1, source_target_pairs={{0,5},{1,4},{2,7},{3,6},{4,1},{5,0},{6,3},{7,2},{8,13},{9,12},{10,... | collective-permute-start | bytes 786440 | tf_op jit(solution)/shard_map/ppermute | solution.py:327
  862.2 21.9 %collective-permute-start.87 = (bf16[128,1024]{1,0:T(8,128)(2,1)S(1)}, bf16[128,1024]{1,0:T(8,128)(2,1)S(1)}, u32[]{:S(2)}, u32[]{:S(2)}) collective-permute-start(bf16[128,1024]{1,0:T(8,128)(2,1)S(1)} %get-tuple-element.214), channel_id=1, source_target_pairs={{0,4},{2,6},{4,0},{6,2},{8,12},{10,14},{12,8},{14,10},{16,20},{18,... | collective-permute-start | bytes 786440 | tf_op jit(solution)/shard_map/ppermute | solution.py:325
  869.2 19.6 %collective-permute-start.86 = (bf16[128,1024]{1,0:T(8,128)(2,1)S(1)}, bf16[128,1024]{1,0:T(8,128)(2,1)S(1)}, u32[]{:S(2)}, u32[]{:S(2)}) collective-permute-start(bf16[128,1024]{1,0:T(8,128)(2,1)S(1)} %get-tuple-element.213.refs_0_), channel_id=1, source_target_pairs={{0,1},{1,0},{2,3},{3,2},{4,5},{5,4},{6,7},{7,6},{8,9},{9,8},{10,11... | collective-permute-start | bytes 786440 | tf_op jit(solution)/shard_map/ppermute | solution.py:323
  872.0 32.6 %collective-permute-start.74 = (bf16[128,4096]{1,0:T(8,128)(2,1)}, bf16[128,4096]{1,0:T(8,128)(2,1)}, u32[]{:S(2)}, u32[]{:S(2)}) collective-permute-start(bf16[128,4096]{1,0:T(8,128)(2,1)} %pad_maximum_fusion.19), channel_id=1, source_target_pairs={{0,4},{2,6},{4,0},{6,2},{8,12},{10,14},{12,8},{14,10},{16,20},{18,... | collective-permute-start | bytes 3145736 | tf_op jit(solution)/shard_map/ppermute | solution.py:325
  877.6 33.9 %collective-permute-start.72 = (bf16[128,4096]{1,0:T(8,128)(2,1)}, bf16[128,4096]{1,0:T(8,128)(2,1)}, u32[]{:S(2)}, u32[]{:S(2)}) collective-permute-start(bf16[128,4096]{1,0:T(8,128)(2,1)} %pad_maximum_fusion.18), channel_id=1, source_target_pairs={{0,1},{1,0},{2,3},{3,2},{4,5},{5,4},{6,7},{7,6},{8,9},{9,8},{10,11... | collective-permute-start | bytes 3145736 | tf_op jit(solution)/shard_map/ppermute | solution.py:323
  891.4 25.6 %collective-permute-start.94 = (bf16[64,2048]{1,0:T(8,128)(2,1)S(1)}, bf16[64,2048]{1,0:T(8,128)(2,1)S(1)}, u32[]{:S(2)}, u32[]{:S(2)}) collective-permute-start(bf16[64,2048]{1,0:T(8,128)(2,1)S(1)} %get-tuple-element.218.refs_4_), channel_id=1, source_target_pairs={{0,3},{1,2},{2,1},{3,0},{4,7},{5,6},{6,5},{7,4},{8,11},{9,10},{10,... | collective-permute-start | bytes 786440 | tf_op jit(solution)/shard_map/ppermute | solution.py:905
  897.8 29.6 %collective-permute-start.93 = (bf16[64,2048]{1,0:T(8,128)(2,1)S(1)}, bf16[64,2048]{1,0:T(8,128)(2,1)S(1)}, u32[]{:S(2)}, u32[]{:S(2)}) collective-permute-start(bf16[64,2048]{1,0:T(8,128)(2,1)S(1)} %get-tuple-element.218.refs_4_), channel_id=1, source_target_pairs={{0,1},{1,0},{2,3},{3,2},{4,5},{5,4},{6,7},{7,6},{8,9},{9,8},{10,11... | collective-permute-start | bytes 786440 | tf_op jit(solution)/shard_map/ppermute | solution.py:323
  899.0 28.4 %collective-permute-start.92 = (bf16[64,2048]{1,0:T(8,128)(2,1)S(1)}, bf16[64,2048]{1,0:T(8,128)(2,1)S(1)}, u32[]{:S(2)}, u32[]{:S(2)}) collective-permute-start(bf16[64,2048]{1,0:T(8,128)(2,1)S(1)} %get-tuple-element.218.refs_4_), channel_id=1, source_target_pairs={{0,2},{2,0},{4,6},{6,4},{8,10},{10,8},{12,14},{14,12},{16,18},{18,... | collective-permute-start | bytes 786440 | tf_op jit(solution)/shard_map/ppermute | solution.py:330
  904.7 34.8 %collective-permute-start.91 = (bf16[128,1536]{1,0:T(8,128)(2,1)S(1)}, bf16[128,1536]{1,0:T(8,128)(2,1)S(1)}, u32[]{:S(2)}, u32[]{:S(2)}) collective-permute-start(bf16[128,1536]{1,0:T(8,128)(2,1)S(1)} %get-tuple-element.217), channel_id=1, source_target_pairs={{0,5},{1,4},{2,7},{3,6},{4,1},{5,0},{6,3},{7,2},{8,13},{9,12},{10,... | collective-permute-start | bytes 1179656 | tf_op jit(solution)/shard_map/ppermute | solution.py:327
  911.4 28.0 %collective-permute-start.90 = (bf16[128,1536]{1,0:T(8,128)(2,1)S(1)}, bf16[128,1536]{1,0:T(8,128)(2,1)S(1)}, u32[]{:S(2)}, u32[]{:S(2)}) collective-permute-start(bf16[128,1536]{1,0:T(8,128)(2,1)S(1)} %get-tuple-element.217), channel_id=1, source_target_pairs={{0,4},{2,6},{4,0},{6,2},{8,12},{10,14},{12,8},{14,10},{16,20},{18,... | collective-permute-start | bytes 1179656 | tf_op jit(solution)/shard_map/ppermute | solution.py:325
  917.0 22.4 %collective-permute-start.89 = (bf16[128,1536]{1,0:T(8,128)(2,1)S(1)}, bf16[128,1536]{1,0:T(8,128)(2,1)S(1)}, u32[]{:S(2)}, u32[]{:S(2)}) collective-permute-start(bf16[128,1536]{1,0:T(8,128)(2,1)S(1)} %get-tuple-element.216.refs_0_), channel_id=1, source_target_pairs={{0,1},{1,0},{2,3},{3,2},{4,5},{5,4},{6,7},{7,6},{8,9},{9,8},{10,11... | collective-permute-start | bytes 1179656 | tf_op jit(solution)/shard_map/ppermute | solution.py:323
  (173 other events, 2568.4 us)
Sparse Core Ops, SparseCore 0:
  26.3 83.8 all-gather.4
  112.4 115.1 all-gather.6
  229.8 80.3 all-gather.8
  312.2 80.5 all-gather.10
  456.2 90.6 reduce-scatter.5
  549.1 87.9 reduce-scatter.7
  639.4 87.9 reduce-scatter.9
  735.3 51.6 reduce-scatter.11
  789.3 88.2 reduce-scatter.13
